TPU v7x, 32 devices: a whole 2x2x4 slice. The times are simulated.
32 devices in a mesh: lev: 4 (over z), wave: 8 (over y, x, core).
Axes of the slice: x: 2, y: 2, z: 4, core: 2. Of those that a mesh axis runs over, the one named last changes fastest.
Arguments:
- legendre: float32 [320, 16, 641], P('wave'), may hold values from -0.25 to 0.25
- spectral: float32 [320, 8, 2, 641], P('wave', 'lev'), may hold values from -0.12 to 0.12
- pair_low: int32 [320], replicated, may hold values from 0 to 319, each once
- dep_lat: int32 [320], P('wave'), may hold values from 0 to 14, as said below
- dep_col: int32 [320], P('wave'), may hold values from 0 to 1279, as said below
- lon_steps: int32 [320, 128], P('wave'), may hold values from 0 to 24
- tilt_steps: int32 [320, 128], P('wave'), may hold values from 0 to 15
Outputs:
- grid_field: float32 [8, 32, 1280], P('lev', 'wave')
- departed: float32 [8, 32, 1280], P('lev', 'wave')
Inputs may be any that keep to these rules, and one draw needn't show every extreme that they name: dep_lat lies between the arrival block's own latitude index in its hemisphere minus 2 and that index plus 1, clipped to the band. dep_col is the arrival block's first column plus -3 to 3, modulo 1280.
All inputs are finite; a program needn't handle non-finite values.
Results may differ from a plain program's by a relative error of at most 0.0003.
Values sent between devices are 32-bit elements; how exact they have to be, the bound alone decides.
No kernel may reach another device: no remote copies, remote signals or barrier semaphores. Data moves between devices by JAX's collectives and lax.ppermute only.
A program may use at most 64 MiB of HBM per device.

v0:
```python
import functools
import math

import jax
import jax.numpy as jnp
import ml_dtypes
import numpy as np
from jax import lax
from jax.experimental import pallas as pl
from jax.experimental.pallas import tpu as pltpu
from jax.sharding import PartitionSpec as P

LANES = 128
GROUP = 8
HALO = 2
MIB = 1024 * 1024
NT = (((1,), (1,)), ((), ()))
NN = (((1,), (0,)), ((), ()))


def split(value):
    high = value.astype(jnp.bfloat16)
    low = (value - high.astype(jnp.float32)).astype(jnp.bfloat16)
    return high, low


def legendre_kernel(slot_count, pair_local, lat_dev, low_ref, spec_ref, leg_ref, out_ref):
    group, lat_all, width = leg_ref.shape
    level_count = spec_ref.shape[1]
    pair_total = low_ref.shape[0]
    base = lax.axis_index("wave") * pair_local + pl.program_id(0) * group
    slot_of_row = lax.broadcasted_iota(jnp.int32, (group, LANES), 0)
    first = jnp.zeros((group, LANES), jnp.int32)
    for slot in range(group):
        low = low_ref[jnp.minimum(base + slot, pair_total - 1)]
        first = jnp.where(slot_of_row == slot, slot_count - 1 - low, first)
    first = jnp.concatenate([first] * (width // LANES), axis=1)
    slot_pos = lax.broadcasted_iota(jnp.int32, (group, width), 1)
    inside = slot_pos < slot_count
    second = slot_pos >= first
    offset = jnp.where(second, slot_pos - first, slot_pos)
    sign = (1 - 2 * (offset & 1)).astype(jnp.float32)
    pieces = []
    for level in range(level_count):
        for part in range(2):
            row = jnp.where(inside, spec_ref[:, level, part, :], 0.0)
            for hemi in range(2):
                signed = row * sign if hemi else row
                pieces.append(jnp.where(second, 0.0, signed))
                pieces.append(jnp.where(second, signed, 0.0))
    columns = jnp.concatenate(split(jnp.concatenate(pieces, axis=0)), axis=0)
    count = group * len(pieces)
    table_pos = lax.broadcasted_iota(jnp.int32, (group * lat_all, width), 1)
    table = jnp.where(table_pos < slot_count, leg_ref[...].reshape(group * lat_all, width), 0.0)
    rows = jnp.concatenate(split(table), axis=0)
    crossed = lax.dot_general(rows, columns, NT, preferred_element_type=jnp.float32)
    half = group * lat_all
    crossed = (crossed[:half, :count] + crossed[:half, count:]) + (
        crossed[half:, :count] + crossed[half:, count:]
    )
    slot_of_lane = lax.broadcasted_iota(jnp.int32, (lat_all, count), 1) % group
    sums = jnp.zeros((lat_all, count), jnp.float32)
    for slot in range(group):
        block = crossed[slot * lat_all : (slot + 1) * lat_all]
        sums = jnp.where(slot_of_lane == slot, block, sums)
    edge = jnp.zeros((HALO, count), jnp.float32)
    tail = jnp.zeros((2 * HALO, count), jnp.float32)
    padded = jnp.concatenate([edge, sums, tail], axis=0)
    for dest in range(out_ref.shape[0]):
        out_ref[dest] = padded[dest * lat_dev : dest * lat_dev + out_ref.shape[1]]


def legendre_sums(pair_low, spectral, legendre, pair_local, slot_count, wave_size):
    slots, level_count = spectral.shape[:2]
    lat_all = legendre.shape[1]
    lat_dev = lat_all // wave_size
    width = pl.cdiv(slot_count, 256) * 256
    count = GROUP * 8 * level_count
    ext_pad = pl.cdiv(lat_dev + 2 * HALO, 8) * 8
    return pl.pallas_call(
        functools.partial(legendre_kernel, slot_count, pair_local, lat_dev),
        grid=(slots // GROUP,),
        in_specs=[
            pl.BlockSpec(memory_space=pltpu.SMEM),
            pl.BlockSpec((GROUP, level_count, 2, width), lambda g: (g, 0, 0, 0)),
            pl.BlockSpec((GROUP, lat_all, width), lambda g: (g, 0, 0)),
        ],
        out_specs=pl.BlockSpec((wave_size, ext_pad, count), lambda g: (0, 0, g)),
        out_shape=jax.ShapeDtypeStruct(
            (wave_size, ext_pad, count * (slots // GROUP)), jnp.float32
        ),
        compiler_params=pltpu.CompilerParams(vmem_limit_bytes=60 * MIB),
        name="legendre",
    )(pair_low, spectral, legendre)


def fourier_tables(wavenumber_count):
    lon_count = 2 * wavenumber_count
    half_lon = lon_count // 2
    tables = []
    for parity in range(2):
        wave = np.arange(parity, wavenumber_count, 2)
        phase = wave[:, None] * np.arange(half_lon)[None, :] % lon_count
        angle = phase * (2.0 * math.pi / lon_count)
        weight = np.where(wave == 0, 1.0, 2.0)[:, None]
        parts = [weight * np.cos(angle), -weight * np.sin(angle)]
        tables.append(np.concatenate(parts if parity == 0 else parts[::-1], axis=0))
    exact = np.stack(tables)
    high = exact.astype(ml_dtypes.bfloat16)
    low = (exact - high.astype(np.float64)).astype(ml_dtypes.bfloat16)
    return high, low


def regroup(pieces, level, lane):
    piece_lanes = LANES // 8
    upper = lane // piece_lanes >= 4
    if level == 0:
        pieces = [
            jnp.where(upper, pltpu.roll(pieces[i + 4], 4 * piece_lanes, 1), pieces[i])
            for i in range(4)
        ]
    else:
        pieces = [
            jnp.where(upper, pieces[i + 4], pltpu.roll(pieces[i], 4 * piece_lanes, 1))
            for i in range(4)
        ]
    for bit in (1, 2):
        upper = (lane // piece_lanes & bit) != 0
        for one in range(4):
            if one & bit:
                continue
            a, b = pieces[one], pieces[one | bit]
            pieces[one] = jnp.where(upper, pltpu.roll(b, piece_lanes * bit, 1), a)
            pieces[one | bit] = jnp.where(
                upper, b, pltpu.roll(a, LANES - piece_lanes * bit, 1)
            )
    return pieces


def level_rows(level, recv_ref, select_ref, high_ref, low_ref):
    source_count, ext_pad, width = recv_ref.shape
    half = high_ref.shape[2]
    lane = lax.broadcasted_iota(jnp.int32, (ext_pad, LANES), 1)
    vectors = [
        recv_ref[source, :, LANES * i : LANES * (i + 1)]
        for source in range(source_count)
        for i in range(width // LANES)
    ]
    columns = [[] for _ in range(4)]
    for start in range(0, len(vectors), 8):
        for kind, piece in enumerate(regroup(vectors[start : start + 8], level, lane)):
            columns[kind].append(piece)
    matrix = jnp.concatenate([jnp.concatenate(c, axis=1) for c in columns], axis=0)
    high, low = split(matrix)
    count = high.shape[0] // 2
    ordered = lax.dot_general(
        jnp.concatenate([high[:count], low[:count], high[count:], low[count:]], axis=0),
        select_ref[...],
        NT,
        preferred_element_type=jnp.float32,
    )
    real = ordered[: 2 * count]
    imag = pltpu.roll(ordered[2 * count :], half // 2, 1)
    first_half = lax.broadcasted_iota(jnp.int32, real.shape, 1) < half // 2
    even = jnp.where(first_half, real, imag).astype(jnp.bfloat16)
    odd = jnp.where(first_half, imag, real).astype(jnp.bfloat16)
    sums = []
    for parity, operand in enumerate((even, odd)):
        main = lax.dot_general(
            operand, high_ref[parity], NN, preferred_element_type=jnp.float32
        )
        rest = lax.dot_general(
            operand[:count], low_ref[parity], NN, preferred_element_type=jnp.float32
        )
        sums.append(main[:count] + (main[count:] + rest))
    return sums


def interpolate(sums, field_ref, level, lat_dev, lon, tilt, row_step, col_step, near_ref):
    half = sums[0].shape[1]
    count = sums[0].shape[0]
    ext_pad = count // 2
    blocks = 2 * half // LANES
    for block in range(blocks // 2):
        here = slice(block * LANES, (block + 1) * LANES)
        for at, rows in (
            (block, sums[0][:, here] + sums[1][:, here]),
            (block + blocks // 2, sums[0][:, here] - sums[1][:, here]),
        ):
            there = slice(at * LANES, (at + 1) * LANES)
            for hemi in range(2):
                start = hemi * ext_pad + HALO
                field_ref[level, hemi * lat_dev : (hemi + 1) * lat_dev, there] = rows[
                    start : start + lat_dev
                ]
            for side in range(3):
                place = (at + 1 - side) % blocks
                near_ref[side, pl.ds(place, count, stride=blocks), :] = rows
    points = 2 * lat_dev * blocks
    point = lax.broadcasted_iota(jnp.int32, (points, LANES), 1)
    quarters = 4 * col_step + lon - 12
    step = point + (quarters >> 2)
    f = (quarters & 3).astype(jnp.float32) * 0.25
    g = (tilt & 3).astype(jnp.float32) * 0.25

    def line(side, j):
        return jnp.concatenate(
            [
                near_ref[side, pl.ds((hemi * ext_pad + j) * blocks, lat_dev * blocks), :]
                for hemi in range(2)
            ],
            axis=0,
        )

    lines = [[line(side, j) for j in range(2 * HALO + 1)] for side in range(3)]
    values = []
    for upper in range(2):
        picked = []
        for side in range(3):
            choice = lines[side][upper]
            for j in range(1, 2 * HALO):
                choice = jnp.where(row_step == j, lines[side][j + upper], choice)
            picked.append(choice)
        left = jnp.where(point >= LANES - 28, picked[0], picked[1])
        right = jnp.where(point < 28, picked[2], picked[1])
        for shift in range(2):
            place = (step + shift) & (LANES - 1)
            values.append(
                jnp.where(
                    point < LANES // 2,
                    jnp.take_along_axis(left, place, axis=1),
                    jnp.take_along_axis(right, place, axis=1),
                )
            )
    lower = (1.0 - f) * values[0] + f * values[1]
    higher = (1.0 - f) * values[2] + f * values[3]
    return (1.0 - g) * lower + g * higher


def first_kernel(
    lat_dev,
    recv_ref,
    select_ref,
    high_ref,
    low_ref,
    row_ref,
    col_ref,
    lon_ref,
    tilt_ref,
    field_ref,
    horizontal_ref,
    near_ref,
):
    sums = level_rows(0, recv_ref, select_ref, high_ref, low_ref)
    horizontal_ref[...] = interpolate(
        sums,
        field_ref,
        0,
        lat_dev,
        lon_ref[...],
        tilt_ref[...],
        row_ref[...],
        col_ref[...],
        near_ref,
    )


def later_kernel(
    lat_dev,
    recv_ref,
    select_ref,
    high_ref,
    low_ref,
    row_ref,
    col_ref,
    lon_ref,
    tilt_ref,
    below_ref,
    field_ref,
    departed_ref,
    horizontal_ref,
    near_ref,
):
    level_count = departed_ref.shape[0] + 1
    tilt = tilt_ref[...]
    vertical = (tilt >> 2).astype(jnp.float32) * 0.25
    below = below_ref[...]
    for level in range(1, level_count):
        sums = level_rows(level, recv_ref, select_ref, high_ref, low_ref)
        horizontal = interpolate(
            sums,
            field_ref,
            level - 1,
            lat_dev,
            lon_ref[...],
            tilt,
            row_ref[...],
            col_ref[...],
            near_ref,
        )
        departed_ref[level - 1] = (1.0 - vertical) * below + vertical * horizontal
        below = horizontal
    horizontal_ref[...] = below


def last_kernel(below_ref, above_ref, tilt_ref, out_ref):
    is_last = lax.axis_index("lev") == lax.axis_size("lev") - 1
    vertical = (tilt_ref[...] >> 2).astype(jnp.float32) * 0.25
    below = below_ref[...]
    above = jnp.where(is_last, below, above_ref[...])
    out_ref[...] = (1.0 - vertical) * below + vertical * above


def per_device(legendre, spectral, pair_low, dep_lat, dep_col, lon_steps, tilt_steps):
    pair_local, level_count, _, slot_count = spectral.shape
    wavenumber_count = slot_count - 1
    lon_count = 2 * wavenumber_count
    lat_all = legendre.shape[1]
    wave_size = lax.axis_size("wave")
    lev_size = lax.axis_size("lev")
    wave_id = lax.axis_index("wave")
    lat_dev = lat_all // wave_size
    slots = pl.cdiv(pair_local, GROUP) * GROUP
    extra = slots - pair_local
    if extra:
        spectral = jnp.pad(spectral, ((0, extra), (0, 0), (0, 0), (0, 0)))
        legendre = jnp.pad(legendre, ((0, extra), (0, 0), (0, 0)))
    sums = legendre_sums(pair_low, spectral, legendre, pair_local, slot_count, wave_size)
    received = lax.all_to_all(sums, "wave", split_axis=0, concat_axis=0, tiled=True)

    all_low = pair_low.reshape(wave_size, pair_local)
    waves = jnp.stack([all_low, wavenumber_count - 1 - all_low], axis=1)
    waves = jnp.pad(waves, ((0, 0), (0, 0), (0, extra)), constant_values=-1)
    waves = waves.reshape(wave_size, 2, slots // GROUP, GROUP).transpose(0, 2, 1, 3)
    order = np.arange(wavenumber_count)
    order = np.concatenate([order[::2], order[1::2]]).astype(np.int32)
    select = (waves.reshape(1, -1) == order[:, None]).astype(jnp.bfloat16)

    blocks = lon_count // LANES
    points = 2 * lat_dev * blocks
    row = jnp.arange(points, dtype=jnp.int32)
    own_lat = wave_id * lat_dev + row // blocks % lat_dev
    row_step = dep_lat - own_lat + HALO
    col_step = dep_col - LANES * (row % blocks)
    col_step = (col_step + lon_count // 2) % lon_count - lon_count // 2
    row_step = jnp.broadcast_to(row_step[:, None], (points, LANES))
    col_step = jnp.broadcast_to(col_step[:, None], (points, LANES))

    high, low = fourier_tables(wavenumber_count)
    ext_pad = received.shape[1]
    vmem = pl.BlockSpec(memory_space=pltpu.VMEM)
    params = pltpu.CompilerParams(vmem_limit_bytes=24 * MIB)
    operands = (
        received,
        select,
        jnp.asarray(high),
        jnp.asarray(low),
        row_step,
        col_step,
        lon_steps,
        tilt_steps,
    )
    near = pltpu.VMEM((3, 2 * ext_pad * blocks, LANES), jnp.float32)
    flat = jax.ShapeDtypeStruct((points, LANES), jnp.float32)
    field_first, horizontal = pl.pallas_call(
        functools.partial(first_kernel, lat_dev),
        in_specs=[vmem] * 8,
        out_specs=[vmem] * 2,
        out_shape=[jax.ShapeDtypeStruct((1, 2 * lat_dev, lon_count), jnp.float32), flat],
        scratch_shapes=[near],
        compiler_params=params,
        name="first_level",
    )(*operands)
    above = lax.ppermute(horizontal, "lev", [(i, i - 1) for i in range(1, lev_size)])
    field_later, departed, top = pl.pallas_call(
        functools.partial(later_kernel, lat_dev),
        in_specs=[vmem] * 9,
        out_specs=[vmem] * 3,
        out_shape=[
            jax.ShapeDtypeStruct((level_count - 1, 2 * lat_dev, lon_count), jnp.float32),
            jax.ShapeDtypeStruct((level_count - 1, points, LANES), jnp.float32),
            flat,
        ],
        scratch_shapes=[near],
        compiler_params=params,
        cost_estimate=pl.CostEstimate(
            flops=10**8, bytes_accessed=4 * 10**6, transcendentals=0
        ),
        name="later_levels",
    )(*operands, horizontal)
    grid_field = jnp.concatenate([field_first, field_later], axis=0)
    final = pl.pallas_call(
        last_kernel,
        in_specs=[vmem] * 3,
        out_specs=vmem,
        out_shape=flat,
        compiler_params=params,
        name="top_level",
    )(top, above, tilt_steps)
    departed = jnp.concatenate([departed, final[None]], axis=0)
    return grid_field, departed.reshape(level_count, 2 * lat_dev, lon_count)


def solution(mesh):
    return jax.shard_map(
        per_device,
        mesh=mesh,
        in_specs=(
            P("wave", None, None),
            P("wave", "lev", None, None),
            P(),
            P("wave"),
            P("wave"),
            P("wave", None),
            P("wave", None),
        ),
        out_specs=(P("lev", "wave", None), P("lev", "wave", None)),
        check_vma=False,
    )
```

profile of v0, /device:TPU:0, one launch (start us, length us, event | category | flops | bytes accessed | tf_op | source)
XLA Modules:
  0.0 26.1 jit_solution(6568659779344651955)
XLA Ops:
  0.6 0.0 copy-start.5
  0.6 0.0 copy-start
  0.7 0.0 copy-start.4
  0.7 0.0 copy-start.6
  0.7 0.0 copy-start.7
  0.7 0.0 copy-start.2
  0.7 0.0 copy-start.3
  0.7 5.0 %legendre.1 = f32[8,8,640]{2,1,0:T(8,128)} custom-call(s32[320]{0:T(512)} %low_ref.3, f32[40,2,2,641]{3,2,1,0:T(2,128)} %spec_ref.1, f32[40,16,641]{2,1,0:T(8,128)} %leg_ref.1), custom_call_target="tpu_custom_call" | custom-call | tf_op jit(solution)/shard_map/legendre/pallas_call | solution.py:80
  5.7 5.2 %all-to-all-start = ((f32[8,8,640]{2,1,0:T(8,128)}), f32[8,8,640]{2,1,0:T(8,128)S(1)}, u32[]{:S(2)}, u32[]{:S(2)}) async-start(f32[8,8,640]{2,1,0:T(8,128)} %legendre.1), calls=%async_computation | async-start | bytes 327680 | tf_op jit(solution)/shard_map/all_to_all | solution.py:329
  10.9 0.0 copy-done.4
  10.9 0.1 stack.6
  11.0 0.0 copy-done.6
  11.1 0.1 eq.21
  11.2 0.0 copy-done.5
  11.2 0.2 compare_convert_fusion.select_ref
  11.4 0.0 copy-done.7
  11.5 5.3 %all-to-all-done.recv_ref = f32[8,8,640]{2,1,0:T(8,128)S(1)} async-done(((f32[8,8,640]{2,1,0:T(8,128)}), f32[8,8,640]{2,1,0:T(8,128)S(1)}, u32[]{:S(2)}, u32[]{:S(2)}) %all-to-all-start) | async-done | bytes 163872 | tf_op jit(solution)/shard_map/all_to_all | solution.py:329
  16.8 0.1 broadcast_in_dim.5.col_ref
  16.9 0.1 broadcast_in_dim.4.row_ref
  16.9 0.0 copy-done
  16.9 0.0 copy-done.2
  16.9 0.0 copy-done.3
  16.9 0.0 copy-start.1
  17.0 1.4 %copy-done.1 = bf16[2,640,640]{2,1,0:T(8,128)(2,1)S(1)} copy-done((bf16[2,640,640]{2,1,0:T(8,128)(2,1)S(1)}, bf16[2,640,640]{2,1,0:T(8,128)(2,1)}, u32[]{:S(2)}) %copy-start.1) | copy-done | bytes 1638424
  18.4 1.4 %first_level.1 = (f32[1,4,1280]{2,1,0:T(4,128)S(1)}, f32[40,128]{1,0:T(8,128)S(1)}) custom-call(f32[8,8,640]{2,1,0:T(8,128)S(1)} %all-to-all-done.recv_ref, bf16[640,640]{1,0:T(8,128)(2,1)S(1)} %compare_convert_fusion.select_ref, bf16[2,640,640]{2,1,0:T(8,128)(2,1)S(1)} %copy-done.1, bf16[2,640,640]{2,1,0:T(8,128)(2,1)S(1)} %copy-done, ...), custom_call_target="tpu_custom_call" | custom-call | tf_op jit(solution)/shard_map/first_level/pallas_call | solution.py:365
  19.7 1.3 %collective-permute-start = (f32[40,128]{1,0:T(8,128)S(1)}, f32[40,128]{1,0:T(8,128)S(1)}, u32[]{:S(2)}, u32[]{:S(2)}) collective-permute-start(f32[40,128]{1,0:T(8,128)S(1)} %get-tuple-element.8.below_ref), channel_id=1, source_target_pairs={{8,0},{16,8},{24,16},{9,1},{17,9},{25,17},{10,2},{18,10},{26,18},{... | collective-permute-start | bytes 61448 | tf_op jit(solution)/shard_map/ppermute | solution.py:374
  21.0 1.4 %later_levels.1 = (f32[1,4,1280]{2,1,0:T(4,128)S(1)}, f32[1,40,128]{2,1,0:T(8,128)S(1)}, f32[40,128]{1,0:T(8,128)S(1)}) custom-call(f32[8,8,640]{2,1,0:T(8,128)S(1)} %all-to-all-done.recv_ref, bf16[640,640]{1,0:T(8,128)(2,1)S(1)} %compare_convert_fusion.select_ref, bf16[2,640,640]{2,1,0:T(8,128)(2,1)S(1)} %copy-done.1, bf16[2,640,640]{2,1,0:T(8,128)(2,1)S(1)} %copy-done, ...), custom_call_target="tpu_custom_call" | custom-call | flops 100000000 | bytes 4000000 | tf_op jit(solution)/shard_map/later_levels/pallas_call | solution.py:375
  22.4 0.6 %pad_maximum_fusion = f32[2,4,1280]{2,1,0:T(4,128)} fusion(f32[1,4,1280]{2,1,0:T(4,128)S(1)} %get-tuple-element.9, f32[1,4,1280]{2,1,0:T(4,128)S(1)} %get-tuple-element.7), kind=kLoop, calls=%fused_computation.2 | loop fusion | flops 10240 | bytes 81920 | tf_op jit(solution)/shard_map/concatenate | solution.py:391
  23.0 2.4 %collective-permute-done.above_ref = f32[40,128]{1,0:T(8,128)S(1)} collective-permute-done((f32[40,128]{1,0:T(8,128)S(1)}, f32[40,128]{1,0:T(8,128)S(1)}, u32[]{:S(2)}, u32[]{:S(2)}) %collective-permute-start) | collective-permute-done | bytes 20512 | tf_op jit(solution)/shard_map/ppermute | solution.py:374
  25.4 0.6 %pad_maximum_fusion.1 = f32[2,4,1280]{2,1,0:T(4,128)} fusion(f32[1,4,1280]{2,1,0:T(4,128)S(1)} %concatenate.14, f32[1,4,1280]{2,1,0:T(4,128)S(1)} %concatenate.13), kind=kLoop, calls=%fused_computation.3 | loop fusion | flops 10240 | bytes 81920 | tf_op jit(solution)/shard_map/concatenate | solution.py:400
  (8 shorter events, 0.1 us)
Async XLA Ops:
  0.6 10.6 %copy-start.5 = (s32[640]{0:T(1024)S(1)}, s32[640]{0:T(1024)}, u32[]{:S(2)}) copy-start(s32[640]{0:T(1024)} %constant.62) | copy-start | bytes 7684
  0.6 16.3 %copy-start = (bf16[2,640,640]{2,1,0:T(8,128)(2,1)S(1)}, bf16[2,640,640]{2,1,0:T(8,128)(2,1)}, u32[]{:S(2)}) copy-start(bf16[2,640,640]{2,1,0:T(8,128)(2,1)} %constant.60.clone.low_ref) | copy-start | bytes 4915204
  0.7 10.2 %copy-start.4 = (s32[320]{0:T(512)S(1)}, s32[320]{0:T(512)}, u32[]{:S(2)}) copy-start(s32[320]{0:T(512)} %low_ref.3) | copy-start | bytes 3844
  0.7 10.3 %copy-start.6 = (s32[40]{0:T(128)S(1)}, s32[40]{0:T(128)}, u32[]{:S(2)}) copy-start(s32[40]{0:T(128)} %param.14) | copy-start | bytes 484
  0.7 10.8 %copy-start.7 = (s32[40]{0:T(128)S(1)}, s32[40]{0:T(128)}, u32[]{:S(2)}) copy-start(s32[40]{0:T(128)} %param.13) | copy-start | bytes 484
  0.7 16.2 %copy-start.2 = (s32[40,128]{1,0:T(8,128)S(1)}, s32[40,128]{1,0:T(8,128)}, u32[]{:S(2)}) copy-start(s32[40,128]{1,0:T(8,128)} %tilt_ref.5) | copy-start | bytes 61444
  0.7 16.2 %copy-start.3 = (s32[40,128]{1,0:T(8,128)S(1)}, s32[40,128]{1,0:T(8,128)}, u32[]{:S(2)}) copy-start(s32[40,128]{1,0:T(8,128)} %lon_ref.3) | copy-start | bytes 61444
  5.7 11.1 %all-to-all-start = ((f32[8,8,640]{2,1,0:T(8,128)}), f32[8,8,640]{2,1,0:T(8,128)S(1)}, u32[]{:S(2)}, u32[]{:S(2)}) async-start(f32[8,8,640]{2,1,0:T(8,128)} %legendre.1), calls=%async_computation | async-start | bytes 327680 | tf_op jit(solution)/shard_map/all_to_all | solution.py:329
  16.9 1.4 %copy-start.1 = (bf16[2,640,640]{2,1,0:T(8,128)(2,1)S(1)}, bf16[2,640,640]{2,1,0:T(8,128)(2,1)}, u32[]{:S(2)}) copy-start(bf16[2,640,640]{2,1,0:T(8,128)(2,1)} %constant.59.clone.high_ref) | copy-start | bytes 4915204
  19.7 5.7 %collective-permute-start = (f32[40,128]{1,0:T(8,128)S(1)}, f32[40,128]{1,0:T(8,128)S(1)}, u32[]{:S(2)}, u32[]{:S(2)}) collective-permute-start(f32[40,128]{1,0:T(8,128)S(1)} %get-tuple-element.8.below_ref), channel_id=1, source_target_pairs={{8,0},{16,8},{24,16},{9,1},{17,9},{25,17},{10,2},{18,10},{26,18},{... | collective-permute-start | bytes 61448 | tf_op jit(solution)/shard_map/ppermute | solution.py:374
where the time goes:
time: 26.4 us; the launch traced here: 26.1 us
  Pallas kernels  7.74 us (29%)
  waiting for transfers between devices  7.69 us (29%)
  starting transfers between devices  6.46 us (24%)
  local copies, waits for them, and re-layouts  1.85 us (7%)
  other arithmetic  1.52 us (6%)
  between operations  0.8 us (3%)
    all_to_all x1, waiting for transfers between devices, per_device(): lax.all_to_all(sums, 'wave', split_axis=0, concat_axis=0, tiled=True)  5.33 us
    all_to_all x1, starting transfers between devices, per_device(): lax.all_to_all(sums, 'wave', split_axis=0, concat_axis=0, tiled=True)  5.17 us
    pallas_call x1, Pallas kernels, legendre_sums(): pl.pallas_call(functools.partial(legendre_kernel, slot_count, pair_local,...  5.02 us
    ppermute x1, waiting for transfers between devices, per_device(): lax.ppermute(horizontal, 'lev', [(i, i - 1) for i in range(1, lev_size)])  2.37 us
    unnamed x16, local copies, waits for them, and re-layouts  1.46 us
    pallas_call x1, Pallas kernels, per_device(): pl.pallas_call(functools.partial(later_kernel, lat_dev), in_specs=[vmem]...  1.36 us
    pallas_call x1, Pallas kernels, per_device(): pl.pallas_call(functools.partial(first_kernel, lat_dev), in_specs=[vmem]...  1.35 us
    ppermute x1, starting transfers between devices, per_device(): lax.ppermute(horizontal, 'lev', [(i, i - 1) for i in range(1, lev_size)])  1.29 us
  transfers between devices with their start and end apart: 2, of which 2 were waited for; matrix products, arithmetic and copies ran while one was open for 4% of the time, Pallas kernels for 5%

commit v1 on v0

v1 whole, which is shorter than its diff:
```python
import functools
import math

import jax
import jax.numpy as jnp
import ml_dtypes
import numpy as np
from jax import lax
from jax.experimental import pallas as pl
from jax.experimental.pallas import tpu as pltpu
from jax.sharding import PartitionSpec as P

LANES = 128
GROUP = 8
HALO = 2
MIB = 1024 * 1024
NT = (((1,), (1,)), ((), ()))
NN = (((1,), (0,)), ((), ()))


def split(value):
    high = value.astype(jnp.bfloat16)
    low = (value - high.astype(jnp.float32)).astype(jnp.bfloat16)
    return high, low


def widen(value, width):
    lane = lax.broadcasted_iota(jnp.int32, (value.shape[0], LANES), 1)
    full = value.shape[1] // LANES * LANES
    parts = [value[:, :full]]
    for start in range(full, value.shape[1]):
        column = jnp.broadcast_to(value[:, start : start + 1], lane.shape)
        parts.append(jnp.where(lane == start - full, column, 0.0))
    assert len(parts) <= 2 and full + LANES * (len(parts) - 1) == width
    return jnp.concatenate(parts, axis=1)


def legendre_kernel(
    pair_local,
    lat_dev,
    low_hbm,
    spec_hbm,
    leg_hbm,
    *refs,
):
    chip_refs = refs[:-7]
    low_ref, spec_ref, leg_ref, sums_ref, low_sem, spec_sem, leg_sem = refs[-7:]
    slots, lat_all, slot_count = leg_ref.shape
    level_count = spec_ref.shape[1]
    pair_total = low_ref.shape[0]
    ext_pad = sums_ref.shape[1]
    width = pl.cdiv(slot_count, LANES) * LANES
    low_copy = pltpu.make_async_copy(low_hbm, low_ref, low_sem)
    low_copy.start()
    copies = []
    for start in range(0, slots, GROUP):
        part = pl.ds(start, GROUP)
        index = start // GROUP
        pair = (
            pltpu.make_async_copy(spec_hbm.at[part], spec_ref.at[part], spec_sem.at[index]),
            pltpu.make_async_copy(leg_hbm.at[part], leg_ref.at[part], leg_sem.at[index]),
        )
        for copy in pair:
            copy.start()
        copies.append(pair)
    wave = lax.axis_index("wave")
    slot_of_row = lax.broadcasted_iota(jnp.int32, (GROUP, LANES), 0)
    slot_pos = lax.broadcasted_iota(jnp.int32, (GROUP, width), 1)
    low_copy.wait()
    for start in range(0, slots, GROUP):
        base = wave * pair_local + start
        first = jnp.zeros((GROUP, LANES), jnp.int32)
        for slot in range(GROUP):
            low = low_ref[jnp.minimum(base + slot, pair_total - 1)]
            first = jnp.where(slot_of_row == slot, slot_count - 1 - low, first)
        first = jnp.concatenate([first] * (width // LANES), axis=1)
        second = slot_pos >= first
        sign = (1 - 2 * ((slot_pos - jnp.where(second, first, 0)) & 1)).astype(jnp.float32)
        member = [jnp.where(second, 0.0, 1.0), jnp.where(second, 1.0, 0.0)]
        masks = [
            jnp.concatenate(member, axis=0).astype(jnp.bfloat16),
            jnp.concatenate([m * sign for m in member], axis=0).astype(jnp.bfloat16),
        ]
        for copy in copies[start // GROUP]:
            copy.wait()
        highs, lows = [], []
        for level in range(level_count):
            for part in range(2):
                row = widen(spec_ref[pl.ds(start, GROUP), level, part, :], width)
                high, low = split(jnp.concatenate([row, row], axis=0))
                highs += [high * mask for mask in masks]
                lows += [low * mask for mask in masks]
        columns = jnp.concatenate(highs + lows, axis=0)
        count = columns.shape[0] // 2
        half = GROUP * lat_all
        table = leg_ref[pl.ds(start, GROUP)].reshape(half, slot_count)
        rows = jnp.concatenate(split(widen(table, width)), axis=0)
        crossed = lax.dot_general(rows, columns, NT, preferred_element_type=jnp.float32)
        crossed = (crossed[:half, :count] + crossed[:half, count:]) + (
            crossed[half:, :count] + crossed[half:, count:]
        )
        slot_of_lane = lax.broadcasted_iota(jnp.int32, (lat_all, count), 1) % GROUP
        sums = crossed[:lat_all]
        for slot in range(1, GROUP):
            block = crossed[slot * lat_all : (slot + 1) * lat_all]
            sums = jnp.where(slot_of_lane == slot, block, sums)
        edge = jnp.zeros((HALO, count), jnp.float32)
        tail = jnp.zeros((ext_pad, count), jnp.float32)
        padded = jnp.concatenate([edge, sums, tail], axis=0)
        here = slice(start // GROUP * count, (start // GROUP + 1) * count)
        for dest in range(sums_ref.shape[0]):
            sums_ref[dest, :, here] = padded[dest * lat_dev : dest * lat_dev + ext_pad]
    for step, chip_ref in enumerate(chip_refs):
        dest = (wave // 2 ^ step) * 2
        for core in range(2):
            chip_ref[core] = sums_ref[dest + core]


def legendre_sums(pair_low, spectral, legendre, pair_local, wave_size):
    slots, level_count = spectral.shape[:2]
    lat_all, slot_count = legendre.shape[1:]
    lat_dev = lat_all // wave_size
    lanes = 8 * level_count * slots
    ext_pad = pl.cdiv(lat_dev + 2 * HALO, 8) * 8
    chips = wave_size // 2
    out = jax.ShapeDtypeStruct((2, ext_pad, lanes), jnp.float32)
    operands = [
        pltpu.with_memory_space_constraint(x, pltpu.HBM) for x in (pair_low, spectral, legendre)
    ]
    return pl.pallas_call(
        functools.partial(legendre_kernel, pair_local, lat_dev),
        in_specs=[pl.BlockSpec(memory_space=pltpu.HBM)] * 3,
        out_specs=[pl.BlockSpec(memory_space=pltpu.VMEM)] * chips,
        out_shape=[out] * chips,
        scratch_shapes=[
            pltpu.SMEM(pair_low.shape, jnp.int32),
            pltpu.VMEM(spectral.shape, jnp.float32),
            pltpu.VMEM(legendre.shape, jnp.float32),
            pltpu.VMEM((wave_size, ext_pad, lanes), jnp.float32),
            pltpu.SemaphoreType.DMA,
            pltpu.SemaphoreType.DMA((slots // GROUP,)),
            pltpu.SemaphoreType.DMA((slots // GROUP,)),
        ],
        compiler_params=pltpu.CompilerParams(vmem_limit_bytes=24 * MIB),
        name="legendre",
    )(*operands)


def swap(value, by):
    wave_size = lax.axis_size("wave")
    return lax.ppermute(value, "wave", [(i, i ^ by) for i in range(wave_size)])


def plan_kernel(
    pair_local,
    lat_dev,
    after_ref,
    low_hbm,
    lat_hbm,
    col_hbm,
    lon_hbm,
    tilt_hbm,
    table_hbm,
    select_ref,
    row_step_ref,
    place_ref,
    lon_frac_ref,
    lat_frac_ref,
    vertical_ref,
    table_ref,
    low_ref,
    lat_ref,
    col_ref,
    lon_ref,
    tilt_ref,
    sems,
):
    pairs = [
        (low_hbm, low_ref),
        (lat_hbm, lat_ref),
        (col_hbm, col_ref),
        (lon_hbm, lon_ref),
        (tilt_hbm, tilt_ref),
        (table_hbm, table_ref),
    ]
    copies = [
        pltpu.make_async_copy(there, here, sems.at[i]) for i, (there, here) in enumerate(pairs)
    ]
    for copy in copies:
        copy.start()
    for copy in copies[:-1]:
        copy.wait()
    wave = lax.axis_index("wave")
    half, slot_lanes = select_ref.shape
    lon_count = 2 * half
    points = lon_ref.shape[0]
    blocks = points // (2 * lat_dev)
    sources = low_ref.shape[0] // pair_local
    per_source = slot_lanes // (sources * 2 * GROUP)
    lane = lax.broadcasted_iota(jnp.int32, (GROUP, LANES), 1)
    order = lax.broadcasted_iota(jnp.int32, (half, LANES), 0)
    order = jnp.where(order < half // 2, 2 * order, 2 * order - half + 1)
    per_vector = LANES // (2 * GROUP)
    for block in range(slot_lanes // LANES):
        waves = jnp.full((GROUP, LANES), -2 * half, jnp.int32)
        for index in range(per_vector):
            source, group = divmod(block * per_vector + index, per_source)
            base = (wave ^ source) * pair_local + group * GROUP
            for slot in range(min(GROUP, pair_local - group * GROUP)):
                here = (lane & ~GROUP) == index * 2 * GROUP + slot
                waves = jnp.where(here, low_ref[base + slot], waves)
        waves = jnp.where((lane & GROUP) != 0, half - 1 - waves, waves)
        match = jnp.broadcast_to(waves[0:1], order.shape) == order
        select_ref[:, block * LANES : (block + 1) * LANES] = jnp.where(match, 1.0, 0.0).astype(
            jnp.bfloat16
        )
    row = lax.broadcasted_iota(jnp.int32, (points, LANES), 0)
    point = lax.broadcasted_iota(jnp.int32, (points, LANES), 1)
    row_step = jnp.zeros((points, LANES), jnp.int32)
    col_step = jnp.zeros((points, LANES), jnp.int32)
    for index in range(points):
        own = wave * lat_dev + index // blocks % lat_dev - HALO
        row_step = jnp.where(row == index, lat_ref[index] - own, row_step)
        first = LANES * (index % blocks)
        col_step = jnp.where(row == index, col_ref[index] - first, col_step)
    col_step = jnp.where(col_step >= half, col_step - lon_count, col_step)
    col_step = jnp.where(col_step < -half, col_step + lon_count, col_step)
    quarters = 4 * col_step + lon_ref[...] - 12
    row_step_ref[...] = row_step
    place_ref[...] = point + (quarters >> 2)
    lon_frac_ref[...] = (quarters & 3).astype(jnp.float32) * 0.25
    lat_frac_ref[...] = (tilt_ref[...] & 3).astype(jnp.float32) * 0.25
    vertical_ref[...] = (tilt_ref[...] >> 2).astype(jnp.float32) * 0.25
    copies[-1].wait()


def plan(after, tables, pair_low, dep_lat, dep_col, lon_steps, tilt_steps, pair_local, lat_dev, lanes):
    vmem = pl.BlockSpec(memory_space=pltpu.VMEM)
    whole = jax.ShapeDtypeStruct(lon_steps.shape, jnp.int32)
    fraction = jax.ShapeDtypeStruct(lon_steps.shape, jnp.float32)
    half = tables.shape[1]
    operands = [
        pltpu.with_memory_space_constraint(x, pltpu.HBM)
        for x in (pair_low, dep_lat, dep_col, lon_steps, tilt_steps, tables)
    ]
    return pl.pallas_call(
        functools.partial(plan_kernel, pair_local, lat_dev),
        in_specs=[pl.BlockSpec(memory_space=pl.ANY)]
        + [pl.BlockSpec(memory_space=pltpu.HBM)] * len(operands),
        out_specs=[vmem] * 7,
        out_shape=[
            jax.ShapeDtypeStruct((half, lanes), jnp.bfloat16),
            whole,
            whole,
            fraction,
            fraction,
            fraction,
            jax.ShapeDtypeStruct(tables.shape, tables.dtype),
        ],
        scratch_shapes=[
            pltpu.SMEM(pair_low.shape, jnp.int32),
            pltpu.SMEM(dep_lat.shape, jnp.int32),
            pltpu.SMEM(dep_col.shape, jnp.int32),
            pltpu.VMEM(lon_steps.shape, jnp.int32),
            pltpu.VMEM(tilt_steps.shape, jnp.int32),
            pltpu.SemaphoreType.DMA((len(operands),)),
        ],
        compiler_params=pltpu.CompilerParams(vmem_limit_bytes=24 * MIB),
        cost_estimate=pl.CostEstimate(
            flops=10**7, bytes_accessed=4 * 10**6, transcendentals=0
        ),
        name="plan",
    )(after, *operands)


def fourier_tables(wavenumber_count):
    lon_count = 2 * wavenumber_count
    half_lon = lon_count // 2
    tables = []
    for parity in range(2):
        wave = np.arange(parity, wavenumber_count, 2)
        phase = wave[:, None] * np.arange(half_lon)[None, :] % lon_count
        angle = phase * (2.0 * math.pi / lon_count)
        weight = np.where(wave == 0, 1.0, 2.0)[:, None]
        parts = [weight * np.cos(angle), -weight * np.sin(angle)]
        tables.append(np.concatenate(parts if parity == 0 else parts[::-1], axis=0))
    exact = np.stack(tables)
    high = exact.astype(ml_dtypes.bfloat16)
    low = (exact - high.astype(np.float64)).astype(ml_dtypes.bfloat16)
    return np.concatenate([high, low], axis=2)


def regroup(pieces, level, lane):
    piece_lanes = LANES // 8
    upper = lane // piece_lanes >= 4
    if level == 0:
        pieces = [
            jnp.where(upper, pltpu.roll(pieces[i + 4], 4 * piece_lanes, 1), pieces[i])
            for i in range(4)
        ]
    else:
        pieces = [
            jnp.where(upper, pieces[i + 4], pltpu.roll(pieces[i], 4 * piece_lanes, 1))
            for i in range(4)
        ]
    for bit in (1, 2):
        upper = (lane // piece_lanes & bit) != 0
        for one in range(4):
            if one & bit:
                continue
            a, b = pieces[one], pieces[one | bit]
            pieces[one] = jnp.where(upper, pltpu.roll(b, piece_lanes * bit, 1), a)
            pieces[one | bit] = jnp.where(
                upper, b, pltpu.roll(a, LANES - piece_lanes * bit, 1)
            )
    return pieces


def level_rows(level, piece_refs, select_ref, table_ref):
    half = table_ref.shape[2] // 2
    core = lax.axis_index("wave") % 2
    vectors = []
    for ref in piece_refs:
        source = ref[core]
        vectors += [
            source[:, start : start + LANES] for start in range(0, source.shape[1], LANES)
        ]
    lane = lax.broadcasted_iota(jnp.int32, vectors[0].shape, 1)
    columns = [[] for _ in range(4)]
    for start in range(0, len(vectors), 8):
        for kind, piece in enumerate(regroup(vectors[start : start + 8], level, lane)):
            columns[kind].append(piece)
    matrix = jnp.concatenate([jnp.concatenate(c, axis=1) for c in columns], axis=0)
    high, low = split(matrix)
    count = high.shape[0] // 2
    ordered = lax.dot_general(
        jnp.concatenate([high[:count], low[:count], high[count:], low[count:]], axis=0),
        select_ref[...],
        NT,
        preferred_element_type=jnp.float32,
    )
    real = ordered[: 2 * count]
    imag = pltpu.roll(ordered[2 * count :], half // 2, 1)
    first_half = lax.broadcasted_iota(jnp.int32, real.shape, 1) < half // 2
    even = jnp.where(first_half, real, imag).astype(jnp.bfloat16)
    odd = jnp.where(first_half, imag, real).astype(jnp.bfloat16)
    sums = []
    for parity, operand in enumerate((even, odd)):
        main = lax.dot_general(
            operand, table_ref[parity], NN, preferred_element_type=jnp.float32
        )
        sums.append(main[:count, :half] + (main[count:, :half] + main[:count, half:]))
    return sums


def interpolate(sums, field_ref, level, lat_dev, row_step, step, f, g, near_ref):
    half = sums[0].shape[1]
    count = sums[0].shape[0]
    ext_pad = count // 2
    blocks = 2 * half // LANES
    for block in range(blocks // 2):
        here = slice(block * LANES, (block + 1) * LANES)
        for at, rows in (
            (block, sums[0][:, here] + sums[1][:, here]),
            (block + blocks // 2, sums[0][:, here] - sums[1][:, here]),
        ):
            there = slice(at * LANES, (at + 1) * LANES)
            for hemi in range(2):
                start = hemi * ext_pad + HALO
                field_ref[level, hemi * lat_dev : (hemi + 1) * lat_dev, there] = rows[
                    start : start + lat_dev
                ]
            for side in range(3):
                place = (at + 1 - side) % blocks
                near_ref[side, pl.ds(place, count, stride=blocks), :] = rows
    points = 2 * lat_dev * blocks
    point = lax.broadcasted_iota(jnp.int32, (points, LANES), 1)

    def line(side, j):
        return jnp.concatenate(
            [
                near_ref[side, pl.ds((hemi * ext_pad + j) * blocks, lat_dev * blocks), :]
                for hemi in range(2)
            ],
            axis=0,
        )

    lines = [[line(side, j) for j in range(2 * HALO + 1)] for side in range(3)]
    values = []
    for upper in range(2):
        picked = []
        for side in range(3):
            choice = lines[side][upper]
            for j in range(1, 2 * HALO):
                choice = jnp.where(row_step == j, lines[side][j + upper], choice)
            picked.append(choice)
        left = jnp.where(point >= LANES - 28, picked[0], picked[1])
        right = jnp.where(point < 28, picked[2], picked[1])
        for shift in range(2):
            place = (step + shift) & (LANES - 1)
            values.append(
                jnp.where(
                    point < LANES // 2,
                    jnp.take_along_axis(left, place, axis=1),
                    jnp.take_along_axis(right, place, axis=1),
                )
            )
    lower = (1.0 - f) * values[0] + f * values[1]
    higher = (1.0 - f) * values[2] + f * values[3]
    return (1.0 - g) * lower + g * higher


def first_kernel(lat_dev, piece_count, *refs):
    piece_refs, plan_refs = refs[:piece_count], refs[piece_count + 2 : -3]
    select_ref, table_ref = refs[piece_count : piece_count + 2]
    field_ref, horizontal_ref, near_ref = refs[-3:]
    sums = level_rows(0, piece_refs, select_ref, table_ref)
    plans = [ref[...] for ref in plan_refs]
    horizontal_ref[...] = interpolate(sums, field_ref, 0, lat_dev, *plans, near_ref)


def later_kernel(lat_dev, piece_count, *refs):
    piece_refs, plan_refs = refs[:piece_count], refs[piece_count + 2 : -6]
    select_ref, table_ref = refs[piece_count : piece_count + 2]
    vertical_ref, below_ref, field_ref, departed_ref, horizontal_ref, near_ref = refs[-6:]
    vertical = vertical_ref[...]
    below = below_ref[...]
    plans = [ref[...] for ref in plan_refs]
    for level in range(1, departed_ref.shape[0] + 1):
        sums = level_rows(level, piece_refs, select_ref, table_ref)
        horizontal = interpolate(sums, field_ref, level - 1, lat_dev, *plans, near_ref)
        departed_ref[level - 1] = (1.0 - vertical) * below + vertical * horizontal
        below = horizontal
    horizontal_ref[...] = below


def last_kernel(below_ref, above_ref, vertical_ref, out_ref):
    is_last = lax.axis_index("lev") == lax.axis_size("lev") - 1
    vertical = vertical_ref[...]
    below = below_ref[...]
    above = jnp.where(is_last, below, above_ref[...])
    out_ref[...] = (1.0 - vertical) * below + vertical * above


def per_device(legendre, spectral, pair_low, dep_lat, dep_col, lon_steps, tilt_steps):
    pair_local, level_count, _, slot_count = spectral.shape
    wavenumber_count = slot_count - 1
    lon_count = 2 * wavenumber_count
    lat_all = legendre.shape[1]
    wave_size = lax.axis_size("wave")
    lev_size = lax.axis_size("lev")
    lat_dev = lat_all // wave_size
    slots = pl.cdiv(pair_local, GROUP) * GROUP
    extra = slots - pair_local
    if extra:
        spectral = jnp.pad(spectral, ((0, extra), (0, 0), (0, 0), (0, 0)))
        legendre = jnp.pad(legendre, ((0, extra), (0, 0), (0, 0)))
    parts = legendre_sums(pair_low, spectral, legendre, pair_local, wave_size)
    received = [swap(part, 2 * step) if step else part for step, part in enumerate(parts)]
    blocks = lon_count // LANES
    points = 2 * lat_dev * blocks
    ext_pad = parts[0].shape[1]
    select, *plans, vertical, tables = plan(
        parts[0],
        jnp.asarray(fourier_tables(wavenumber_count)),
        pair_low,
        dep_lat,
        dep_col,
        lon_steps,
        tilt_steps,
        pair_local,
        lat_dev,
        2 * wave_size * slots,
    )
    *received, select = lax.optimization_barrier((*received, select))
    pieces = []
    for piece in received:
        pieces += [piece, swap(piece, 1)]
    vmem = pl.BlockSpec(memory_space=pltpu.VMEM)
    params = pltpu.CompilerParams(vmem_limit_bytes=24 * MIB)
    operands = (
        *pieces,
        select,
        tables,
        *plans,
    )
    near = pltpu.VMEM((3, 2 * ext_pad * blocks, LANES), jnp.float32)
    flat = jax.ShapeDtypeStruct((points, LANES), jnp.float32)
    field_first, horizontal = pl.pallas_call(
        functools.partial(first_kernel, lat_dev, len(pieces)),
        in_specs=[vmem] * len(operands),
        out_specs=[vmem] * 2,
        out_shape=[jax.ShapeDtypeStruct((1, 2 * lat_dev, lon_count), jnp.float32), flat],
        scratch_shapes=[near],
        compiler_params=params,
        cost_estimate=pl.CostEstimate(
            flops=10**8, bytes_accessed=4 * 10**6, transcendentals=0
        ),
        name="first_level",
    )(*operands)
    above = lax.ppermute(horizontal, "lev", [(i, i - 1) for i in range(1, lev_size)])
    field_later, departed, top = pl.pallas_call(
        functools.partial(later_kernel, lat_dev, len(pieces)),
        in_specs=[vmem] * (len(operands) + 2),
        out_specs=[vmem] * 3,
        out_shape=[
            jax.ShapeDtypeStruct((level_count - 1, 2 * lat_dev, lon_count), jnp.float32),
            jax.ShapeDtypeStruct((level_count - 1, points, LANES), jnp.float32),
            flat,
        ],
        scratch_shapes=[near],
        compiler_params=params,
        cost_estimate=pl.CostEstimate(
            flops=10**8, bytes_accessed=4 * 10**6, transcendentals=0
        ),
        name="later_levels",
    )(*operands, vertical, horizontal)
    grid_field = jnp.concatenate([field_first, field_later], axis=0)
    final = pl.pallas_call(
        last_kernel,
        in_specs=[vmem] * 3,
        out_specs=vmem,
        out_shape=flat,
        compiler_params=params,
        name="top_level",
    )(top, above, vertical)
    departed = jnp.concatenate([departed, final[None]], axis=0)
    return grid_field, departed.reshape(level_count, 2 * lat_dev, lon_count)


def solution(mesh):
    return jax.shard_map(
        per_device,
        mesh=mesh,
        in_specs=(
            P("wave", None, None),
            P("wave", "lev", None, None),
            P(),
            P("wave"),
            P("wave"),
            P("wave", None),
            P("wave", None),
        ),
        out_specs=(P("lev", "wave", None), P("lev", "wave", None)),
        check_vma=False,
    )
```

time: 26.4 us -> 23 us (0.87)
  local copies, waits for them, and re-layouts: 1.85 us -> 0.03 us
  waiting for transfers between devices: 7.69 us -> 6.05 us
  starting transfers between devices: 6.46 us -> 6.85 us
    ppermute x0 -> x7, starting transfers between devices: none -> 5.56 us  [swap(): return lax.ppermute(value, 'wave', [(i, i ^ by) for i in range(wave_size)])]
    all_to_all x1 -> x0, waiting for transfers between devices: 5.33 us -> none  [per_device(): lax.all_to_all(sums, 'wave', split_axis=0, concat_axis=0, tiled=True)]
    all_to_all x1 -> x0, starting transfers between devices: 5.17 us -> none  [per_device(): lax.all_to_all(sums, 'wave', split_axis=0, concat_axis=0, tiled=True)]
    ppermute x0 -> x7, waiting for transfers between devices: none -> 3.72 us  [swap(): return lax.ppermute(value, 'wave', [(i, i ^ by) for i in range(wave_size)])]
    unnamed x16 -> x0, local copies, waits for them, and re-layouts: 1.46 us -> none
    pallas_call x3 -> x4, Pallas kernels: 7.73 us -> 7.93 us  [the longest x1 3.15 us: legendre_sums(): pl.pallas_call(functools.partial(legendre_kernel, pair_local, lat_dev), i...]
  transfers between devices with their start and end apart: 2 -> 8, of which waited for: 2 -> 7; matrix products, arithmetic and copies ran while one was open for 4% -> 3% of each run, Pallas kernels for 5% -> 15%
where the time goes in v1:
time: 23 us; the launch traced here: 22.8 us
  Pallas kernels  7.94 us (35%)
  starting transfers between devices  6.85 us (30%)
  waiting for transfers between devices  6.05 us (26%)
  other arithmetic  1.26 us (5%)
  between operations  0.69 us (3%)
    ppermute x7, starting transfers between devices, swap(): return lax.ppermute(value, 'wave', [(i, i ^ by) for i in range(wave_size)])  5.56 us
    ppermute x7, waiting for transfers between devices, swap(): return lax.ppermute(value, 'wave', [(i, i ^ by) for i in range(wave_size)])  3.72 us
    pallas_call x1, Pallas kernels, legendre_sums(): pl.pallas_call(functools.partial(legendre_kernel, pair_local, lat_dev), i...  3.15 us
    ppermute x1, waiting for transfers between devices, per_device(): lax.ppermute(horizontal, 'lev', [(i, i - 1) for i in range(1, lev_size)])  2.33 us
    pallas_call x1, Pallas kernels, plan(): pl.pallas_call(functools.partial(plan_kernel, pair_local, lat_dev), in_sp...  2.01 us
    pallas_call x1, Pallas kernels, per_device(): pl.pallas_call(functools.partial(later_kernel, lat_dev, len(pieces)), in_...  1.39 us
    pallas_call x1, Pallas kernels, per_device(): pl.pallas_call(functools.partial(first_kernel, lat_dev, len(pieces)), in_...  1.38 us
    ppermute x1, starting transfers between devices, per_device(): lax.ppermute(horizontal, 'lev', [(i, i - 1) for i in range(1, lev_size)])  1.29 us
  transfers between devices with their start and end apart: 8, of which 7 were waited for; matrix products, arithmetic and copies ran while one was open for 3% of the time, Pallas kernels for 15%

profile of v1, /device:TPU:0, one launch (start us, length us, event | category | flops | bytes accessed | tf_op | source)
XLA Modules:
  0.0 22.8 jit_solution(12076774397765012366)
XLA Ops:
  0.6 3.1 %legendre.1 = (f32[2,8,640]{2,1,0:T(8,128)S(1)}, f32[2,8,640]{2,1,0:T(8,128)S(1)}, f32[2,8,640]{2,1,0:T(8,128)S(1)}, f32[2,8,640]{2,1,0:T(8,128)S(1)}) custom-call(s32[320]{0:T(512)} %low_hbm.3, f32[40,2,2,641]{3,2,1,0:T(2,128)} %spec_hbm.1, f32[40,16,641]{2,1,0:T(8,128)} %leg_hbm.1), custom_call_target="tpu_custom_call" | custom-call | tf_op jit(solution)/shard_map/legendre/pallas_call | solution.py:130
  3.8 3.0 %collective-permute-start = (f32[2,8,640]{2,1,0:T(8,128)S(1)}, f32[2,8,640]{2,1,0:T(8,128)S(1)}, u32[]{:S(2)}, u32[]{:S(2)}) collective-permute-start(f32[2,8,640]{2,1,0:T(8,128)S(1)} %get-tuple-element.24), channel_id=1, source_target_pairs={{0,2},{1,3},{2,0},{3,1},{4,6},{5,7},{6,4},{7,5},{8,10},{9,11},{10,... | collective-permute-start | bytes 122888 | tf_op jit(solution)/shard_map/ppermute | solution.py:151
  6.8 1.5 %collective-permute-start.1 = (f32[2,8,640]{2,1,0:T(8,128)S(1)}, f32[2,8,640]{2,1,0:T(8,128)S(1)}, u32[]{:S(2)}, u32[]{:S(2)}) collective-permute-start(f32[2,8,640]{2,1,0:T(8,128)S(1)} %get-tuple-element.25), channel_id=1, source_target_pairs={{0,4},{1,5},{2,6},{3,7},{4,0},{5,1},{6,2},{7,3},{8,12},{9,13},{10,... | collective-permute-start | bytes 122888 | tf_op jit(solution)/shard_map/ppermute | solution.py:151
  8.3 0.0 collective-permute-start.2
  8.3 2.0 %plan.1 = (bf16[640,640]{1,0:T(8,128)(2,1)S(1)}, s32[40,128]{1,0:T(8,128)S(1)}, s32[40,128]{1,0:T(8,128)S(1)}, f32[40,128]{1,0:T(8,128)S(1)}, f32[40,128]{1,0:T(...) custom-call(f32[2,8,640]{2,1,0:T(8,128)S(1)} %get-tuple-element.28.after_ref.refs_0_, s32[320]{0:T(512)} %low_hbm.3, ...), custom_call_target="tpu_custom_call" | custom-call | flops 10000000 | bytes 4000000 | tf_op jit(solution)/shard_map/plan/pallas_call | solution.py:246
  10.3 0.0 collective-permute-done.refs_2_
  10.4 0.4 %collective-permute-done.1.refs_4_ = f32[2,8,640]{2,1,0:T(8,128)S(1)} collective-permute-done((f32[2,8,640]{2,1,0:T(8,128)S(1)}, f32[2,8,640]{2,1,0:T(8,128)S(1)}, u32[]{:S(2)}, u32[]{:S(2)}) %collective-permute-start.1) | collective-permute-done | bytes 40992 | tf_op jit(solution)/shard_map/ppermute | solution.py:151
  10.8 2.4 %collective-permute-done.2.refs_6_ = f32[2,8,640]{2,1,0:T(8,128)S(1)} collective-permute-done((f32[2,8,640]{2,1,0:T(8,128)S(1)}, f32[2,8,640]{2,1,0:T(8,128)S(1)}, u32[]{:S(2)}, u32[]{:S(2)}) %collective-permute-start.2) | collective-permute-done | bytes 40992 | tf_op jit(solution)/shard_map/ppermute | solution.py:151
  13.2 0.0 collective-permute-start.3
  13.2 0.5 %collective-permute-start.4 = (f32[2,8,640]{2,1,0:T(8,128)S(1)}, f32[2,8,640]{2,1,0:T(8,128)S(1)}, u32[]{:S(2)}, u32[]{:S(2)}) collective-permute-start(f32[2,8,640]{2,1,0:T(8,128)S(1)} %collective-permute-done.refs_2_), channel_id=1, source_target_pairs={{0,1},{1,0},{2,3},{3,2},{4,5},{5,4},{6,7},{7,6},{8,9},{9,8},{10,11... | collective-permute-start | bytes 122888 | tf_op jit(solution)/shard_map/ppermute | solution.py:151
  13.7 0.0 collective-permute-start.5
  13.7 0.5 %collective-permute-start.6 = (f32[2,8,640]{2,1,0:T(8,128)S(1)}, f32[2,8,640]{2,1,0:T(8,128)S(1)}, u32[]{:S(2)}, u32[]{:S(2)}) collective-permute-start(f32[2,8,640]{2,1,0:T(8,128)S(1)} %collective-permute-done.2.refs_6_), channel_id=1, source_target_pairs={{0,1},{1,0},{2,3},{3,2},{4,5},{5,4},{6,7},{7,6},{8,9},{9,8},{10,11... | collective-permute-start | bytes 122888 | tf_op jit(solution)/shard_map/ppermute | solution.py:151
  14.2 0.2 collective-permute-done.3.refs_1_
  14.4 0.2 collective-permute-done.4.refs_3_
  14.6 0.3 %collective-permute-done.5.refs_5_ = f32[2,8,640]{2,1,0:T(8,128)S(1)} collective-permute-done((f32[2,8,640]{2,1,0:T(8,128)S(1)}, f32[2,8,640]{2,1,0:T(8,128)S(1)}, u32[]{:S(2)}, u32[]{:S(2)}) %collective-permute-start.5) | collective-permute-done | bytes 40992 | tf_op jit(solution)/shard_map/ppermute | solution.py:151
  14.9 0.2 collective-permute-done.6.refs_7_
  15.1 1.4 %first_level.1 = (f32[1,4,1280]{2,1,0:T(4,128)S(1)}, f32[40,128]{1,0:T(8,128)S(1)}) custom-call(f32[2,8,640]{2,1,0:T(8,128)S(1)} %get-tuple-element.28.after_ref.refs_0_, f32[2,8,640]{2,1,0:T(8,128)S(1)} %collective-permute-done.3.refs_1_, f32[2,8,640]{2,1,0:T(8,128)S(1)} %collective-permute-done.refs_2_, f32[2,8,640]{2,1,0:T(8,128)S(1)} %collective-permute-done.4.refs_3_, ...), custom_call_target="tpu_custom_call" | custom-call | flops 100000000 | bytes 4000000 | tf_op jit(solution)/shard_map/first_level/pallas_call | solution.py:489
  16.5 1.3 %collective-permute-start.7 = (f32[40,128]{1,0:T(8,128)S(1)}, f32[40,128]{1,0:T(8,128)S(1)}, u32[]{:S(2)}, u32[]{:S(2)}) collective-permute-start(f32[40,128]{1,0:T(8,128)S(1)} %get-tuple-element.40.refs_15_), channel_id=1, source_target_pairs={{8,0},{16,8},{24,16},{9,1},{17,9},{25,17},{10,2},{18,10},{26,18},{... | collective-permute-start | bytes 61448 | tf_op jit(solution)/shard_map/ppermute | solution.py:501
  17.8 1.4 %later_levels.1 = (f32[1,4,1280]{2,1,0:T(4,128)S(1)}, f32[1,40,128]{2,1,0:T(8,128)S(1)}, f32[40,128]{1,0:T(8,128)S(1)}) custom-call(f32[2,8,640]{2,1,0:T(8,128)S(1)} %get-tuple-element.28.after_ref.refs_0_, f32[2,8,640]{2,1,0:T(8,128)S(1)} %collective-permute-done.3.refs_1_, f32[2,8,640]{2,1,0:T(8,128)S(1)} %collective-permute-done.refs_2_, ...), custom_call_target="tpu_custom_call" | custom-call | flops 100000000 | bytes 4000000 | tf_op jit(solution)/shard_map/later_levels/pallas_call | solution.py:502
  19.2 0.6 %pad_maximum_fusion = f32[2,4,1280]{2,1,0:T(4,128)} fusion(f32[1,4,1280]{2,1,0:T(4,128)S(1)} %get-tuple-element.41, f32[1,4,1280]{2,1,0:T(4,128)S(1)} %get-tuple-element.38), kind=kLoop, calls=%fused_computation | loop fusion | flops 10240 | bytes 81920 | tf_op jit(solution)/shard_map/concatenate | solution.py:518
  19.8 2.3 %collective-permute-done.7.above_ref = f32[40,128]{1,0:T(8,128)S(1)} collective-permute-done((f32[40,128]{1,0:T(8,128)S(1)}, f32[40,128]{1,0:T(8,128)S(1)}, u32[]{:S(2)}, u32[]{:S(2)}) %collective-permute-start.7) | collective-permute-done | bytes 20512 | tf_op jit(solution)/shard_map/ppermute | solution.py:501
  22.2 0.6 %pad_maximum_fusion.1 = f32[2,4,1280]{2,1,0:T(4,128)} fusion(f32[1,4,1280]{2,1,0:T(4,128)S(1)} %concatenate.13, f32[1,4,1280]{2,1,0:T(4,128)S(1)} %concatenate.12), kind=kLoop, calls=%fused_computation.1 | loop fusion | flops 10240 | bytes 81920 | tf_op jit(solution)/shard_map/concatenate | solution.py:527
  (3 shorter events, 0.0 us)
Async XLA Ops:
  3.8 6.6 %collective-permute-start = (f32[2,8,640]{2,1,0:T(8,128)S(1)}, f32[2,8,640]{2,1,0:T(8,128)S(1)}, u32[]{:S(2)}, u32[]{:S(2)}) collective-permute-start(f32[2,8,640]{2,1,0:T(8,128)S(1)} %get-tuple-element.24), channel_id=1, source_target_pairs={{0,2},{1,3},{2,0},{3,1},{4,6},{5,7},{6,4},{7,5},{8,10},{9,11},{10,... | collective-permute-start | bytes 122888 | tf_op jit(solution)/shard_map/ppermute | solution.py:151
  6.8 4.0 %collective-permute-start.1 = (f32[2,8,640]{2,1,0:T(8,128)S(1)}, f32[2,8,640]{2,1,0:T(8,128)S(1)}, u32[]{:S(2)}, u32[]{:S(2)}) collective-permute-start(f32[2,8,640]{2,1,0:T(8,128)S(1)} %get-tuple-element.25), channel_id=1, source_target_pairs={{0,4},{1,5},{2,6},{3,7},{4,0},{5,1},{6,2},{7,3},{8,12},{9,13},{10,... | collective-permute-start | bytes 122888 | tf_op jit(solution)/shard_map/ppermute | solution.py:151
  8.3 4.9 %collective-permute-start.2 = (f32[2,8,640]{2,1,0:T(8,128)S(1)}, f32[2,8,640]{2,1,0:T(8,128)S(1)}, u32[]{:S(2)}, u32[]{:S(2)}) collective-permute-start(f32[2,8,640]{2,1,0:T(8,128)S(1)} %get-tuple-element.26), channel_id=1, source_target_pairs={{0,6},{1,7},{2,4},{3,5},{4,2},{5,3},{6,0},{7,1},{8,14},{9,15},{10,... | collective-permute-start | bytes 122888 | tf_op jit(solution)/shard_map/ppermute | solution.py:151
  13.2 1.2 %collective-permute-start.3 = (f32[2,8,640]{2,1,0:T(8,128)S(1)}, f32[2,8,640]{2,1,0:T(8,128)S(1)}, u32[]{:S(2)}, u32[]{:S(2)}) collective-permute-start(f32[2,8,640]{2,1,0:T(8,128)S(1)} %get-tuple-element.28.after_ref.refs_0_), channel_id=1, source_target_pairs={{0,1},{1,0},{2,3},{3,2},{4,5},{5,4},{6,7},{7,6},{8,9},{9,8},{10,11... | collective-permute-start | bytes 122888 | tf_op jit(solution)/shard_map/ppermute | solution.py:151
  13.2 1.4 %collective-permute-start.4 = (f32[2,8,640]{2,1,0:T(8,128)S(1)}, f32[2,8,640]{2,1,0:T(8,128)S(1)}, u32[]{:S(2)}, u32[]{:S(2)}) collective-permute-start(f32[2,8,640]{2,1,0:T(8,128)S(1)} %collective-permute-done.refs_2_), channel_id=1, source_target_pairs={{0,1},{1,0},{2,3},{3,2},{4,5},{5,4},{6,7},{7,6},{8,9},{9,8},{10,11... | collective-permute-start | bytes 122888 | tf_op jit(solution)/shard_map/ppermute | solution.py:151
  13.7 1.2 %collective-permute-start.5 = (f32[2,8,640]{2,1,0:T(8,128)S(1)}, f32[2,8,640]{2,1,0:T(8,128)S(1)}, u32[]{:S(2)}, u32[]{:S(2)}) collective-permute-start(f32[2,8,640]{2,1,0:T(8,128)S(1)} %collective-permute-done.1.refs_4_), channel_id=1, source_target_pairs={{0,1},{1,0},{2,3},{3,2},{4,5},{5,4},{6,7},{7,6},{8,9},{9,8},{10,11... | collective-permute-start | bytes 122888 | tf_op jit(solution)/shard_map/ppermute | solution.py:151
  13.7 1.4 %collective-permute-start.6 = (f32[2,8,640]{2,1,0:T(8,128)S(1)}, f32[2,8,640]{2,1,0:T(8,128)S(1)}, u32[]{:S(2)}, u32[]{:S(2)}) collective-permute-start(f32[2,8,640]{2,1,0:T(8,128)S(1)} %collective-permute-done.2.refs_6_), channel_id=1, source_target_pairs={{0,1},{1,0},{2,3},{3,2},{4,5},{5,4},{6,7},{7,6},{8,9},{9,8},{10,11... | collective-permute-start | bytes 122888 | tf_op jit(solution)/shard_map/ppermute | solution.py:151
  16.5 5.7 %collective-permute-start.7 = (f32[40,128]{1,0:T(8,128)S(1)}, f32[40,128]{1,0:T(8,128)S(1)}, u32[]{:S(2)}, u32[]{:S(2)}) collective-permute-start(f32[40,128]{1,0:T(8,128)S(1)} %get-tuple-element.40.refs_15_), channel_id=1, source_target_pairs={{8,0},{16,8},{24,16},{9,1},{17,9},{25,17},{10,2},{18,10},{26,18},{... | collective-permute-start | bytes 61448 | tf_op jit(solution)/shard_map/ppermute | solution.py:501

commit v2 on v1

--- a/solution.py
+++ b/solution.py
@@ -13,6 +13,7 @@
 LANES = 128
 GROUP = 8
 HALO = 2
+WAIT_AT = (0, 2)
 MIB = 1024 * 1024
 NT = (((1,), (1,)), ((), ()))
 NN = (((1,), (0,)), ((), ()))
@@ -67,7 +68,14 @@
     slot_of_row = lax.broadcasted_iota(jnp.int32, (GROUP, LANES), 0)
     slot_pos = lax.broadcasted_iota(jnp.int32, (GROUP, width), 1)
     low_copy.wait()
-    for start in range(0, slots, GROUP):
+    groups = slots // GROUP
+    for index in range(groups):
+        if index in WAIT_AT:
+            later = [at for at in WAIT_AT if at > index]
+            for at in range(index, later[0] if later else groups):
+                for copy in copies[at]:
+                    copy.wait()
+        start = index * GROUP
         base = wave * pair_local + start
         first = jnp.zeros((GROUP, LANES), jnp.int32)
         for slot in range(GROUP):
@@ -81,8 +89,6 @@
             jnp.concatenate(member, axis=0).astype(jnp.bfloat16),
             jnp.concatenate([m * sign for m in member], axis=0).astype(jnp.bfloat16),
         ]
-        for copy in copies[start // GROUP]:
-            copy.wait()
         highs, lows = [], []
         for level in range(level_count):
             for part in range(2):
@@ -107,7 +113,7 @@
         edge = jnp.zeros((HALO, count), jnp.float32)
         tail = jnp.zeros((ext_pad, count), jnp.float32)
         padded = jnp.concatenate([edge, sums, tail], axis=0)
-        here = slice(start // GROUP * count, (start // GROUP + 1) * count)
+        here = slice(index * count, (index + 1) * count)
         for dest in range(sums_ref.shape[0]):
             sums_ref[dest, :, here] = padded[dest * lat_dev : dest * lat_dev + ext_pad]
     for step, chip_ref in enumerate(chip_refs):
@@ -149,6 +155,17 @@
 def swap(value, by):
     wave_size = lax.axis_size("wave")
     return lax.ppermute(value, "wave", [(i, i ^ by) for i in range(wave_size)])
+
+
+def trade(value, offset):
+    lev_size, wave_size = lax.axis_size("lev"), lax.axis_size("wave")
+    pairs = []
+    for lev in range(lev_size):
+        other = lev + 1 if (lev - offset) % 2 == 0 else lev - 1
+        for wave in range(wave_size):
+            there = (other, wave) if 0 <= other < lev_size else (lev, wave ^ 1)
+            pairs.append((lev * wave_size + wave, there[0] * wave_size + there[1]))
+    return lax.ppermute(value, ("lev", "wave"), pairs)
 
 
 def plan_kernel(
@@ -434,11 +451,13 @@
     horizontal_ref[...] = below
 
 
-def last_kernel(below_ref, above_ref, vertical_ref, out_ref):
-    is_last = lax.axis_index("lev") == lax.axis_size("lev") - 1
+def last_kernel(below_ref, even_ref, odd_ref, vertical_ref, out_ref):
+    lev = lax.axis_index("lev")
+    is_last = lev == lax.axis_size("lev") - 1
     vertical = vertical_ref[...]
     below = below_ref[...]
-    above = jnp.where(is_last, below, above_ref[...])
+    above = jnp.where(lev % 2 == 0, even_ref[...], odd_ref[...])
+    above = jnp.where(is_last, below, above)
     out_ref[...] = (1.0 - vertical) * below + vertical * above
 
 
@@ -448,7 +467,6 @@
     lon_count = 2 * wavenumber_count
     lat_all = legendre.shape[1]
     wave_size = lax.axis_size("wave")
-    lev_size = lax.axis_size("lev")
     lat_dev = lat_all // wave_size
     slots = pl.cdiv(pair_local, GROUP) * GROUP
     extra = slots - pair_local
@@ -472,7 +490,8 @@
         lat_dev,
         2 * wave_size * slots,
     )
-    *received, select = lax.optimization_barrier((*received, select))
+    if len(received) > 1:
+        received[1], select = lax.optimization_barrier((received[1], select))
     pieces = []
     for piece in received:
         pieces += [piece, swap(piece, 1)]
@@ -498,7 +517,8 @@
         ),
         name="first_level",
     )(*operands)
-    above = lax.ppermute(horizontal, "lev", [(i, i - 1) for i in range(1, lev_size)])
+    above_even = trade(horizontal, 0)
+    above_odd = trade(horizontal, 1)
     field_later, departed, top = pl.pallas_call(
         functools.partial(later_kernel, lat_dev, len(pieces)),
         in_specs=[vmem] * (len(operands) + 2),
@@ -518,12 +538,12 @@
     grid_field = jnp.concatenate([field_first, field_later], axis=0)
     final = pl.pallas_call(
         last_kernel,
-        in_specs=[vmem] * 3,
+        in_specs=[vmem] * 4,
         out_specs=vmem,
         out_shape=flat,
         compiler_params=params,
         name="top_level",
-    )(top, above, vertical)
+    )(top, above_even, above_odd, vertical)
     departed = jnp.concatenate([departed, final[None]], axis=0)
     return grid_field, departed.reshape(level_count, 2 * lat_dev, lon_count)
 

time: 23 us -> 21.4 us (0.930)
  waiting for transfers between devices: 6.05 us -> 3.56 us
  starting transfers between devices: 6.85 us -> 8.43 us
  Pallas kernels: 7.94 us -> 7.28 us
    ppermute x1 -> x2, waiting for transfers between devices: 2.33 us -> 0.01 us  [trade(): return lax.ppermute(value, ('lev', 'wave'), pairs)]
    ppermute x1 -> x2, starting transfers between devices: 1.29 us -> 3.21 us  [trade(): return lax.ppermute(value, ('lev', 'wave'), pairs)]
    pallas_call x1, Pallas kernels: 3.15 us -> 2.48 us  [legendre_sums(): pl.pallas_call(functools.partial(legendre_kernel, pair_local, lat_dev), i...]
    ppermute x7, starting transfers between devices: 5.56 us -> 5.22 us  [swap(): return lax.ppermute(value, 'wave', [(i, i ^ by) for i in range(wave_size)])]
  transfers between devices with their start and end apart: 8 -> 9, of which waited for: 7 -> 4; matrix products, arithmetic and copies ran while one was open for 3% -> 3% of each run, Pallas kernels for 15% -> 16%
where the time goes in v2:
time: 21.4 us; the launch traced here: 21.3 us
  starting transfers between devices  8.43 us (39%)
  Pallas kernels  7.28 us (34%)
  waiting for transfers between devices  3.56 us (17%)
  other arithmetic  1.26 us (6%)
  between operations  0.7 us (3%)
    ppermute x7, starting transfers between devices, swap(): return lax.ppermute(value, 'wave', [(i, i ^ by) for i in range(wave_size)])  5.22 us
    ppermute x7, waiting for transfers between devices, swap(): return lax.ppermute(value, 'wave', [(i, i ^ by) for i in range(wave_size)])  3.56 us
    ppermute x2, starting transfers between devices, trade(): return lax.ppermute(value, ('lev', 'wave'), pairs)  3.21 us
    pallas_call x1, Pallas kernels, legendre_sums(): pl.pallas_call(functools.partial(legendre_kernel, pair_local, lat_dev), i...  2.48 us
    pallas_call x1, Pallas kernels, plan(): pl.pallas_call(functools.partial(plan_kernel, pair_local, lat_dev), in_sp...  2.01 us
    pallas_call x1, Pallas kernels, per_device(): pl.pallas_call(functools.partial(later_kernel, lat_dev, len(pieces)), in_...  1.38 us
    pallas_call x1, Pallas kernels, per_device(): pl.pallas_call(functools.partial(first_kernel, lat_dev, len(pieces)), in_...  1.38 us
    concatenate x1, other arithmetic, per_device(): grid_field = jnp.concatenate([field_first, field_later], axis=0)  0.63 us
  transfers between devices with their start and end apart: 9, of which 4 were waited for; matrix products, arithmetic and copies ran while one was open for 3% of the time, Pallas kernels for 16%

profile of v2, /device:TPU:0, one launch (start us, length us, event | category | flops | bytes accessed | tf_op | source)
XLA Modules:
  0.0 21.3 jit_solution(5651414620831757382)
XLA Ops:
  0.6 2.5 %legendre.1 = (f32[2,8,640]{2,1,0:T(8,128)S(1)}, f32[2,8,640]{2,1,0:T(8,128)S(1)}, f32[2,8,640]{2,1,0:T(8,128)S(1)}, f32[2,8,640]{2,1,0:T(8,128)S(1)}) custom-call(s32[320]{0:T(512)} %low_hbm.3, f32[40,2,2,641]{3,2,1,0:T(2,128)} %spec_hbm.1, f32[40,16,641]{2,1,0:T(8,128)} %leg_hbm.1), custom_call_target="tpu_custom_call" | custom-call | tf_op jit(solution)/shard_map/legendre/pallas_call | solution.py:136
  3.1 3.0 %collective-permute-start.1 = (f32[2,8,640]{2,1,0:T(8,128)S(1)}, f32[2,8,640]{2,1,0:T(8,128)S(1)}, u32[]{:S(2)}, u32[]{:S(2)}) collective-permute-start(f32[2,8,640]{2,1,0:T(8,128)S(1)} %get-tuple-element.21), channel_id=1, source_target_pairs={{0,2},{1,3},{2,0},{3,1},{4,6},{5,7},{6,4},{7,5},{8,10},{9,11},{10,... | collective-permute-start | bytes 122888 | tf_op jit(solution)/shard_map/ppermute | solution.py:157
  6.1 1.5 %collective-permute-start.3 = (f32[2,8,640]{2,1,0:T(8,128)S(1)}, f32[2,8,640]{2,1,0:T(8,128)S(1)}, u32[]{:S(2)}, u32[]{:S(2)}) collective-permute-start(f32[2,8,640]{2,1,0:T(8,128)S(1)} %get-tuple-element.24), channel_id=1, source_target_pairs={{0,4},{1,5},{2,6},{3,7},{4,0},{5,1},{6,2},{7,3},{8,12},{9,13},{10,... | collective-permute-start | bytes 122888 | tf_op jit(solution)/shard_map/ppermute | solution.py:157
  7.7 0.0 collective-permute-start.5
  7.7 0.0 collective-permute-start
  7.7 2.0 %plan.1 = (bf16[640,640]{1,0:T(8,128)(2,1)S(1)}, s32[40,128]{1,0:T(8,128)S(1)}, s32[40,128]{1,0:T(8,128)S(1)}, f32[40,128]{1,0:T(8,128)S(1)}, f32[40,128]{1,0:T(...) custom-call(f32[2,8,640]{2,1,0:T(8,128)S(1)} %get-tuple-element.20.after_ref.refs_0_, s32[320]{0:T(512)} %low_hbm.3, ...), custom_call_target="tpu_custom_call" | custom-call | flops 10000000 | bytes 4000000 | tf_op jit(solution)/shard_map/plan/pallas_call | solution.py:263
  9.7 0.0 collective-permute-done.1.refs_2_
  9.7 0.4 %collective-permute-done.3.refs_4_ = f32[2,8,640]{2,1,0:T(8,128)S(1)} collective-permute-done((f32[2,8,640]{2,1,0:T(8,128)S(1)}, f32[2,8,640]{2,1,0:T(8,128)S(1)}, u32[]{:S(2)}, u32[]{:S(2)}) %collective-permute-start.3) | collective-permute-done | bytes 40992 | tf_op jit(solution)/shard_map/ppermute | solution.py:157
  10.1 0.2 collective-permute-start.4
  10.3 2.3 %collective-permute-done.5.refs_6_ = f32[2,8,640]{2,1,0:T(8,128)S(1)} collective-permute-done((f32[2,8,640]{2,1,0:T(8,128)S(1)}, f32[2,8,640]{2,1,0:T(8,128)S(1)}, u32[]{:S(2)}, u32[]{:S(2)}) %collective-permute-start.5) | collective-permute-done | bytes 40992 | tf_op jit(solution)/shard_map/ppermute | solution.py:157
  12.6 0.0 collective-permute-start.6
  12.6 0.5 %collective-permute-start.2 = (f32[2,8,640]{2,1,0:T(8,128)S(1)}, f32[2,8,640]{2,1,0:T(8,128)S(1)}, u32[]{:S(2)}, u32[]{:S(2)}) collective-permute-start(f32[2,8,640]{2,1,0:T(8,128)S(1)} %collective-permute-done.1.refs_2_), channel_id=1, source_target_pairs={{0,1},{1,0},{2,3},{3,2},{4,5},{5,4},{6,7},{7,6},{8,9},{9,8},{10,11... | collective-permute-start | bytes 122888 | tf_op jit(solution)/shard_map/ppermute | solution.py:157
  13.1 0.0 collective-permute-done.refs_1_
  13.1 0.0 collective-permute-done.4.refs_5_
  13.1 0.7 %collective-permute-done.6.refs_7_ = f32[2,8,640]{2,1,0:T(8,128)S(1)} collective-permute-done((f32[2,8,640]{2,1,0:T(8,128)S(1)}, f32[2,8,640]{2,1,0:T(8,128)S(1)}, u32[]{:S(2)}, u32[]{:S(2)}) %collective-permute-start.6) | collective-permute-done | bytes 40992 | tf_op jit(solution)/shard_map/ppermute | solution.py:157
  13.8 0.2 collective-permute-done.2.refs_3_
  13.9 1.4 %first_level.1 = (f32[1,4,1280]{2,1,0:T(4,128)S(1)}, f32[40,128]{1,0:T(8,128)S(1)}) custom-call(f32[2,8,640]{2,1,0:T(8,128)S(1)} %get-tuple-element.20.after_ref.refs_0_, f32[2,8,640]{2,1,0:T(8,128)S(1)} %collective-permute-done.refs_1_, f32[2,8,640]{2,1,0:T(8,128)S(1)} %collective-permute-done.1.refs_2_, f32[2,8,640]{2,1,0:T(8,128)S(1)} %collective-permute-done.2.refs_3_, ...), custom_call_target="tpu_custom_call" | custom-call | flops 100000000 | bytes 4000000 | tf_op jit(solution)/shard_map/first_level/pallas_call | solution.py:508
  15.3 0.4 %collective-permute-start.8 = (f32[40,128]{1,0:T(8,128)S(1)}, f32[40,128]{1,0:T(8,128)S(1)}, u32[]{:S(2)}, u32[]{:S(2)}) collective-permute-start(f32[40,128]{1,0:T(8,128)S(1)} %get-tuple-element.34.refs_15_), channel_id=1, source_target_pairs={{0,1},{1,0},{2,3},{3,2},{4,5},{5,4},{6,7},{7,6},{8,16},{9,17},{10,... | collective-permute-start | bytes 61448 | tf_op jit(solution)/shard_map/ppermute | solution.py:168
  15.7 2.8 %collective-permute-start.7 = (f32[40,128]{1,0:T(8,128)S(1)}, f32[40,128]{1,0:T(8,128)S(1)}, u32[]{:S(2)}, u32[]{:S(2)}) collective-permute-start(f32[40,128]{1,0:T(8,128)S(1)} %get-tuple-element.34.refs_15_), channel_id=1, source_target_pairs={{0,8},{1,9},{2,10},{3,11},{4,12},{5,13},{6,14},{7,15},{8,0},{9,1},... | collective-permute-start | bytes 61448 | tf_op jit(solution)/shard_map/ppermute | solution.py:168
  18.5 1.4 %later_levels.1 = (f32[1,4,1280]{2,1,0:T(4,128)S(1)}, f32[1,40,128]{2,1,0:T(8,128)S(1)}, f32[40,128]{1,0:T(8,128)S(1)}) custom-call(f32[2,8,640]{2,1,0:T(8,128)S(1)} %get-tuple-element.20.after_ref.refs_0_, f32[2,8,640]{2,1,0:T(8,128)S(1)} %collective-permute-done.refs_1_, f32[2,8,640]{2,1,0:T(8,128)S(1)} %collective-permute-done.1.refs_2_, ...), custom_call_target="tpu_custom_call" | custom-call | flops 100000000 | bytes 4000000 | tf_op jit(solution)/shard_map/later_levels/pallas_call | solution.py:522
  19.9 0.6 %pad_maximum_fusion = f32[2,4,1280]{2,1,0:T(4,128)} fusion(f32[1,4,1280]{2,1,0:T(4,128)S(1)} %get-tuple-element.35, f32[1,4,1280]{2,1,0:T(4,128)S(1)} %get-tuple-element.32), kind=kLoop, calls=%fused_computation | loop fusion | flops 10240 | bytes 81920 | tf_op jit(solution)/shard_map/concatenate | solution.py:538
  20.6 0.0 collective-permute-done.8.odd_ref
  20.6 0.0 collective-permute-done.7.even_ref
  20.6 0.6 %pad_maximum_fusion.1 = f32[2,4,1280]{2,1,0:T(4,128)} fusion(f32[1,4,1280]{2,1,0:T(4,128)S(1)} %concatenate.13, f32[1,4,1280]{2,1,0:T(4,128)S(1)} %concatenate.12), kind=kLoop, calls=%fused_computation.1 | loop fusion | flops 10240 | bytes 81920 | tf_op jit(solution)/shard_map/concatenate | solution.py:547
  (3 shorter events, 0.1 us)
Async XLA Ops:
  3.1 6.6 %collective-permute-start.1 = (f32[2,8,640]{2,1,0:T(8,128)S(1)}, f32[2,8,640]{2,1,0:T(8,128)S(1)}, u32[]{:S(2)}, u32[]{:S(2)}) collective-permute-start(f32[2,8,640]{2,1,0:T(8,128)S(1)} %get-tuple-element.21), channel_id=1, source_target_pairs={{0,2},{1,3},{2,0},{3,1},{4,6},{5,7},{6,4},{7,5},{8,10},{9,11},{10,... | collective-permute-start | bytes 122888 | tf_op jit(solution)/shard_map/ppermute | solution.py:157
  6.1 4.0 %collective-permute-start.3 = (f32[2,8,640]{2,1,0:T(8,128)S(1)}, f32[2,8,640]{2,1,0:T(8,128)S(1)}, u32[]{:S(2)}, u32[]{:S(2)}) collective-permute-start(f32[2,8,640]{2,1,0:T(8,128)S(1)} %get-tuple-element.24), channel_id=1, source_target_pairs={{0,4},{1,5},{2,6},{3,7},{4,0},{5,1},{6,2},{7,3},{8,12},{9,13},{10,... | collective-permute-start | bytes 122888 | tf_op jit(solution)/shard_map/ppermute | solution.py:157
  7.7 4.9 %collective-permute-start.5 = (f32[2,8,640]{2,1,0:T(8,128)S(1)}, f32[2,8,640]{2,1,0:T(8,128)S(1)}, u32[]{:S(2)}, u32[]{:S(2)}) collective-permute-start(f32[2,8,640]{2,1,0:T(8,128)S(1)} %get-tuple-element.25), channel_id=1, source_target_pairs={{0,6},{1,7},{2,4},{3,5},{4,2},{5,3},{6,0},{7,1},{8,14},{9,15},{10,... | collective-permute-start | bytes 122888 | tf_op jit(solution)/shard_map/ppermute | solution.py:157
  7.7 5.4 %collective-permute-start = (f32[2,8,640]{2,1,0:T(8,128)S(1)}, f32[2,8,640]{2,1,0:T(8,128)S(1)}, u32[]{:S(2)}, u32[]{:S(2)}) collective-permute-start(f32[2,8,640]{2,1,0:T(8,128)S(1)} %get-tuple-element.20.after_ref.refs_0_), channel_id=1, source_target_pairs={{0,1},{1,0},{2,3},{3,2},{4,5},{5,4},{6,7},{7,6},{8,9},{9,8},{10,11... | collective-permute-start | bytes 122888 | tf_op jit(solution)/shard_map/ppermute | solution.py:157
  10.1 2.9 %collective-permute-start.4 = (f32[2,8,640]{2,1,0:T(8,128)S(1)}, f32[2,8,640]{2,1,0:T(8,128)S(1)}, u32[]{:S(2)}, u32[]{:S(2)}) collective-permute-start(f32[2,8,640]{2,1,0:T(8,128)S(1)} %collective-permute-done.3.refs_4_), channel_id=1, source_target_pairs={{0,1},{1,0},{2,3},{3,2},{4,5},{5,4},{6,7},{7,6},{8,9},{9,8},{10,11... | collective-permute-start | bytes 122888 | tf_op jit(solution)/shard_map/ppermute | solution.py:157
  12.6 1.2 %collective-permute-start.6 = (f32[2,8,640]{2,1,0:T(8,128)S(1)}, f32[2,8,640]{2,1,0:T(8,128)S(1)}, u32[]{:S(2)}, u32[]{:S(2)}) collective-permute-start(f32[2,8,640]{2,1,0:T(8,128)S(1)} %collective-permute-done.5.refs_6_), channel_id=1, source_target_pairs={{0,1},{1,0},{2,3},{3,2},{4,5},{5,4},{6,7},{7,6},{8,9},{9,8},{10,11... | collective-permute-start | bytes 122888 | tf_op jit(solution)/shard_map/ppermute | solution.py:157
  12.6 1.4 %collective-permute-start.2 = (f32[2,8,640]{2,1,0:T(8,128)S(1)}, f32[2,8,640]{2,1,0:T(8,128)S(1)}, u32[]{:S(2)}, u32[]{:S(2)}) collective-permute-start(f32[2,8,640]{2,1,0:T(8,128)S(1)} %collective-permute-done.1.refs_2_), channel_id=1, source_target_pairs={{0,1},{1,0},{2,3},{3,2},{4,5},{5,4},{6,7},{7,6},{8,9},{9,8},{10,11... | collective-permute-start | bytes 122888 | tf_op jit(solution)/shard_map/ppermute | solution.py:157
  15.3 5.3 %collective-permute-start.8 = (f32[40,128]{1,0:T(8,128)S(1)}, f32[40,128]{1,0:T(8,128)S(1)}, u32[]{:S(2)}, u32[]{:S(2)}) collective-permute-start(f32[40,128]{1,0:T(8,128)S(1)} %get-tuple-element.34.refs_15_), channel_id=1, source_target_pairs={{0,1},{1,0},{2,3},{3,2},{4,5},{5,4},{6,7},{7,6},{8,16},{9,17},{10,... | collective-permute-start | bytes 61448 | tf_op jit(solution)/shard_map/ppermute | solution.py:168
  15.7 4.8 %collective-permute-start.7 = (f32[40,128]{1,0:T(8,128)S(1)}, f32[40,128]{1,0:T(8,128)S(1)}, u32[]{:S(2)}, u32[]{:S(2)}) collective-permute-start(f32[40,128]{1,0:T(8,128)S(1)} %get-tuple-element.34.refs_15_), channel_id=1, source_target_pairs={{0,8},{1,9},{2,10},{3,11},{4,12},{5,13},{6,14},{7,15},{8,0},{9,1},... | collective-permute-start | bytes 61448 | tf_op jit(solution)/shard_map/ppermute | solution.py:168

commit v3 on v2

--- a/solution.py
+++ b/solution.py
@@ -15,6 +15,8 @@
 HALO = 2
 WAIT_AT = (0, 2)
 MIB = 1024 * 1024
+FAR = -(2**20)
+ORDER = (0, 2, 1, 3)
 NT = (((1,), (1,)), ((), ()))
 NN = (((1,), (0,)), ((), ()))
 
@@ -36,22 +38,52 @@
     return jnp.concatenate(parts, axis=1)
 
 
-def legendre_kernel(
-    pair_local,
-    lat_dev,
-    low_hbm,
-    spec_hbm,
-    leg_hbm,
-    *refs,
-):
-    chip_refs = refs[:-7]
-    low_ref, spec_ref, leg_ref, sums_ref, low_sem, spec_sem, leg_sem = refs[-7:]
+def wave_rows(low_ref, wave, pair_local, waves_ref):
+    row = lax.broadcasted_iota(jnp.int32, (GROUP, LANES), 0)
+    groups = pl.cdiv(pair_local, GROUP)
+    for index in range(waves_ref.shape[0] // GROUP):
+        source, group = divmod(index, groups)
+        base = (wave ^ source) * pair_local + group * GROUP
+        value = jnp.full((GROUP, LANES), FAR, jnp.int32)
+        for slot in range(min(GROUP, pair_local - group * GROUP)):
+            value = jnp.where(row == slot, low_ref[base + slot], value)
+        waves_ref[index * GROUP : (index + 1) * GROUP] = value
+
+
+def departure(wave, lat_dev, half, lat_ref, col_ref, lon, tilt, out_refs):
+    row_step_ref, place_ref, lon_frac_ref, lat_frac_ref, vertical_ref = out_refs
+    points = lon.shape[0]
+    blocks = points // (2 * lat_dev)
+    row = lax.broadcasted_iota(jnp.int32, lon.shape, 0)
+    point = lax.broadcasted_iota(jnp.int32, lon.shape, 1)
+    row_step = jnp.zeros(lon.shape, jnp.int32)
+    col_step = jnp.zeros(lon.shape, jnp.int32)
+    for index in range(points):
+        own = wave * lat_dev + index // blocks % lat_dev - HALO
+        row_step = jnp.where(row == index, lat_ref[index] - own, row_step)
+        first = LANES * (index % blocks)
+        col_step = jnp.where(row == index, col_ref[index] - first, col_step)
+    col_step = jnp.where(col_step >= half, col_step - 2 * half, col_step)
+    col_step = jnp.where(col_step < -half, col_step + 2 * half, col_step)
+    quarters = 4 * col_step + lon - 12
+    row_step_ref[...] = row_step
+    place_ref[...] = point + (quarters >> 2)
+    lon_frac_ref[...] = (quarters & 3).astype(jnp.float32) * 0.25
+    lat_frac_ref[...] = (tilt & 3).astype(jnp.float32) * 0.25
+    vertical_ref[...] = (tilt >> 2).astype(jnp.float32) * 0.25
+
+
+def legendre_kernel(pair_local, lat_dev, *refs):
+    low_hbm, spec_hbm, leg_hbm, table_hbm = refs[:4]
+    *chip_refs, table_ref = refs[4:-7]
+    low_ref, spec_ref, leg_ref, sums_ref, small_sem, spec_sem, leg_sem = refs[-7:]
     slots, lat_all, slot_count = leg_ref.shape
     level_count = spec_ref.shape[1]
     pair_total = low_ref.shape[0]
     ext_pad = sums_ref.shape[1]
     width = pl.cdiv(slot_count, LANES) * LANES
-    low_copy = pltpu.make_async_copy(low_hbm, low_ref, low_sem)
+    low_copy = pltpu.make_async_copy(low_hbm, low_ref, small_sem.at[0])
+    table_copy = pltpu.make_async_copy(table_hbm, table_ref, small_sem.at[1])
     low_copy.start()
     copies = []
     for start in range(0, slots, GROUP):
@@ -64,6 +96,7 @@
         for copy in pair:
             copy.start()
         copies.append(pair)
+    table_copy.start()
     wave = lax.axis_index("wave")
     slot_of_row = lax.broadcasted_iota(jnp.int32, (GROUP, LANES), 0)
     slot_pos = lax.broadcasted_iota(jnp.int32, (GROUP, width), 1)
@@ -120,36 +153,37 @@
         dest = (wave // 2 ^ step) * 2
         for core in range(2):
             chip_ref[core] = sums_ref[dest + core]
-
-
-def legendre_sums(pair_low, spectral, legendre, pair_local, wave_size):
+    table_copy.wait()
+
+
+def legendre_sums(operands, pair_local, wave_size):
+    pair_low, spectral, legendre, tables = operands
     slots, level_count = spectral.shape[:2]
-    lat_all, slot_count = legendre.shape[1:]
+    lat_all = legendre.shape[1]
     lat_dev = lat_all // wave_size
     lanes = 8 * level_count * slots
     ext_pad = pl.cdiv(lat_dev + 2 * HALO, 8) * 8
     chips = wave_size // 2
     out = jax.ShapeDtypeStruct((2, ext_pad, lanes), jnp.float32)
-    operands = [
-        pltpu.with_memory_space_constraint(x, pltpu.HBM) for x in (pair_low, spectral, legendre)
-    ]
-    return pl.pallas_call(
+    outs = [out] * chips + [jax.ShapeDtypeStruct(tables.shape, tables.dtype)]
+    results = pl.pallas_call(
         functools.partial(legendre_kernel, pair_local, lat_dev),
-        in_specs=[pl.BlockSpec(memory_space=pltpu.HBM)] * 3,
-        out_specs=[pl.BlockSpec(memory_space=pltpu.VMEM)] * chips,
-        out_shape=[out] * chips,
+        in_specs=[pl.BlockSpec(memory_space=pltpu.HBM)] * len(operands),
+        out_specs=[pl.BlockSpec(memory_space=pltpu.VMEM)] * len(outs),
+        out_shape=outs,
         scratch_shapes=[
             pltpu.SMEM(pair_low.shape, jnp.int32),
             pltpu.VMEM(spectral.shape, jnp.float32),
             pltpu.VMEM(legendre.shape, jnp.float32),
             pltpu.VMEM((wave_size, ext_pad, lanes), jnp.float32),
-            pltpu.SemaphoreType.DMA,
+            pltpu.SemaphoreType.DMA((2,)),
             pltpu.SemaphoreType.DMA((slots // GROUP,)),
             pltpu.SemaphoreType.DMA((slots // GROUP,)),
         ],
         compiler_params=pltpu.CompilerParams(vmem_limit_bytes=24 * MIB),
         name="legendre",
-    )(*operands)
+    )(*[pltpu.with_memory_space_constraint(x, pltpu.HBM) for x in operands])
+    return results[:chips], results[chips]
 
 
 def swap(value, by):
@@ -168,118 +202,61 @@
     return lax.ppermute(value, ("lev", "wave"), pairs)
 
 
-def plan_kernel(
-    pair_local,
-    lat_dev,
-    after_ref,
-    low_hbm,
-    lat_hbm,
-    col_hbm,
-    lon_hbm,
-    tilt_hbm,
-    table_hbm,
-    select_ref,
-    row_step_ref,
-    place_ref,
-    lon_frac_ref,
-    lat_frac_ref,
-    vertical_ref,
-    table_ref,
-    low_ref,
-    lat_ref,
-    col_ref,
-    lon_ref,
-    tilt_ref,
-    sems,
-):
-    pairs = [
-        (low_hbm, low_ref),
-        (lat_hbm, lat_ref),
-        (col_hbm, col_ref),
-        (lon_hbm, lon_ref),
-        (tilt_hbm, tilt_ref),
-        (table_hbm, table_ref),
-    ]
+def plan_kernel(pair_local, lat_dev, after_ref, *refs):
+    sources = refs[:5]
+    select_ref, *plan_refs = refs[5:-7]
+    low_ref, lat_ref, col_ref, lon_ref, tilt_ref, waves_ref, sems = refs[-7:]
     copies = [
-        pltpu.make_async_copy(there, here, sems.at[i]) for i, (there, here) in enumerate(pairs)
+        pltpu.make_async_copy(there, here, sems.at[i])
+        for i, (there, here) in enumerate(zip(sources, refs[-7:-2], strict=True))
     ]
     for copy in copies:
         copy.start()
-    for copy in copies[:-1]:
+    half = select_ref.shape[1]
+    quarter = half // 4
+    lane = lax.broadcasted_iota(jnp.int32, (2 * GROUP, half), 1)
+    kind = sum((lane >= quarter * i).astype(jnp.int32) for i in range(1, 4))
+    order = 4 * (lane - quarter * kind)
+    for i, first in enumerate(ORDER):
+        order = jnp.where(kind == i, order + first, order)
+    wave = lax.axis_index("wave")
+    for copy in copies:
         copy.wait()
-    wave = lax.axis_index("wave")
-    half, slot_lanes = select_ref.shape
-    lon_count = 2 * half
-    points = lon_ref.shape[0]
-    blocks = points // (2 * lat_dev)
-    sources = low_ref.shape[0] // pair_local
-    per_source = slot_lanes // (sources * 2 * GROUP)
-    lane = lax.broadcasted_iota(jnp.int32, (GROUP, LANES), 1)
-    order = lax.broadcasted_iota(jnp.int32, (half, LANES), 0)
-    order = jnp.where(order < half // 2, 2 * order, 2 * order - half + 1)
-    per_vector = LANES // (2 * GROUP)
-    for block in range(slot_lanes // LANES):
-        waves = jnp.full((GROUP, LANES), -2 * half, jnp.int32)
-        for index in range(per_vector):
-            source, group = divmod(block * per_vector + index, per_source)
-            base = (wave ^ source) * pair_local + group * GROUP
-            for slot in range(min(GROUP, pair_local - group * GROUP)):
-                here = (lane & ~GROUP) == index * 2 * GROUP + slot
-                waves = jnp.where(here, low_ref[base + slot], waves)
-        waves = jnp.where((lane & GROUP) != 0, half - 1 - waves, waves)
-        match = jnp.broadcast_to(waves[0:1], order.shape) == order
-        select_ref[:, block * LANES : (block + 1) * LANES] = jnp.where(match, 1.0, 0.0).astype(
-            jnp.bfloat16
-        )
-    row = lax.broadcasted_iota(jnp.int32, (points, LANES), 0)
-    point = lax.broadcasted_iota(jnp.int32, (points, LANES), 1)
-    row_step = jnp.zeros((points, LANES), jnp.int32)
-    col_step = jnp.zeros((points, LANES), jnp.int32)
-    for index in range(points):
-        own = wave * lat_dev + index // blocks % lat_dev - HALO
-        row_step = jnp.where(row == index, lat_ref[index] - own, row_step)
-        first = LANES * (index % blocks)
-        col_step = jnp.where(row == index, col_ref[index] - first, col_step)
-    col_step = jnp.where(col_step >= half, col_step - lon_count, col_step)
-    col_step = jnp.where(col_step < -half, col_step + lon_count, col_step)
-    quarters = 4 * col_step + lon_ref[...] - 12
-    row_step_ref[...] = row_step
-    place_ref[...] = point + (quarters >> 2)
-    lon_frac_ref[...] = (quarters & 3).astype(jnp.float32) * 0.25
-    lat_frac_ref[...] = (tilt_ref[...] & 3).astype(jnp.float32) * 0.25
-    vertical_ref[...] = (tilt_ref[...] >> 2).astype(jnp.float32) * 0.25
-    copies[-1].wait()
-
-
-def plan(after, tables, pair_low, dep_lat, dep_col, lon_steps, tilt_steps, pair_local, lat_dev, lanes):
-    vmem = pl.BlockSpec(memory_space=pltpu.VMEM)
-    whole = jax.ShapeDtypeStruct(lon_steps.shape, jnp.int32)
+    departure(wave, lat_dev, half, lat_ref, col_ref, lon_ref[...], tilt_ref[...], plan_refs)
+    wave_rows(low_ref, wave, pair_local, waves_ref)
+    for start in range(0, waves_ref.shape[0], GROUP):
+        waves = waves_ref[start : start + GROUP]
+        waves = jnp.concatenate([waves, half - 1 - waves], axis=0)
+        waves = jnp.concatenate([waves] * (half // LANES), axis=1)
+        match = jnp.where(waves == order, 1.0, 0.0).astype(jnp.bfloat16)
+        select_ref[2 * start : 2 * (start + GROUP)] = match
+
+
+def plan(after, pair_low, dep_lat, dep_col, lon_steps, tilt_steps, pair_local, lat_dev, slots, half):
+    operands = (pair_low, dep_lat, dep_col, lon_steps, tilt_steps)
+    integer = jax.ShapeDtypeStruct(lon_steps.shape, jnp.int32)
     fraction = jax.ShapeDtypeStruct(lon_steps.shape, jnp.float32)
-    half = tables.shape[1]
-    operands = [
-        pltpu.with_memory_space_constraint(x, pltpu.HBM)
-        for x in (pair_low, dep_lat, dep_col, lon_steps, tilt_steps, tables)
+    outs = [
+        jax.ShapeDtypeStruct((2 * slots, half), jnp.bfloat16),
+        integer,
+        integer,
+        fraction,
+        fraction,
+        fraction,
     ]
     return pl.pallas_call(
         functools.partial(plan_kernel, pair_local, lat_dev),
         in_specs=[pl.BlockSpec(memory_space=pl.ANY)]
         + [pl.BlockSpec(memory_space=pltpu.HBM)] * len(operands),
-        out_specs=[vmem] * 7,
-        out_shape=[
-            jax.ShapeDtypeStruct((half, lanes), jnp.bfloat16),
-            whole,
-            whole,
-            fraction,
-            fraction,
-            fraction,
-            jax.ShapeDtypeStruct(tables.shape, tables.dtype),
-        ],
+        out_specs=[pl.BlockSpec(memory_space=pltpu.VMEM)] * len(outs),
+        out_shape=outs,
         scratch_shapes=[
             pltpu.SMEM(pair_low.shape, jnp.int32),
             pltpu.SMEM(dep_lat.shape, jnp.int32),
             pltpu.SMEM(dep_col.shape, jnp.int32),
             pltpu.VMEM(lon_steps.shape, jnp.int32),
             pltpu.VMEM(tilt_steps.shape, jnp.int32),
+            pltpu.VMEM((slots, LANES), jnp.int32),
             pltpu.SemaphoreType.DMA((len(operands),)),
         ],
         compiler_params=pltpu.CompilerParams(vmem_limit_bytes=24 * MIB),
@@ -287,16 +264,18 @@
             flops=10**7, bytes_accessed=4 * 10**6, transcendentals=0
         ),
         name="plan",
-    )(after, *operands)
+    )(after, *[pltpu.with_memory_space_constraint(x, pltpu.HBM) for x in operands])
 
 
 def fourier_tables(wavenumber_count):
     lon_count = 2 * wavenumber_count
-    half_lon = lon_count // 2
+    quarter = lon_count // 4
+    whole = quarter // LANES * LANES
     tables = []
     for parity in range(2):
-        wave = np.arange(parity, wavenumber_count, 2)
-        phase = wave[:, None] * np.arange(half_lon)[None, :] % lon_count
+        kinds = ORDER[2 * parity : 2 * parity + 2]
+        wave = np.concatenate([np.arange(kind, wavenumber_count, 4) for kind in kinds])
+        phase = wave[:, None] * np.arange(quarter)[None, :] % lon_count
         angle = phase * (2.0 * math.pi / lon_count)
         weight = np.where(wave == 0, 1.0, 2.0)[:, None]
         parts = [weight * np.cos(angle), -weight * np.sin(angle)]
@@ -304,7 +283,31 @@
     exact = np.stack(tables)
     high = exact.astype(ml_dtypes.bfloat16)
     low = (exact - high.astype(np.float64)).astype(ml_dtypes.bfloat16)
-    return np.concatenate([high, low], axis=2)
+    return np.concatenate(
+        [high[..., :whole], low[..., :whole], high[..., whole:], low[..., whole:]], axis=2
+    )
+
+
+def add_halves(product, start, count):
+    high = product[start : start + count]
+    low = product[start + count : start + 2 * count]
+    whole = (product.shape[1] - LANES) // 2
+    tail = high[:, 2 * whole :]
+    tail = tail + (low[:, 2 * whole :] + pltpu.roll(tail, LANES // 2, 1))
+    pieces = [
+        high[:, at : at + LANES] + (low[:, at : at + LANES] + high[:, whole + at : whole + at + LANES])
+        for at in range(0, whole, LANES)
+    ]
+    return pieces + [tail]
+
+
+def join(first, second):
+    lane = lax.broadcasted_iota(jnp.int32, first[0].shape, 1)
+    rolled = [pltpu.roll(piece, LANES // 2, 1) for piece in second]
+    before = [first[-1], *rolled[:-1]]
+    return first[:-1] + [
+        jnp.where(lane < LANES // 2, a, b) for a, b in zip(before, rolled, strict=True)
+    ]
 
 
 def regroup(pieces, level, lane):
@@ -353,43 +356,59 @@
     ordered = lax.dot_general(
         jnp.concatenate([high[:count], low[:count], high[count:], low[count:]], axis=0),
         select_ref[...],
-        NT,
+        NN,
         preferred_element_type=jnp.float32,
     )
+    half = ordered.shape[1]
     real = ordered[: 2 * count]
     imag = pltpu.roll(ordered[2 * count :], half // 2, 1)
-    first_half = lax.broadcasted_iota(jnp.int32, real.shape, 1) < half // 2
-    even = jnp.where(first_half, real, imag).astype(jnp.bfloat16)
-    odd = jnp.where(first_half, imag, real).astype(jnp.bfloat16)
-    sums = []
-    for parity, operand in enumerate((even, odd)):
-        main = lax.dot_general(
-            operand, table_ref[parity], NN, preferred_element_type=jnp.float32
+    lane = lax.broadcasted_iota(jnp.int32, real.shape, 1)
+    first_half = lane < half // 2
+    outer = (lane < half // 4) | (lane >= half // 4 * 3)
+    even = jnp.where(first_half, real, imag)
+    odd = jnp.where(first_half, imag, real)
+    turned = pltpu.roll(odd, half // 2, 1)
+    even_turned = jnp.where(first_half == outer, even, -even)
+    odd_turned = jnp.where(outer, turned, -turned)
+    products = [
+        lax.dot_general(
+            jnp.concatenate(rows, axis=0).astype(jnp.bfloat16),
+            table_ref[parity],
+            NN,
+            preferred_element_type=jnp.float32,
         )
-        sums.append(main[:count, :half] + (main[count:, :half] + main[:count, half:]))
-    return sums
-
-
-def interpolate(sums, field_ref, level, lat_dev, row_step, step, f, g, near_ref):
-    half = sums[0].shape[1]
-    count = sums[0].shape[0]
-    ext_pad = count // 2
-    blocks = 2 * half // LANES
-    for block in range(blocks // 2):
-        here = slice(block * LANES, (block + 1) * LANES)
-        for at, rows in (
-            (block, sums[0][:, here] + sums[1][:, here]),
-            (block + blocks // 2, sums[0][:, here] - sums[1][:, here]),
-        ):
-            there = slice(at * LANES, (at + 1) * LANES)
-            for hemi in range(2):
-                start = hemi * ext_pad + HALO
-                field_ref[level, hemi * lat_dev : (hemi + 1) * lat_dev, there] = rows[
-                    start : start + lat_dev
-                ]
-            for side in range(3):
-                place = (at + 1 - side) % blocks
-                near_ref[side, pl.ds(place, count, stride=blocks), :] = rows
+        for parity, rows in enumerate(((even, even_turned), (odd, odd_turned)))
+    ]
+    near, far = [
+        [add_halves(product, start, count) for product in products] for start in (0, 2 * count)
+    ]
+    first = join(
+        [a + b for a, b in zip(*near, strict=True)], [a + b for a, b in zip(*far, strict=True)]
+    )
+    later = join(
+        [a - b for a, b in zip(*near, strict=True)], [a - b for a, b in zip(*far, strict=True)]
+    )
+    return first + later
+
+
+def store_rows(rows, field_ref, level, lat_dev, near_ref):
+    blocks = len(rows)
+    count = rows[0].shape[0]
+    for at, value in enumerate(rows):
+        there = slice(at * LANES, (at + 1) * LANES)
+        for hemi in range(2):
+            start = hemi * (count // 2) + HALO
+            field_ref[level, hemi * lat_dev : (hemi + 1) * lat_dev, there] = value[
+                start : start + lat_dev
+            ]
+        for side in range(3):
+            place = (at + 1 - side) % blocks
+            near_ref[side, pl.ds(place, count, stride=blocks), :] = value
+
+
+def interpolate(lat_dev, row_step, step, f, g, near_ref):
+    blocks = row_step.shape[0] // (2 * lat_dev)
+    ext_pad = near_ref.shape[1] // (2 * blocks)
     points = 2 * lat_dev * blocks
     point = lax.broadcasted_iota(jnp.int32, (points, LANES), 1)
 
@@ -431,24 +450,35 @@
     piece_refs, plan_refs = refs[:piece_count], refs[piece_count + 2 : -3]
     select_ref, table_ref = refs[piece_count : piece_count + 2]
     field_ref, horizontal_ref, near_ref = refs[-3:]
-    sums = level_rows(0, piece_refs, select_ref, table_ref)
-    plans = [ref[...] for ref in plan_refs]
-    horizontal_ref[...] = interpolate(sums, field_ref, 0, lat_dev, *plans, near_ref)
+    rows = level_rows(0, piece_refs, select_ref, table_ref)
+    store_rows(rows, field_ref, 0, lat_dev, near_ref)
+    horizontal_ref[...] = interpolate(lat_dev, *[ref[...] for ref in plan_refs], near_ref)
 
 
 def later_kernel(lat_dev, piece_count, *refs):
-    piece_refs, plan_refs = refs[:piece_count], refs[piece_count + 2 : -6]
+    piece_refs, plan_refs = refs[:piece_count], refs[piece_count + 2 : -9]
     select_ref, table_ref = refs[piece_count : piece_count + 2]
-    vertical_ref, below_ref, field_ref, departed_ref, horizontal_ref, near_ref = refs[-6:]
+    vertical_ref, below_ref, first_ref = refs[-9:-6]
+    field_hbm, departed_ref, horizontal_ref, field_ref, near_ref, sems = refs[-6:]
+    copies = [pltpu.make_async_copy(first_ref, field_hbm.at[pl.ds(0, 1)], sems.at[0])]
+    copies[0].start()
     vertical = vertical_ref[...]
     below = below_ref[...]
     plans = [ref[...] for ref in plan_refs]
     for level in range(1, departed_ref.shape[0] + 1):
-        sums = level_rows(level, piece_refs, select_ref, table_ref)
-        horizontal = interpolate(sums, field_ref, level - 1, lat_dev, *plans, near_ref)
+        rows = level_rows(level, piece_refs, select_ref, table_ref)
+        store_rows(rows, field_ref, level - 1, lat_dev, near_ref)
+        copy = pltpu.make_async_copy(
+            field_ref.at[pl.ds(level - 1, 1)], field_hbm.at[pl.ds(level, 1)], sems.at[level]
+        )
+        copy.start()
+        copies.append(copy)
+        horizontal = interpolate(lat_dev, *plans, near_ref)
         departed_ref[level - 1] = (1.0 - vertical) * below + vertical * horizontal
         below = horizontal
     horizontal_ref[...] = below
+    for copy in copies:
+        copy.wait()
 
 
 def last_kernel(below_ref, even_ref, odd_ref, vertical_ref, out_ref):
@@ -473,14 +503,13 @@
     if extra:
         spectral = jnp.pad(spectral, ((0, extra), (0, 0), (0, 0), (0, 0)))
         legendre = jnp.pad(legendre, ((0, extra), (0, 0), (0, 0)))
-    parts = legendre_sums(pair_low, spectral, legendre, pair_local, wave_size)
+    tables = jnp.asarray(fourier_tables(wavenumber_count))
+    parts, tables = legendre_sums(
+        (pair_low, spectral, legendre, tables), pair_local, wave_size
+    )
     received = [swap(part, 2 * step) if step else part for step, part in enumerate(parts)]
-    blocks = lon_count // LANES
-    points = 2 * lat_dev * blocks
-    ext_pad = parts[0].shape[1]
-    select, *plans, vertical, tables = plan(
+    select, *plans, vertical = plan(
         parts[0],
-        jnp.asarray(fourier_tables(wavenumber_count)),
         pair_low,
         dep_lat,
         dep_col,
@@ -488,10 +517,13 @@
         tilt_steps,
         pair_local,
         lat_dev,
-        2 * wave_size * slots,
-    )
-    if len(received) > 1:
-        received[1], select = lax.optimization_barrier((received[1], select))
+        wave_size * slots,
+        wavenumber_count,
+    )
+    *received[:2], select = lax.optimization_barrier((*received[:2], select))
+    blocks = lon_count // LANES
+    points = 2 * lat_dev * blocks
+    ext_pad = parts[0].shape[1]
     pieces = []
     for piece in received:
         pieces += [piece, swap(piece, 1)]
@@ -519,23 +551,27 @@
     )(*operands)
     above_even = trade(horizontal, 0)
     above_odd = trade(horizontal, 1)
-    field_later, departed, top = pl.pallas_call(
+    levels = jax.ShapeDtypeStruct((level_count, 2 * lat_dev, lon_count), jnp.float32)
+    grid_field, departed, top = pl.pallas_call(
         functools.partial(later_kernel, lat_dev, len(pieces)),
-        in_specs=[vmem] * (len(operands) + 2),
-        out_specs=[vmem] * 3,
+        in_specs=[vmem] * (len(operands) + 3),
+        out_specs=[pl.BlockSpec(memory_space=pltpu.HBM), vmem, vmem],
         out_shape=[
-            jax.ShapeDtypeStruct((level_count - 1, 2 * lat_dev, lon_count), jnp.float32),
+            levels,
             jax.ShapeDtypeStruct((level_count - 1, points, LANES), jnp.float32),
             flat,
         ],
-        scratch_shapes=[near],
+        scratch_shapes=[
+            pltpu.VMEM((level_count - 1, 2 * lat_dev, lon_count), jnp.float32),
+            near,
+            pltpu.SemaphoreType.DMA((level_count,)),
+        ],
         compiler_params=params,
         cost_estimate=pl.CostEstimate(
             flops=10**8, bytes_accessed=4 * 10**6, transcendentals=0
         ),
         name="later_levels",
-    )(*operands, vertical, horizontal)
-    grid_field = jnp.concatenate([field_first, field_later], axis=0)
+    )(*operands, vertical, horizontal, field_first)
     final = pl.pallas_call(
         last_kernel,
         in_specs=[vmem] * 4,

time: 21.4 us -> 21 us (0.981)
  waiting for transfers between devices: 3.56 us -> 4.65 us
  Pallas kernels: 7.28 us -> 6.45 us
  other arithmetic: 1.26 us -> 0.63 us
    ppermute x7, waiting for transfers between devices: 3.56 us -> 4.58 us  [swap(): return lax.ppermute(value, 'wave', [(i, i ^ by) for i in range(wave_size)])]
    pallas_call x1, Pallas kernels: 2.01 us -> 1.07 us  [plan(): pl.pallas_call(functools.partial(plan_kernel, pair_local, lat_dev), in_sp...]
    concatenate x1 -> x0, other arithmetic: 0.63 us -> none  [per_device(): grid_field = jnp.concatenate([field_first, field_later], axis=0)]
    pallas_call x1, Pallas kernels: 1.38 us -> 1.66 us  [per_device(): pl.pallas_call(functools.partial(later_kernel, lat_dev, len(pieces)), in_...]
  transfers between devices with their start and end apart: 9 -> 9, of which waited for: 4 -> 5; matrix products, arithmetic and copies ran while one was open for 3% -> 0% of each run, Pallas kernels for 16% -> 13%
where the time goes in v3:
time: 21 us; the launch traced here: 20.8 us
  starting transfers between devices  8.35 us (40%)
  Pallas kernels  6.45 us (31%)
  waiting for transfers between devices  4.65 us (22%)
  between operations  0.7 us (3%)
  other arithmetic  0.63 us (3%)
    ppermute x7, starting transfers between devices, swap(): return lax.ppermute(value, 'wave', [(i, i ^ by) for i in range(wave_size)])  5.13 us
    ppermute x7, waiting for transfers between devices, swap(): return lax.ppermute(value, 'wave', [(i, i ^ by) for i in range(wave_size)])  4.58 us
    ppermute x2, starting transfers between devices, trade(): return lax.ppermute(value, ('lev', 'wave'), pairs)  3.22 us
    pallas_call x1, Pallas kernels, legendre_sums(): pl.pallas_call(functools.partial(legendre_kernel, pair_local, lat_dev), i...  2.5 us
    pallas_call x1, Pallas kernels, per_device(): pl.pallas_call(functools.partial(later_kernel, lat_dev, len(pieces)), in_...  1.66 us
    pallas_call x1, Pallas kernels, per_device(): pl.pallas_call(functools.partial(first_kernel, lat_dev, len(pieces)), in_...  1.21 us
    pallas_call x1, Pallas kernels, plan(): pl.pallas_call(functools.partial(plan_kernel, pair_local, lat_dev), in_sp...  1.07 us
    concatenate x1, other arithmetic, per_device(): departed = jnp.concatenate([departed, final[None]], axis=0)  0.63 us
  transfers between devices with their start and end apart: 9, of which 5 were waited for; matrix products, arithmetic and copies ran while one was open for 0% of the time, Pallas kernels for 13%

profile of v3, /device:TPU:0, one launch (start us, length us, event | category | flops | bytes accessed | tf_op | source)
XLA Modules:
  0.0 20.8 jit_solution(3827476371179332152)
XLA Ops:
  0.6 2.5 %legendre.1 = (f32[2,8,640]{2,1,0:T(8,128)S(1)}, f32[2,8,640]{2,1,0:T(8,128)S(1)}, f32[2,8,640]{2,1,0:T(8,128)S(1)}, f32[2,8,640]{2,1,0:T(8,128)S(1)}, bf16[2,640,640]{2,1,0:T(8,128)(2,1)S(1)}) custom-call(s32[320]{0:T(512)} %refs_0_.3, f32[40,2,2,641]{3,2,1,0:T(2,128)} %refs_1_.2, f32[40,16,641]{2,1,0:T(8,128)} %refs_2_.2, ...), custom_call_target="tpu_custom_call" | custom-call | tf_op jit(solution)/shard_map/legendre/pallas_call | solution.py:169
  3.1 3.0 %collective-permute-start = (f32[2,8,640]{2,1,0:T(8,128)S(1)}, f32[2,8,640]{2,1,0:T(8,128)S(1)}, u32[]{:S(2)}, u32[]{:S(2)}) collective-permute-start(f32[2,8,640]{2,1,0:T(8,128)S(1)} %get-tuple-element.22), channel_id=1, source_target_pairs={{0,2},{1,3},{2,0},{3,1},{4,6},{5,7},{6,4},{7,5},{8,10},{9,11},{10,... | collective-permute-start | bytes 122888 | tf_op jit(solution)/shard_map/ppermute | solution.py:191
  6.1 1.5 %collective-permute-start.3 = (f32[2,8,640]{2,1,0:T(8,128)S(1)}, f32[2,8,640]{2,1,0:T(8,128)S(1)}, u32[]{:S(2)}, u32[]{:S(2)}) collective-permute-start(f32[2,8,640]{2,1,0:T(8,128)S(1)} %get-tuple-element.26), channel_id=1, source_target_pairs={{0,4},{1,5},{2,6},{3,7},{4,0},{5,1},{6,2},{7,3},{8,12},{9,13},{10,... | collective-permute-start | bytes 122888 | tf_op jit(solution)/shard_map/ppermute | solution.py:191
  7.7 0.0 collective-permute-start.5
  7.7 1.1 %plan.1 = (bf16[640,640]{1,0:T(8,128)(2,1)S(1)}, s32[40,128]{1,0:T(8,128)S(1)}, s32[40,128]{1,0:T(8,128)S(1)}, f32[40,128]{1,0:T(8,128)S(1)}, f32[40,128]{1,0:T(8,128)S(1)}, /*index=5*/f32[40,128]{1,0:T(8,128)S(1)}) custom-call(f32[2,8,640]{2,1,0:T(8,128)S(1)} %get-tuple-element.24.after_ref.refs_0_, s32[320]{0:T(512)} %refs_0_.3, s32[40]{0:T(128)} %refs_1_.3, ...), custom_call_target="tpu_custom_call" | custom-call | flops 10000000 | bytes 4000000 | tf_op jit(solution)/shard_map/plan/pallas_call | solution.py:247
  8.8 0.0 collective-permute-done.refs_2_
  8.8 0.1 collective-permute-start.1
  8.8 1.3 %collective-permute-done.3.refs_4_ = f32[2,8,640]{2,1,0:T(8,128)S(1)} collective-permute-done((f32[2,8,640]{2,1,0:T(8,128)S(1)}, f32[2,8,640]{2,1,0:T(8,128)S(1)}, u32[]{:S(2)}, u32[]{:S(2)}) %collective-permute-start.3) | collective-permute-done | bytes 40992 | tf_op jit(solution)/shard_map/ppermute | solution.py:191
  10.1 0.0 collective-permute-start.4
  10.1 2.4 %collective-permute-done.5.refs_6_ = f32[2,8,640]{2,1,0:T(8,128)S(1)} collective-permute-done((f32[2,8,640]{2,1,0:T(8,128)S(1)}, f32[2,8,640]{2,1,0:T(8,128)S(1)}, u32[]{:S(2)}, u32[]{:S(2)}) %collective-permute-start.5) | collective-permute-done | bytes 40992 | tf_op jit(solution)/shard_map/ppermute | solution.py:191
  12.6 0.0 collective-permute-start.6
  12.6 0.5 %collective-permute-start.2 = (f32[2,8,640]{2,1,0:T(8,128)S(1)}, f32[2,8,640]{2,1,0:T(8,128)S(1)}, u32[]{:S(2)}, u32[]{:S(2)}) collective-permute-start(f32[2,8,640]{2,1,0:T(8,128)S(1)} %collective-permute-done.refs_2_), channel_id=1, source_target_pairs={{0,1},{1,0},{2,3},{3,2},{4,5},{5,4},{6,7},{7,6},{8,9},{9,8},{10,11... | collective-permute-start | bytes 122888 | tf_op jit(solution)/shard_map/ppermute | solution.py:191
  13.1 0.0 collective-permute-done.4.refs_5_
  13.1 0.7 %collective-permute-done.6.refs_7_ = f32[2,8,640]{2,1,0:T(8,128)S(1)} collective-permute-done((f32[2,8,640]{2,1,0:T(8,128)S(1)}, f32[2,8,640]{2,1,0:T(8,128)S(1)}, u32[]{:S(2)}, u32[]{:S(2)}) %collective-permute-start.6) | collective-permute-done | bytes 40992 | tf_op jit(solution)/shard_map/ppermute | solution.py:191
  13.8 0.0 collective-permute-done.1.refs_1_
  13.8 0.2 collective-permute-done.2.refs_3_
  13.9 1.2 %first_level.1 = (f32[1,4,1280]{2,1,0:T(4,128)S(1)}, f32[40,128]{1,0:T(8,128)S(1)}) custom-call(f32[2,8,640]{2,1,0:T(8,128)S(1)} %get-tuple-element.24.after_ref.refs_0_, f32[2,8,640]{2,1,0:T(8,128)S(1)} %collective-permute-done.1.refs_1_, f32[2,8,640]{2,1,0:T(8,128)S(1)} %collective-permute-done.refs_2_, f32[2,8,640]{2,1,0:T(8,128)S(1)} %collective-permute-done.2.refs_3_, ...), custom_call_target="tpu_custom_call" | custom-call | flops 100000000 | bytes 4000000 | tf_op jit(solution)/shard_map/first_level/pallas_call | solution.py:540
  15.2 0.4 %collective-permute-start.8 = (f32[40,128]{1,0:T(8,128)S(1)}, f32[40,128]{1,0:T(8,128)S(1)}, u32[]{:S(2)}, u32[]{:S(2)}) collective-permute-start(f32[40,128]{1,0:T(8,128)S(1)} %get-tuple-element.35.refs_15_), channel_id=1, source_target_pairs={{0,1},{1,0},{2,3},{3,2},{4,5},{5,4},{6,7},{7,6},{8,16},{9,17},{10,... | collective-permute-start | bytes 61448 | tf_op jit(solution)/shard_map/ppermute | solution.py:202
  15.6 2.8 %collective-permute-start.7 = (f32[40,128]{1,0:T(8,128)S(1)}, f32[40,128]{1,0:T(8,128)S(1)}, u32[]{:S(2)}, u32[]{:S(2)}) collective-permute-start(f32[40,128]{1,0:T(8,128)S(1)} %get-tuple-element.35.refs_15_), channel_id=1, source_target_pairs={{0,8},{1,9},{2,10},{3,11},{4,12},{5,13},{6,14},{7,15},{8,0},{9,1},... | collective-permute-start | bytes 61448 | tf_op jit(solution)/shard_map/ppermute | solution.py:202
  18.4 1.7 %later_levels.1 = (f32[2,4,1280]{2,1,0:T(4,128)}, f32[1,40,128]{2,1,0:T(8,128)S(1)}, f32[40,128]{1,0:T(8,128)S(1)}) custom-call(f32[2,8,640]{2,1,0:T(8,128)S(1)} %get-tuple-element.24.after_ref.refs_0_, f32[2,8,640]{2,1,0:T(8,128)S(1)} %collective-permute-done.1.refs_1_, f32[2,8,640]{2,1,0:T(8,128)S(1)} %collective-permute-done.refs_2_, ...), custom_call_target="tpu_custom_call" | custom-call | flops 100000000 | bytes 4000000 | tf_op jit(solution)/shard_map/later_levels/pallas_call | solution.py:555
  20.1 0.0 collective-permute-done.8.odd_ref
  20.1 0.1 collective-permute-done.7.even_ref
  20.2 0.6 %pad_maximum_fusion = f32[2,4,1280]{2,1,0:T(4,128)} fusion(f32[1,4,1280]{2,1,0:T(4,128)S(1)} %concatenate.9, f32[1,4,1280]{2,1,0:T(4,128)S(1)} %concatenate.8), kind=kLoop, calls=%fused_computation | loop fusion | flops 10240 | bytes 81920 | tf_op jit(solution)/shard_map/concatenate | solution.py:583
  (3 shorter events, 0.0 us)
Async XLA Ops:
  3.1 5.6 %collective-permute-start = (f32[2,8,640]{2,1,0:T(8,128)S(1)}, f32[2,8,640]{2,1,0:T(8,128)S(1)}, u32[]{:S(2)}, u32[]{:S(2)}) collective-permute-start(f32[2,8,640]{2,1,0:T(8,128)S(1)} %get-tuple-element.22), channel_id=1, source_target_pairs={{0,2},{1,3},{2,0},{3,1},{4,6},{5,7},{6,4},{7,5},{8,10},{9,11},{10,... | collective-permute-start | bytes 122888 | tf_op jit(solution)/shard_map/ppermute | solution.py:191
  6.1 4.0 %collective-permute-start.3 = (f32[2,8,640]{2,1,0:T(8,128)S(1)}, f32[2,8,640]{2,1,0:T(8,128)S(1)}, u32[]{:S(2)}, u32[]{:S(2)}) collective-permute-start(f32[2,8,640]{2,1,0:T(8,128)S(1)} %get-tuple-element.26), channel_id=1, source_target_pairs={{0,4},{1,5},{2,6},{3,7},{4,0},{5,1},{6,2},{7,3},{8,12},{9,13},{10,... | collective-permute-start | bytes 122888 | tf_op jit(solution)/shard_map/ppermute | solution.py:191
  7.7 4.9 %collective-permute-start.5 = (f32[2,8,640]{2,1,0:T(8,128)S(1)}, f32[2,8,640]{2,1,0:T(8,128)S(1)}, u32[]{:S(2)}, u32[]{:S(2)}) collective-permute-start(f32[2,8,640]{2,1,0:T(8,128)S(1)} %get-tuple-element.27), channel_id=1, source_target_pairs={{0,6},{1,7},{2,4},{3,5},{4,2},{5,3},{6,0},{7,1},{8,14},{9,15},{10,... | collective-permute-start | bytes 122888 | tf_op jit(solution)/shard_map/ppermute | solution.py:191
  8.8 5.0 %collective-permute-start.1 = (f32[2,8,640]{2,1,0:T(8,128)S(1)}, f32[2,8,640]{2,1,0:T(8,128)S(1)}, u32[]{:S(2)}, u32[]{:S(2)}) collective-permute-start(f32[2,8,640]{2,1,0:T(8,128)S(1)} %get-tuple-element.24.after_ref.refs_0_), channel_id=1, source_target_pairs={{0,1},{1,0},{2,3},{3,2},{4,5},{5,4},{6,7},{7,6},{8,9},{9,8},{10,11... | collective-permute-start | bytes 122888 | tf_op jit(solution)/shard_map/ppermute | solution.py:191
  10.1 2.9 %collective-permute-start.4 = (f32[2,8,640]{2,1,0:T(8,128)S(1)}, f32[2,8,640]{2,1,0:T(8,128)S(1)}, u32[]{:S(2)}, u32[]{:S(2)}) collective-permute-start(f32[2,8,640]{2,1,0:T(8,128)S(1)} %collective-permute-done.3.refs_4_), channel_id=1, source_target_pairs={{0,1},{1,0},{2,3},{3,2},{4,5},{5,4},{6,7},{7,6},{8,9},{9,8},{10,11... | collective-permute-start | bytes 122888 | tf_op jit(solution)/shard_map/ppermute | solution.py:191
  12.6 1.2 %collective-permute-start.6 = (f32[2,8,640]{2,1,0:T(8,128)S(1)}, f32[2,8,640]{2,1,0:T(8,128)S(1)}, u32[]{:S(2)}, u32[]{:S(2)}) collective-permute-start(f32[2,8,640]{2,1,0:T(8,128)S(1)} %collective-permute-done.5.refs_6_), channel_id=1, source_target_pairs={{0,1},{1,0},{2,3},{3,2},{4,5},{5,4},{6,7},{7,6},{8,9},{9,8},{10,11... | collective-permute-start | bytes 122888 | tf_op jit(solution)/shard_map/ppermute | solution.py:191
  12.6 1.4 %collective-permute-start.2 = (f32[2,8,640]{2,1,0:T(8,128)S(1)}, f32[2,8,640]{2,1,0:T(8,128)S(1)}, u32[]{:S(2)}, u32[]{:S(2)}) collective-permute-start(f32[2,8,640]{2,1,0:T(8,128)S(1)} %collective-permute-done.refs_2_), channel_id=1, source_target_pairs={{0,1},{1,0},{2,3},{3,2},{4,5},{5,4},{6,7},{7,6},{8,9},{9,8},{10,11... | collective-permute-start | bytes 122888 | tf_op jit(solution)/shard_map/ppermute | solution.py:191
  15.2 4.9 %collective-permute-start.8 = (f32[40,128]{1,0:T(8,128)S(1)}, f32[40,128]{1,0:T(8,128)S(1)}, u32[]{:S(2)}, u32[]{:S(2)}) collective-permute-start(f32[40,128]{1,0:T(8,128)S(1)} %get-tuple-element.35.refs_15_), channel_id=1, source_target_pairs={{0,1},{1,0},{2,3},{3,2},{4,5},{5,4},{6,7},{7,6},{8,16},{9,17},{10,... | collective-permute-start | bytes 61448 | tf_op jit(solution)/shard_map/ppermute | solution.py:202
  15.6 4.6 %collective-permute-start.7 = (f32[40,128]{1,0:T(8,128)S(1)}, f32[40,128]{1,0:T(8,128)S(1)}, u32[]{:S(2)}, u32[]{:S(2)}) collective-permute-start(f32[40,128]{1,0:T(8,128)S(1)} %get-tuple-element.35.refs_15_), channel_id=1, source_target_pairs={{0,8},{1,9},{2,10},{3,11},{4,12},{5,13},{6,14},{7,15},{8,0},{9,1},... | collective-permute-start | bytes 61448 | tf_op jit(solution)/shard_map/ppermute | solution.py:202

commit v4 on v3

--- a/solution.py
+++ b/solution.py
@@ -186,6 +186,10 @@
     return results[:chips], results[chips]
 
 
+def chip_order(count):
+    return [0, *range(count - 1, 0, -1)]
+
+
 def swap(value, by):
     wave_size = lax.axis_size("wave")
     return lax.ppermute(value, "wave", [(i, i ^ by) for i in range(wave_size)])
@@ -340,7 +344,8 @@
     half = table_ref.shape[2] // 2
     core = lax.axis_index("wave") % 2
     vectors = []
-    for ref in piece_refs:
+    order = chip_order(len(piece_refs) // 2)
+    for ref in [piece_refs[2 * order.index(i // 2) + i % 2] for i in range(len(piece_refs))]:
         source = ref[core]
         vectors += [
             source[:, start : start + LANES] for start in range(0, source.shape[1], LANES)
@@ -481,7 +486,7 @@
         copy.wait()
 
 
-def last_kernel(below_ref, even_ref, odd_ref, vertical_ref, out_ref):
+def last_kernel(below_ref, odd_ref, even_ref, vertical_ref, out_ref):
     lev = lax.axis_index("lev")
     is_last = lev == lax.axis_size("lev") - 1
     vertical = vertical_ref[...]
@@ -520,13 +525,13 @@
         wave_size * slots,
         wavenumber_count,
     )
-    *received[:2], select = lax.optimization_barrier((*received[:2], select))
+    received[-1], select = lax.optimization_barrier((received[-1], select))
     blocks = lon_count // LANES
     points = 2 * lat_dev * blocks
     ext_pad = parts[0].shape[1]
     pieces = []
-    for piece in received:
-        pieces += [piece, swap(piece, 1)]
+    for step in chip_order(len(received)):
+        pieces += [received[step], swap(received[step], 1)]
     vmem = pl.BlockSpec(memory_space=pltpu.VMEM)
     params = pltpu.CompilerParams(vmem_limit_bytes=24 * MIB)
     operands = (
@@ -579,7 +584,7 @@
         out_shape=flat,
         compiler_params=params,
         name="top_level",
-    )(top, above_even, above_odd, vertical)
+    )(top, above_odd, above_even, vertical)
     departed = jnp.concatenate([departed, final[None]], axis=0)
     return grid_field, departed.reshape(level_count, 2 * lat_dev, lon_count)
 

time: 21 us -> 19 us (0.905)
  starting transfers between devices: 8.35 us -> 6.83 us
  waiting for transfers between devices: 4.65 us -> 4.09 us
    ppermute x2, starting transfers between devices: 3.22 us -> 1.71 us  [trade(): return lax.ppermute(value, ('lev', 'wave'), pairs)]
    ppermute x7, waiting for transfers between devices: 4.58 us -> 3.65 us  [swap(): return lax.ppermute(value, 'wave', [(i, i ^ by) for i in range(wave_size)])]
    ppermute x2, waiting for transfers between devices: 0.06 us -> 0.45 us  [trade(): return lax.ppermute(value, ('lev', 'wave'), pairs)]
  transfers between devices with their start and end apart: 9 -> 9, of which waited for: 5 -> 7; matrix products, arithmetic and copies ran while one was open for 0% -> 0% of each run, Pallas kernels for 13% -> 15%
where the time goes in v4:
time: 19 us; the launch traced here: 18.7 us
  starting transfers between devices  6.83 us (36%)
  Pallas kernels  6.46 us (34%)
  waiting for transfers between devices  4.09 us (22%)
  between operations  0.69 us (4%)
  other arithmetic  0.63 us (3%)
    ppermute x7, starting transfers between devices, swap(): return lax.ppermute(value, 'wave', [(i, i ^ by) for i in range(wave_size)])  5.12 us
    ppermute x7, waiting for transfers between devices, swap(): return lax.ppermute(value, 'wave', [(i, i ^ by) for i in range(wave_size)])  3.65 us
    pallas_call x1, Pallas kernels, legendre_sums(): pl.pallas_call(functools.partial(legendre_kernel, pair_local, lat_dev), i...  2.5 us
    ppermute x2, starting transfers between devices, trade(): return lax.ppermute(value, ('lev', 'wave'), pairs)  1.71 us
    pallas_call x1, Pallas kernels, per_device(): pl.pallas_call(functools.partial(later_kernel, lat_dev, len(pieces)), in_...  1.66 us
    pallas_call x1, Pallas kernels, per_device(): pl.pallas_call(functools.partial(first_kernel, lat_dev, len(pieces)), in_...  1.2 us
    pallas_call x1, Pallas kernels, plan(): pl.pallas_call(functools.partial(plan_kernel, pair_local, lat_dev), in_sp...  1.07 us
    concatenate x1, other arithmetic, per_device(): departed = jnp.concatenate([departed, final[None]], axis=0)  0.63 us
  transfers between devices with their start and end apart: 9, of which 7 were waited for; matrix products, arithmetic and copies ran while one was open for 0% of the time, Pallas kernels for 15%

profile of v4, /device:TPU:0, one launch (start us, length us, event | category | flops | bytes accessed | tf_op | source)
XLA Modules:
  0.0 18.7 jit_solution(1279549391050864662)
XLA Ops:
  0.6 2.5 %legendre.1 = (f32[2,8,640]{2,1,0:T(8,128)S(1)}, f32[2,8,640]{2,1,0:T(8,128)S(1)}, f32[2,8,640]{2,1,0:T(8,128)S(1)}, f32[2,8,640]{2,1,0:T(8,128)S(1)}, bf16[2,640,640]{2,1,0:T(8,128)(2,1)S(1)}) custom-call(s32[320]{0:T(512)} %refs_0_.3, f32[40,2,2,641]{3,2,1,0:T(2,128)} %refs_1_.2, f32[40,16,641]{2,1,0:T(8,128)} %refs_2_.2, ...), custom_call_target="tpu_custom_call" | custom-call | tf_op jit(solution)/shard_map/legendre/pallas_call | solution.py:169
  3.1 4.0 %collective-permute-start.1 = (f32[2,8,640]{2,1,0:T(8,128)S(1)}, f32[2,8,640]{2,1,0:T(8,128)S(1)}, u32[]{:S(2)}, u32[]{:S(2)}) collective-permute-start(f32[2,8,640]{2,1,0:T(8,128)S(1)} %get-tuple-element.21), channel_id=1, source_target_pairs={{0,6},{1,7},{2,4},{3,5},{4,2},{5,3},{6,0},{7,1},{8,14},{9,15},{10,... | collective-permute-start | bytes 122888 | tf_op jit(solution)/shard_map/ppermute | solution.py:195
  7.1 0.5 %collective-permute-start.3 = (f32[2,8,640]{2,1,0:T(8,128)S(1)}, f32[2,8,640]{2,1,0:T(8,128)S(1)}, u32[]{:S(2)}, u32[]{:S(2)}) collective-permute-start(f32[2,8,640]{2,1,0:T(8,128)S(1)} %get-tuple-element.24), channel_id=1, source_target_pairs={{0,4},{1,5},{2,6},{3,7},{4,0},{5,1},{6,2},{7,3},{8,12},{9,13},{10,... | collective-permute-start | bytes 122888 | tf_op jit(solution)/shard_map/ppermute | solution.py:195
  7.6 0.1 collective-permute-start.5
  7.7 0.0 collective-permute-start
  7.7 1.1 %plan.1 = (bf16[640,640]{1,0:T(8,128)(2,1)S(1)}, s32[40,128]{1,0:T(8,128)S(1)}, s32[40,128]{1,0:T(8,128)S(1)}, f32[40,128]{1,0:T(8,128)S(1)}, f32[40,128]{1,0:T(8,128)S(1)}, /*index=5*/f32[40,128]{1,0:T(8,128)S(1)}) custom-call(f32[2,8,640]{2,1,0:T(8,128)S(1)} %get-tuple-element.20.after_ref.refs_0_, s32[320]{0:T(512)} %refs_0_.3, s32[40]{0:T(128)} %refs_1_.3, ...), custom_call_target="tpu_custom_call" | custom-call | flops 10000000 | bytes 4000000 | tf_op jit(solution)/shard_map/plan/pallas_call | solution.py:251
  8.8 0.3 %collective-permute-done.1.refs_2_ = f32[2,8,640]{2,1,0:T(8,128)S(1)} collective-permute-done((f32[2,8,640]{2,1,0:T(8,128)S(1)}, f32[2,8,640]{2,1,0:T(8,128)S(1)}, u32[]{:S(2)}, u32[]{:S(2)}) %collective-permute-start.1) | collective-permute-done | bytes 40992 | tf_op jit(solution)/shard_map/ppermute | solution.py:195
  9.1 2.0 %collective-permute-done.3.refs_4_ = f32[2,8,640]{2,1,0:T(8,128)S(1)} collective-permute-done((f32[2,8,640]{2,1,0:T(8,128)S(1)}, f32[2,8,640]{2,1,0:T(8,128)S(1)}, u32[]{:S(2)}, u32[]{:S(2)}) %collective-permute-start.3) | collective-permute-done | bytes 40992 | tf_op jit(solution)/shard_map/ppermute | solution.py:195
  11.1 0.0 collective-permute-start.4
  11.1 0.5 %collective-permute-done.5.refs_6_ = f32[2,8,640]{2,1,0:T(8,128)S(1)} collective-permute-done((f32[2,8,640]{2,1,0:T(8,128)S(1)}, f32[2,8,640]{2,1,0:T(8,128)S(1)}, u32[]{:S(2)}, u32[]{:S(2)}) %collective-permute-start.5) | collective-permute-done | bytes 40992 | tf_op jit(solution)/shard_map/ppermute | solution.py:195
  11.6 0.0 collective-permute-start.6
  11.6 0.5 %collective-permute-start.2 = (f32[2,8,640]{2,1,0:T(8,128)S(1)}, f32[2,8,640]{2,1,0:T(8,128)S(1)}, u32[]{:S(2)}, u32[]{:S(2)}) collective-permute-start(f32[2,8,640]{2,1,0:T(8,128)S(1)} %collective-permute-done.1.refs_2_), channel_id=1, source_target_pairs={{0,1},{1,0},{2,3},{3,2},{4,5},{5,4},{6,7},{7,6},{8,9},{9,8},{10,11... | collective-permute-start | bytes 122888 | tf_op jit(solution)/shard_map/ppermute | solution.py:195
  12.1 0.0 collective-permute-done.refs_1_
  12.1 0.2 %collective-permute-done.4.refs_5_ = f32[2,8,640]{2,1,0:T(8,128)S(1)} collective-permute-done((f32[2,8,640]{2,1,0:T(8,128)S(1)}, f32[2,8,640]{2,1,0:T(8,128)S(1)}, u32[]{:S(2)}, u32[]{:S(2)}) %collective-permute-start.4) | collective-permute-done | bytes 40992 | tf_op jit(solution)/shard_map/ppermute | solution.py:195
  12.3 0.5 %collective-permute-done.6.refs_7_ = f32[2,8,640]{2,1,0:T(8,128)S(1)} collective-permute-done((f32[2,8,640]{2,1,0:T(8,128)S(1)}, f32[2,8,640]{2,1,0:T(8,128)S(1)}, u32[]{:S(2)}, u32[]{:S(2)}) %collective-permute-start.6) | collective-permute-done | bytes 40992 | tf_op jit(solution)/shard_map/ppermute | solution.py:195
  12.8 0.2 collective-permute-done.2.refs_3_
  13.0 1.2 %first_level.1 = (f32[1,4,1280]{2,1,0:T(4,128)S(1)}, f32[40,128]{1,0:T(8,128)S(1)}) custom-call(f32[2,8,640]{2,1,0:T(8,128)S(1)} %get-tuple-element.20.after_ref.refs_0_, f32[2,8,640]{2,1,0:T(8,128)S(1)} %collective-permute-done.refs_1_, f32[2,8,640]{2,1,0:T(8,128)S(1)} %collective-permute-done.1.refs_2_, f32[2,8,640]{2,1,0:T(8,128)S(1)} %collective-permute-done.2.refs_3_, ...), custom_call_target="tpu_custom_call" | custom-call | flops 100000000 | bytes 4000000 | tf_op jit(solution)/shard_map/first_level/pallas_call | solution.py:545
  14.2 1.6 %collective-permute-start.8 = (f32[40,128]{1,0:T(8,128)S(1)}, f32[40,128]{1,0:T(8,128)S(1)}, u32[]{:S(2)}, u32[]{:S(2)}) collective-permute-start(f32[40,128]{1,0:T(8,128)S(1)} %get-tuple-element.33.refs_15_), channel_id=1, source_target_pairs={{0,8},{1,9},{2,10},{3,11},{4,12},{5,13},{6,14},{7,15},{8,0},{9,1},... | collective-permute-start | bytes 61448 | tf_op jit(solution)/shard_map/ppermute | solution.py:206
  15.8 0.1 collective-permute-start.7
  15.9 1.7 %later_levels.1 = (f32[2,4,1280]{2,1,0:T(4,128)}, f32[1,40,128]{2,1,0:T(8,128)S(1)}, f32[40,128]{1,0:T(8,128)S(1)}) custom-call(f32[2,8,640]{2,1,0:T(8,128)S(1)} %get-tuple-element.20.after_ref.refs_0_, f32[2,8,640]{2,1,0:T(8,128)S(1)} %collective-permute-done.refs_1_, f32[2,8,640]{2,1,0:T(8,128)S(1)} %collective-permute-done.1.refs_2_, ...), custom_call_target="tpu_custom_call" | custom-call | flops 100000000 | bytes 4000000 | tf_op jit(solution)/shard_map/later_levels/pallas_call | solution.py:560
  17.6 0.4 %collective-permute-done.8.even_ref = f32[40,128]{1,0:T(8,128)S(1)} collective-permute-done((f32[40,128]{1,0:T(8,128)S(1)}, f32[40,128]{1,0:T(8,128)S(1)}, u32[]{:S(2)}, u32[]{:S(2)}) %collective-permute-start.8) | collective-permute-done | bytes 20512 | tf_op jit(solution)/shard_map/ppermute | solution.py:206
  18.0 0.0 collective-permute-done.7.odd_ref
  18.1 0.6 %pad_maximum_fusion = f32[2,4,1280]{2,1,0:T(4,128)} fusion(f32[1,4,1280]{2,1,0:T(4,128)S(1)} %concatenate.9, f32[1,4,1280]{2,1,0:T(4,128)S(1)} %concatenate.8), kind=kLoop, calls=%fused_computation | loop fusion | flops 10240 | bytes 81920 | tf_op jit(solution)/shard_map/concatenate | solution.py:588
  (3 shorter events, 0.0 us)
Async XLA Ops:
  3.1 5.9 %collective-permute-start.1 = (f32[2,8,640]{2,1,0:T(8,128)S(1)}, f32[2,8,640]{2,1,0:T(8,128)S(1)}, u32[]{:S(2)}, u32[]{:S(2)}) collective-permute-start(f32[2,8,640]{2,1,0:T(8,128)S(1)} %get-tuple-element.21), channel_id=1, source_target_pairs={{0,6},{1,7},{2,4},{3,5},{4,2},{5,3},{6,0},{7,1},{8,14},{9,15},{10,... | collective-permute-start | bytes 122888 | tf_op jit(solution)/shard_map/ppermute | solution.py:195
  7.1 4.0 %collective-permute-start.3 = (f32[2,8,640]{2,1,0:T(8,128)S(1)}, f32[2,8,640]{2,1,0:T(8,128)S(1)}, u32[]{:S(2)}, u32[]{:S(2)}) collective-permute-start(f32[2,8,640]{2,1,0:T(8,128)S(1)} %get-tuple-element.24), channel_id=1, source_target_pairs={{0,4},{1,5},{2,6},{3,7},{4,0},{5,1},{6,2},{7,3},{8,12},{9,13},{10,... | collective-permute-start | bytes 122888 | tf_op jit(solution)/shard_map/ppermute | solution.py:195
  7.6 4.0 %collective-permute-start.5 = (f32[2,8,640]{2,1,0:T(8,128)S(1)}, f32[2,8,640]{2,1,0:T(8,128)S(1)}, u32[]{:S(2)}, u32[]{:S(2)}) collective-permute-start(f32[2,8,640]{2,1,0:T(8,128)S(1)} %get-tuple-element.25), channel_id=1, source_target_pairs={{0,2},{1,3},{2,0},{3,1},{4,6},{5,7},{6,4},{7,5},{8,10},{9,11},{10,... | collective-permute-start | bytes 122888 | tf_op jit(solution)/shard_map/ppermute | solution.py:195
  7.7 4.4 %collective-permute-start = (f32[2,8,640]{2,1,0:T(8,128)S(1)}, f32[2,8,640]{2,1,0:T(8,128)S(1)}, u32[]{:S(2)}, u32[]{:S(2)}) collective-permute-start(f32[2,8,640]{2,1,0:T(8,128)S(1)} %get-tuple-element.20.after_ref.refs_0_), channel_id=1, source_target_pairs={{0,1},{1,0},{2,3},{3,2},{4,5},{5,4},{6,7},{7,6},{8,9},{9,8},{10,11... | collective-permute-start | bytes 122888 | tf_op jit(solution)/shard_map/ppermute | solution.py:195
  11.1 1.2 %collective-permute-start.4 = (f32[2,8,640]{2,1,0:T(8,128)S(1)}, f32[2,8,640]{2,1,0:T(8,128)S(1)}, u32[]{:S(2)}, u32[]{:S(2)}) collective-permute-start(f32[2,8,640]{2,1,0:T(8,128)S(1)} %collective-permute-done.3.refs_4_), channel_id=1, source_target_pairs={{0,1},{1,0},{2,3},{3,2},{4,5},{5,4},{6,7},{7,6},{8,9},{9,8},{10,11... | collective-permute-start | bytes 122888 | tf_op jit(solution)/shard_map/ppermute | solution.py:195
  11.6 1.2 %collective-permute-start.6 = (f32[2,8,640]{2,1,0:T(8,128)S(1)}, f32[2,8,640]{2,1,0:T(8,128)S(1)}, u32[]{:S(2)}, u32[]{:S(2)}) collective-permute-start(f32[2,8,640]{2,1,0:T(8,128)S(1)} %collective-permute-done.5.refs_6_), channel_id=1, source_target_pairs={{0,1},{1,0},{2,3},{3,2},{4,5},{5,4},{6,7},{7,6},{8,9},{9,8},{10,11... | collective-permute-start | bytes 122888 | tf_op jit(solution)/shard_map/ppermute | solution.py:195
  11.6 1.4 %collective-permute-start.2 = (f32[2,8,640]{2,1,0:T(8,128)S(1)}, f32[2,8,640]{2,1,0:T(8,128)S(1)}, u32[]{:S(2)}, u32[]{:S(2)}) collective-permute-start(f32[2,8,640]{2,1,0:T(8,128)S(1)} %collective-permute-done.1.refs_2_), channel_id=1, source_target_pairs={{0,1},{1,0},{2,3},{3,2},{4,5},{5,4},{6,7},{7,6},{8,9},{9,8},{10,11... | collective-permute-start | bytes 122888 | tf_op jit(solution)/shard_map/ppermute | solution.py:195
  14.2 3.8 %collective-permute-start.8 = (f32[40,128]{1,0:T(8,128)S(1)}, f32[40,128]{1,0:T(8,128)S(1)}, u32[]{:S(2)}, u32[]{:S(2)}) collective-permute-start(f32[40,128]{1,0:T(8,128)S(1)} %get-tuple-element.33.refs_15_), channel_id=1, source_target_pairs={{0,8},{1,9},{2,10},{3,11},{4,12},{5,13},{6,14},{7,15},{8,0},{9,1},... | collective-permute-start | bytes 61448 | tf_op jit(solution)/shard_map/ppermute | solution.py:206
  15.8 2.2 %collective-permute-start.7 = (f32[40,128]{1,0:T(8,128)S(1)}, f32[40,128]{1,0:T(8,128)S(1)}, u32[]{:S(2)}, u32[]{:S(2)}) collective-permute-start(f32[40,128]{1,0:T(8,128)S(1)} %get-tuple-element.33.refs_15_), channel_id=1, source_target_pairs={{0,1},{1,0},{2,3},{3,2},{4,5},{5,4},{6,7},{7,6},{8,16},{9,17},{10,... | collective-permute-start | bytes 61448 | tf_op jit(solution)/shard_map/ppermute | solution.py:206

commit v5 on v4

--- a/solution.py
+++ b/solution.py
@@ -13,9 +13,9 @@
 LANES = 128
 GROUP = 8
 HALO = 2
-WAIT_AT = (0, 2)
 MIB = 1024 * 1024
 FAR = -(2**20)
+COLORS = 3
 ORDER = (0, 2, 1, 3)
 NT = (((1,), (1,)), ((), ()))
 NN = (((1,), (0,)), ((), ()))
@@ -80,33 +80,32 @@
     slots, lat_all, slot_count = leg_ref.shape
     level_count = spec_ref.shape[1]
     pair_total = low_ref.shape[0]
-    ext_pad = sums_ref.shape[1]
+    ext = lat_dev + 2 * HALO
     width = pl.cdiv(slot_count, LANES) * LANES
     low_copy = pltpu.make_async_copy(low_hbm, low_ref, small_sem.at[0])
     table_copy = pltpu.make_async_copy(table_hbm, table_ref, small_sem.at[1])
     low_copy.start()
+    groups = slots // GROUP
+    bounds = sorted({0, min(2, groups), groups})
     copies = []
-    for start in range(0, slots, GROUP):
-        part = pl.ds(start, GROUP)
-        index = start // GROUP
+    for index, (start, stop) in enumerate(zip(bounds[:-1], bounds[1:], strict=True)):
+        part = pl.ds(start * GROUP, (stop - start) * GROUP)
         pair = (
             pltpu.make_async_copy(spec_hbm.at[part], spec_ref.at[part], spec_sem.at[index]),
             pltpu.make_async_copy(leg_hbm.at[part], leg_ref.at[part], leg_sem.at[index]),
         )
         for copy in pair:
             copy.start()
-        copies.append(pair)
+        copies.append((start, pair))
     table_copy.start()
     wave = lax.axis_index("wave")
     slot_of_row = lax.broadcasted_iota(jnp.int32, (GROUP, LANES), 0)
     slot_pos = lax.broadcasted_iota(jnp.int32, (GROUP, width), 1)
     low_copy.wait()
-    groups = slots // GROUP
     for index in range(groups):
-        if index in WAIT_AT:
-            later = [at for at in WAIT_AT if at > index]
-            for at in range(index, later[0] if later else groups):
-                for copy in copies[at]:
+        for at, pair in copies:
+            if at == index:
+                for copy in pair:
                     copy.wait()
         start = index * GROUP
         base = wave * pair_local + start
@@ -144,11 +143,12 @@
             block = crossed[slot * lat_all : (slot + 1) * lat_all]
             sums = jnp.where(slot_of_lane == slot, block, sums)
         edge = jnp.zeros((HALO, count), jnp.float32)
-        tail = jnp.zeros((ext_pad, count), jnp.float32)
-        padded = jnp.concatenate([edge, sums, tail], axis=0)
-        here = slice(index * count, (index + 1) * count)
+        padded = jnp.concatenate([edge, sums, edge], axis=0)
+        here = slice(index * ext, (index + 1) * ext)
         for dest in range(sums_ref.shape[0]):
-            sums_ref[dest, :, here] = padded[dest * lat_dev : dest * lat_dev + ext_pad]
+            sums_ref[dest, here] = padded[dest * lat_dev : dest * lat_dev + ext]
+    used = groups * ext
+    sums_ref[:, used:] = jnp.zeros_like(sums_ref[:, used:])
     for step, chip_ref in enumerate(chip_refs):
         dest = (wave // 2 ^ step) * 2
         for core in range(2):
@@ -161,10 +161,11 @@
     slots, level_count = spectral.shape[:2]
     lat_all = legendre.shape[1]
     lat_dev = lat_all // wave_size
-    lanes = 8 * level_count * slots
-    ext_pad = pl.cdiv(lat_dev + 2 * HALO, 8) * 8
+    lanes = 8 * level_count * GROUP
+    ext = lat_dev + 2 * HALO
+    rows = pl.cdiv((slots // GROUP - 1) * ext + pl.cdiv(ext, 8) * 8, 8) * 8
     chips = wave_size // 2
-    out = jax.ShapeDtypeStruct((2, ext_pad, lanes), jnp.float32)
+    out = jax.ShapeDtypeStruct((2, rows, lanes), jnp.float32)
     outs = [out] * chips + [jax.ShapeDtypeStruct(tables.shape, tables.dtype)]
     results = pl.pallas_call(
         functools.partial(legendre_kernel, pair_local, lat_dev),
@@ -175,10 +176,10 @@
             pltpu.SMEM(pair_low.shape, jnp.int32),
             pltpu.VMEM(spectral.shape, jnp.float32),
             pltpu.VMEM(legendre.shape, jnp.float32),
-            pltpu.VMEM((wave_size, ext_pad, lanes), jnp.float32),
+            pltpu.VMEM((wave_size, rows, lanes), jnp.float32),
             pltpu.SemaphoreType.DMA((2,)),
-            pltpu.SemaphoreType.DMA((slots // GROUP,)),
-            pltpu.SemaphoreType.DMA((slots // GROUP,)),
+            pltpu.SemaphoreType.DMA((2,)),
+            pltpu.SemaphoreType.DMA((2,)),
         ],
         compiler_params=pltpu.CompilerParams(vmem_limit_bytes=24 * MIB),
         name="legendre",
@@ -195,14 +196,18 @@
     return lax.ppermute(value, "wave", [(i, i ^ by) for i in range(wave_size)])
 
 
-def trade(value, offset):
+def trade(value, color):
     lev_size, wave_size = lax.axis_size("lev"), lax.axis_size("wave")
     pairs = []
     for lev in range(lev_size):
-        other = lev + 1 if (lev - offset) % 2 == 0 else lev - 1
+        other = lev
+        if lev % COLORS == color and lev + 1 < lev_size:
+            other = lev + 1
+        if lev > 0 and (lev - 1) % COLORS == color:
+            other = lev - 1
         for wave in range(wave_size):
-            there = (other, wave) if 0 <= other < lev_size else (lev, wave ^ 1)
-            pairs.append((lev * wave_size + wave, there[0] * wave_size + there[1]))
+            there = other * wave_size + (wave ^ 1 if other == lev else wave)
+            pairs.append((lev * wave_size + wave, there))
     return lax.ppermute(value, ("lev", "wave"), pairs)
 
 
@@ -340,7 +345,9 @@
     return pieces
 
 
-def level_rows(level, piece_refs, select_ref, table_ref):
+def level_rows(level, lat_dev, piece_refs, select_ref, table_ref):
+    ext = lat_dev + 2 * HALO
+    ext_pad = pl.cdiv(ext, 8) * 8
     half = table_ref.shape[2] // 2
     core = lax.axis_index("wave") % 2
     vectors = []
@@ -348,7 +355,8 @@
     for ref in [piece_refs[2 * order.index(i // 2) + i % 2] for i in range(len(piece_refs))]:
         source = ref[core]
         vectors += [
-            source[:, start : start + LANES] for start in range(0, source.shape[1], LANES)
+            source[start : start + ext_pad]
+            for start in range(0, source.shape[0] - ext_pad + 1, ext)
         ]
     lane = lax.broadcasted_iota(jnp.int32, vectors[0].shape, 1)
     columns = [[] for _ in range(4)]
@@ -455,7 +463,7 @@
     piece_refs, plan_refs = refs[:piece_count], refs[piece_count + 2 : -3]
     select_ref, table_ref = refs[piece_count : piece_count + 2]
     field_ref, horizontal_ref, near_ref = refs[-3:]
-    rows = level_rows(0, piece_refs, select_ref, table_ref)
+    rows = level_rows(0, lat_dev, piece_refs, select_ref, table_ref)
     store_rows(rows, field_ref, 0, lat_dev, near_ref)
     horizontal_ref[...] = interpolate(lat_dev, *[ref[...] for ref in plan_refs], near_ref)
 
@@ -471,7 +479,7 @@
     below = below_ref[...]
     plans = [ref[...] for ref in plan_refs]
     for level in range(1, departed_ref.shape[0] + 1):
-        rows = level_rows(level, piece_refs, select_ref, table_ref)
+        rows = level_rows(level, lat_dev, piece_refs, select_ref, table_ref)
         store_rows(rows, field_ref, level - 1, lat_dev, near_ref)
         copy = pltpu.make_async_copy(
             field_ref.at[pl.ds(level - 1, 1)], field_hbm.at[pl.ds(level, 1)], sems.at[level]
@@ -486,12 +494,15 @@
         copy.wait()
 
 
-def last_kernel(below_ref, odd_ref, even_ref, vertical_ref, out_ref):
+def last_kernel(below_ref, *refs):
+    *above_refs, vertical_ref, out_ref = refs
     lev = lax.axis_index("lev")
     is_last = lev == lax.axis_size("lev") - 1
     vertical = vertical_ref[...]
     below = below_ref[...]
-    above = jnp.where(lev % 2 == 0, even_ref[...], odd_ref[...])
+    above = below
+    for color, above_ref in enumerate(above_refs[::-1]):
+        above = jnp.where(lev % COLORS == color, above_ref[...], above)
     above = jnp.where(is_last, below, above)
     out_ref[...] = (1.0 - vertical) * below + vertical * above
 
@@ -528,7 +539,7 @@
     received[-1], select = lax.optimization_barrier((received[-1], select))
     blocks = lon_count // LANES
     points = 2 * lat_dev * blocks
-    ext_pad = parts[0].shape[1]
+    ext_pad = pl.cdiv(lat_dev + 2 * HALO, 8) * 8
     pieces = []
     for step in chip_order(len(received)):
         pieces += [received[step], swap(received[step], 1)]
@@ -554,8 +565,7 @@
         ),
         name="first_level",
     )(*operands)
-    above_even = trade(horizontal, 0)
-    above_odd = trade(horizontal, 1)
+    above = [trade(horizontal, color) for color in range(COLORS)]
     levels = jax.ShapeDtypeStruct((level_count, 2 * lat_dev, lon_count), jnp.float32)
     grid_field, departed, top = pl.pallas_call(
         functools.partial(later_kernel, lat_dev, len(pieces)),
@@ -579,12 +589,12 @@
     )(*operands, vertical, horizontal, field_first)
     final = pl.pallas_call(
         last_kernel,
-        in_specs=[vmem] * 4,
+        in_specs=[vmem] * (COLORS + 2),
         out_specs=vmem,
         out_shape=flat,
         compiler_params=params,
         name="top_level",
-    )(top, above_odd, above_even, vertical)
+    )(top, *above[::-1], vertical)
     departed = jnp.concatenate([departed, final[None]], axis=0)
     return grid_field, departed.reshape(level_count, 2 * lat_dev, lon_count)
 

time: 19 us -> 18.8 us (0.989)
  waiting for transfers between devices: 4.09 us -> 3.57 us
  starting transfers between devices: 6.83 us -> 7.27 us
    ppermute x2 -> x3, starting transfers between devices: 1.71 us -> 2.15 us  [trade(): return lax.ppermute(value, ('lev', 'wave'), pairs)]
    ppermute x2 -> x3, waiting for transfers between devices: 0.45 us -> 0.02 us  [trade(): return lax.ppermute(value, ('lev', 'wave'), pairs)]
  transfers between devices with their start and end apart: 9 -> 10, of which waited for: 7 -> 6; matrix products, arithmetic and copies ran while one was open for 0% -> 0% of each run, Pallas kernels for 15% -> 15%
where the time goes in v5:
time: 18.8 us; the launch traced here: 18.6 us
  starting transfers between devices  7.27 us (39%)
  Pallas kernels  6.43 us (34%)
  waiting for transfers between devices  3.57 us (19%)
  between operations  0.7 us (4%)
  other arithmetic  0.63 us (3%)
    ppermute x7, starting transfers between devices, swap(): return lax.ppermute(value, 'wave', [(i, i ^ by) for i in range(wave_size)])  5.12 us
    ppermute x7, waiting for transfers between devices, swap(): return lax.ppermute(value, 'wave', [(i, i ^ by) for i in range(wave_size)])  3.55 us
    pallas_call x1, Pallas kernels, legendre_sums(): pl.pallas_call(functools.partial(legendre_kernel, pair_local, lat_dev), i...  2.47 us
    ppermute x3, starting transfers between devices, trade(): return lax.ppermute(value, ('lev', 'wave'), pairs)  2.15 us
    pallas_call x1, Pallas kernels, per_device(): pl.pallas_call(functools.partial(later_kernel, lat_dev, len(pieces)), in_...  1.66 us
    pallas_call x1, Pallas kernels, per_device(): pl.pallas_call(functools.partial(first_kernel, lat_dev, len(pieces)), in_...  1.2 us
    pallas_call x1, Pallas kernels, plan(): pl.pallas_call(functools.partial(plan_kernel, pair_local, lat_dev), in_sp...  1.07 us
    concatenate x1, other arithmetic, per_device(): departed = jnp.concatenate([departed, final[None]], axis=0)  0.63 us
  transfers between devices with their start and end apart: 10, of which 6 were waited for; matrix products, arithmetic and copies ran while one was open for 0% of the time, Pallas kernels for 15%

profile of v5, /device:TPU:0, one launch (start us, length us, event | category | flops | bytes accessed | tf_op | source)
XLA Modules:
  0.0 18.6 jit_solution(455100598145136633)
XLA Ops:
  0.6 2.5 %legendre.1 = (f32[2,32,128]{2,1,0:T(8,128)S(1)}, f32[2,32,128]{2,1,0:T(8,128)S(1)}, f32[2,32,128]{2,1,0:T(8,128)S(1)}, f32[2,32,128]{2,1,0:T(8,128)S(1)}, bf16[2,640,640]{2,1,0:T(8,128)(2,1)S(1)}) custom-call(s32[320]{0:T(512)} %refs_0_.3, f32[40,2,2,641]{3,2,1,0:T(2,128)} %refs_1_.2, f32[40,16,641]{2,1,0:T(8,128)} %refs_2_.2, ...), custom_call_target="tpu_custom_call" | custom-call | tf_op jit(solution)/shard_map/legendre/pallas_call | solution.py:170
  3.1 4.0 %collective-permute-start.1 = (f32[2,32,128]{2,1,0:T(8,128)S(1)}, f32[2,32,128]{2,1,0:T(8,128)S(1)}, u32[]{:S(2)}, u32[]{:S(2)}) collective-permute-start(f32[2,32,128]{2,1,0:T(8,128)S(1)} %get-tuple-element.21), channel_id=1, source_target_pairs={{0,6},{1,7},{2,4},{3,5},{4,2},{5,3},{6,0},{7,1},{8,14},{9,15},{10,... | collective-permute-start | bytes 98312 | tf_op jit(solution)/shard_map/ppermute | solution.py:196
  7.1 0.5 %collective-permute-start.3 = (f32[2,32,128]{2,1,0:T(8,128)S(1)}, f32[2,32,128]{2,1,0:T(8,128)S(1)}, u32[]{:S(2)}, u32[]{:S(2)}) collective-permute-start(f32[2,32,128]{2,1,0:T(8,128)S(1)} %get-tuple-element.24), channel_id=1, source_target_pairs={{0,4},{1,5},{2,6},{3,7},{4,0},{5,1},{6,2},{7,3},{8,12},{9,13},{10,... | collective-permute-start | bytes 98312 | tf_op jit(solution)/shard_map/ppermute | solution.py:196
  7.6 0.1 collective-permute-start.5
  7.7 0.0 collective-permute-start
  7.7 1.1 %plan.1 = (bf16[640,640]{1,0:T(8,128)(2,1)S(1)}, s32[40,128]{1,0:T(8,128)S(1)}, s32[40,128]{1,0:T(8,128)S(1)}, f32[40,128]{1,0:T(8,128)S(1)}, f32[40,128]{1,0:T(8,128)S(1)}, /*index=5*/f32[40,128]{1,0:T(8,128)S(1)}) custom-call(f32[2,32,128]{2,1,0:T(8,128)S(1)} %get-tuple-element.20.after_ref.refs_0_, s32[320]{0:T(512)} %refs_0_.3, s32[40]{0:T(128)} %refs_1_.3, ...), custom_call_target="tpu_custom_call" | custom-call | flops 10000000 | bytes 4000000 | tf_op jit(solution)/shard_map/plan/pallas_call | solution.py:256
  8.8 0.2 collective-permute-done.1.refs_2_
  9.0 2.0 %collective-permute-done.3.refs_4_ = f32[2,32,128]{2,1,0:T(8,128)S(1)} collective-permute-done((f32[2,32,128]{2,1,0:T(8,128)S(1)}, f32[2,32,128]{2,1,0:T(8,128)S(1)}, u32[]{:S(2)}, u32[]{:S(2)}) %collective-permute-start.3) | collective-permute-done | bytes 32800 | tf_op jit(solution)/shard_map/ppermute | solution.py:196
  11.0 0.0 collective-permute-start.4
  11.0 0.5 %collective-permute-done.5.refs_6_ = f32[2,32,128]{2,1,0:T(8,128)S(1)} collective-permute-done((f32[2,32,128]{2,1,0:T(8,128)S(1)}, f32[2,32,128]{2,1,0:T(8,128)S(1)}, u32[]{:S(2)}, u32[]{:S(2)}) %collective-permute-start.5) | collective-permute-done | bytes 32800 | tf_op jit(solution)/shard_map/ppermute | solution.py:196
  11.5 0.0 collective-permute-start.6
  11.5 0.5 %collective-permute-start.2 = (f32[2,32,128]{2,1,0:T(8,128)S(1)}, f32[2,32,128]{2,1,0:T(8,128)S(1)}, u32[]{:S(2)}, u32[]{:S(2)}) collective-permute-start(f32[2,32,128]{2,1,0:T(8,128)S(1)} %collective-permute-done.1.refs_2_), channel_id=1, source_target_pairs={{0,1},{1,0},{2,3},{3,2},{4,5},{5,4},{6,7},{7,6},{8,9},{9,8},{10,11... | collective-permute-start | bytes 98312 | tf_op jit(solution)/shard_map/ppermute | solution.py:196
  12.0 0.0 collective-permute-done.refs_1_
  12.0 0.2 %collective-permute-done.4.refs_5_ = f32[2,32,128]{2,1,0:T(8,128)S(1)} collective-permute-done((f32[2,32,128]{2,1,0:T(8,128)S(1)}, f32[2,32,128]{2,1,0:T(8,128)S(1)}, u32[]{:S(2)}, u32[]{:S(2)}) %collective-permute-start.4) | collective-permute-done | bytes 32800 | tf_op jit(solution)/shard_map/ppermute | solution.py:196
  12.2 0.5 %collective-permute-done.6.refs_7_ = f32[2,32,128]{2,1,0:T(8,128)S(1)} collective-permute-done((f32[2,32,128]{2,1,0:T(8,128)S(1)}, f32[2,32,128]{2,1,0:T(8,128)S(1)}, u32[]{:S(2)}, u32[]{:S(2)}) %collective-permute-start.6) | collective-permute-done | bytes 32800 | tf_op jit(solution)/shard_map/ppermute | solution.py:196
  12.7 0.2 collective-permute-done.2.refs_3_
  12.9 1.2 %first_level.1 = (f32[1,4,1280]{2,1,0:T(4,128)S(1)}, f32[40,128]{1,0:T(8,128)S(1)}) custom-call(f32[2,32,128]{2,1,0:T(8,128)S(1)} %get-tuple-element.20.after_ref.refs_0_, f32[2,32,128]{2,1,0:T(8,128)S(1)} %collective-permute-done.refs_1_, f32[2,32,128]{2,1,0:T(8,128)S(1)} %collective-permute-done.1.refs_2_, ...), custom_call_target="tpu_custom_call" | custom-call | flops 100000000 | bytes 4000000 | tf_op jit(solution)/shard_map/first_level/pallas_call | solution.py:556
  14.1 1.6 %collective-permute-start.9 = (f32[40,128]{1,0:T(8,128)S(1)}, f32[40,128]{1,0:T(8,128)S(1)}, u32[]{:S(2)}, u32[]{:S(2)}) collective-permute-start(f32[40,128]{1,0:T(8,128)S(1)} %get-tuple-element.33.refs_15_), channel_id=1, source_target_pairs={{0,8},{1,9},{2,10},{3,11},{4,12},{5,13},{6,14},{7,15},{8,0},{9,1},... | collective-permute-start | bytes 61448 | tf_op jit(solution)/shard_map/ppermute | solution.py:211
  15.7 0.1 collective-permute-start.8
  15.8 0.4 %collective-permute-start.7 = (f32[40,128]{1,0:T(8,128)S(1)}, f32[40,128]{1,0:T(8,128)S(1)}, u32[]{:S(2)}, u32[]{:S(2)}) collective-permute-start(f32[40,128]{1,0:T(8,128)S(1)} %get-tuple-element.33.refs_15_), channel_id=1, source_target_pairs={{0,1},{1,0},{2,3},{3,2},{4,5},{5,4},{6,7},{7,6},{8,9},{9,8},{10,11... | collective-permute-start | bytes 61448 | tf_op jit(solution)/shard_map/ppermute | solution.py:211
  16.2 1.7 %later_levels.1 = (f32[2,4,1280]{2,1,0:T(4,128)}, f32[1,40,128]{2,1,0:T(8,128)S(1)}, f32[40,128]{1,0:T(8,128)S(1)}) custom-call(f32[2,32,128]{2,1,0:T(8,128)S(1)} %get-tuple-element.20.after_ref.refs_0_, f32[2,32,128]{2,1,0:T(8,128)S(1)} %collective-permute-done.refs_1_, f32[2,32,128]{2,1,0:T(8,128)S(1)} %collective-permute-done.1.refs_2_, ...), custom_call_target="tpu_custom_call" | custom-call | flops 100000000 | bytes 4000000 | tf_op jit(solution)/shard_map/later_levels/pallas_call | solution.py:570
  17.9 0.0 collective-permute-done.9.refs_2_
  17.9 0.0 collective-permute-done.8.refs_1_
  17.9 0.0 collective-permute-done.7.refs_0_
  18.0 0.6 %pad_maximum_fusion = f32[2,4,1280]{2,1,0:T(4,128)} fusion(f32[1,4,1280]{2,1,0:T(4,128)S(1)} %concatenate.9, f32[1,4,1280]{2,1,0:T(4,128)S(1)} %concatenate.8), kind=kLoop, calls=%fused_computation | loop fusion | flops 10240 | bytes 81920 | tf_op jit(solution)/shard_map/concatenate | solution.py:598
  (3 shorter events, 0.1 us)
Async XLA Ops:
  3.1 5.9 %collective-permute-start.1 = (f32[2,32,128]{2,1,0:T(8,128)S(1)}, f32[2,32,128]{2,1,0:T(8,128)S(1)}, u32[]{:S(2)}, u32[]{:S(2)}) collective-permute-start(f32[2,32,128]{2,1,0:T(8,128)S(1)} %get-tuple-element.21), channel_id=1, source_target_pairs={{0,6},{1,7},{2,4},{3,5},{4,2},{5,3},{6,0},{7,1},{8,14},{9,15},{10,... | collective-permute-start | bytes 98312 | tf_op jit(solution)/shard_map/ppermute | solution.py:196
  7.1 3.9 %collective-permute-start.3 = (f32[2,32,128]{2,1,0:T(8,128)S(1)}, f32[2,32,128]{2,1,0:T(8,128)S(1)}, u32[]{:S(2)}, u32[]{:S(2)}) collective-permute-start(f32[2,32,128]{2,1,0:T(8,128)S(1)} %get-tuple-element.24), channel_id=1, source_target_pairs={{0,4},{1,5},{2,6},{3,7},{4,0},{5,1},{6,2},{7,3},{8,12},{9,13},{10,... | collective-permute-start | bytes 98312 | tf_op jit(solution)/shard_map/ppermute | solution.py:196
  7.6 3.9 %collective-permute-start.5 = (f32[2,32,128]{2,1,0:T(8,128)S(1)}, f32[2,32,128]{2,1,0:T(8,128)S(1)}, u32[]{:S(2)}, u32[]{:S(2)}) collective-permute-start(f32[2,32,128]{2,1,0:T(8,128)S(1)} %get-tuple-element.25), channel_id=1, source_target_pairs={{0,2},{1,3},{2,0},{3,1},{4,6},{5,7},{6,4},{7,5},{8,10},{9,11},{10,... | collective-permute-start | bytes 98312 | tf_op jit(solution)/shard_map/ppermute | solution.py:196
  7.7 4.3 %collective-permute-start = (f32[2,32,128]{2,1,0:T(8,128)S(1)}, f32[2,32,128]{2,1,0:T(8,128)S(1)}, u32[]{:S(2)}, u32[]{:S(2)}) collective-permute-start(f32[2,32,128]{2,1,0:T(8,128)S(1)} %get-tuple-element.20.after_ref.refs_0_), channel_id=1, source_target_pairs={{0,1},{1,0},{2,3},{3,2},{4,5},{5,4},{6,7},{7,6},{8,9},{9,8},{10,11... | collective-permute-start | bytes 98312 | tf_op jit(solution)/shard_map/ppermute | solution.py:196
  11.0 1.2 %collective-permute-start.4 = (f32[2,32,128]{2,1,0:T(8,128)S(1)}, f32[2,32,128]{2,1,0:T(8,128)S(1)}, u32[]{:S(2)}, u32[]{:S(2)}) collective-permute-start(f32[2,32,128]{2,1,0:T(8,128)S(1)} %collective-permute-done.3.refs_4_), channel_id=1, source_target_pairs={{0,1},{1,0},{2,3},{3,2},{4,5},{5,4},{6,7},{7,6},{8,9},{9,8},{10,11... | collective-permute-start | bytes 98312 | tf_op jit(solution)/shard_map/ppermute | solution.py:196
  11.5 1.2 %collective-permute-start.6 = (f32[2,32,128]{2,1,0:T(8,128)S(1)}, f32[2,32,128]{2,1,0:T(8,128)S(1)}, u32[]{:S(2)}, u32[]{:S(2)}) collective-permute-start(f32[2,32,128]{2,1,0:T(8,128)S(1)} %collective-permute-done.5.refs_6_), channel_id=1, source_target_pairs={{0,1},{1,0},{2,3},{3,2},{4,5},{5,4},{6,7},{7,6},{8,9},{9,8},{10,11... | collective-permute-start | bytes 98312 | tf_op jit(solution)/shard_map/ppermute | solution.py:196
  11.5 1.4 %collective-permute-start.2 = (f32[2,32,128]{2,1,0:T(8,128)S(1)}, f32[2,32,128]{2,1,0:T(8,128)S(1)}, u32[]{:S(2)}, u32[]{:S(2)}) collective-permute-start(f32[2,32,128]{2,1,0:T(8,128)S(1)} %collective-permute-done.1.refs_2_), channel_id=1, source_target_pairs={{0,1},{1,0},{2,3},{3,2},{4,5},{5,4},{6,7},{7,6},{8,9},{9,8},{10,11... | collective-permute-start | bytes 98312 | tf_op jit(solution)/shard_map/ppermute | solution.py:196
  14.1 3.8 %collective-permute-start.9 = (f32[40,128]{1,0:T(8,128)S(1)}, f32[40,128]{1,0:T(8,128)S(1)}, u32[]{:S(2)}, u32[]{:S(2)}) collective-permute-start(f32[40,128]{1,0:T(8,128)S(1)} %get-tuple-element.33.refs_15_), channel_id=1, source_target_pairs={{0,8},{1,9},{2,10},{3,11},{4,12},{5,13},{6,14},{7,15},{8,0},{9,1},... | collective-permute-start | bytes 61448 | tf_op jit(solution)/shard_map/ppermute | solution.py:211
  15.7 2.2 %collective-permute-start.8 = (f32[40,128]{1,0:T(8,128)S(1)}, f32[40,128]{1,0:T(8,128)S(1)}, u32[]{:S(2)}, u32[]{:S(2)}) collective-permute-start(f32[40,128]{1,0:T(8,128)S(1)} %get-tuple-element.33.refs_15_), channel_id=1, source_target_pairs={{0,1},{1,0},{2,3},{3,2},{4,5},{5,4},{6,7},{7,6},{8,16},{9,17},{10,... | collective-permute-start | bytes 61448 | tf_op jit(solution)/shard_map/ppermute | solution.py:211
  15.8 2.1 %collective-permute-start.7 = (f32[40,128]{1,0:T(8,128)S(1)}, f32[40,128]{1,0:T(8,128)S(1)}, u32[]{:S(2)}, u32[]{:S(2)}) collective-permute-start(f32[40,128]{1,0:T(8,128)S(1)} %get-tuple-element.33.refs_15_), channel_id=1, source_target_pairs={{0,1},{1,0},{2,3},{3,2},{4,5},{5,4},{6,7},{7,6},{8,9},{9,8},{10,11... | collective-permute-start | bytes 61448 | tf_op jit(solution)/shard_map/ppermute | solution.py:211

commit v6 on v5

--- a/solution.py
+++ b/solution.py
@@ -38,15 +38,23 @@
     return jnp.concatenate(parts, axis=1)
 
 
+def half_vectors(chips, groups):
+    return pl.cdiv(chips * groups, 8) * 8
+
+
 def wave_rows(low_ref, wave, pair_local, waves_ref):
     row = lax.broadcasted_iota(jnp.int32, (GROUP, LANES), 0)
     groups = pl.cdiv(pair_local, GROUP)
-    for index in range(waves_ref.shape[0] // GROUP):
-        source, group = divmod(index, groups)
-        base = (wave ^ source) * pair_local + group * GROUP
+    chips = low_ref.shape[0] // pair_local // 2
+    count = half_vectors(chips, groups)
+    for index in range(2 * count):
+        half, place = divmod(index, count)
+        chip, group = divmod(place, groups)
         value = jnp.full((GROUP, LANES), FAR, jnp.int32)
-        for slot in range(min(GROUP, pair_local - group * GROUP)):
-            value = jnp.where(row == slot, low_ref[base + slot], value)
+        if chip < chips:
+            base = (wave ^ (2 * chip + half)) * pair_local + group * GROUP
+            for slot in range(min(GROUP, pair_local - group * GROUP)):
+                value = jnp.where(row == slot, low_ref[base + slot], value)
         waves_ref[index * GROUP : (index + 1) * GROUP] = value
 
 
@@ -345,19 +353,19 @@
     return pieces
 
 
-def level_rows(level, lat_dev, piece_refs, select_ref, table_ref):
+def ordered_part(level, lat_dev, piece_refs, half, select_ref):
     ext = lat_dev + 2 * HALO
     ext_pad = pl.cdiv(ext, 8) * 8
-    half = table_ref.shape[2] // 2
     core = lax.axis_index("wave") % 2
     vectors = []
-    order = chip_order(len(piece_refs) // 2)
-    for ref in [piece_refs[2 * order.index(i // 2) + i % 2] for i in range(len(piece_refs))]:
+    order = chip_order(len(piece_refs))
+    for ref in [piece_refs[order.index(step)] for step in range(len(piece_refs))]:
         source = ref[core]
         vectors += [
             source[start : start + ext_pad]
             for start in range(0, source.shape[0] - ext_pad + 1, ext)
         ]
+    vectors += [jnp.zeros_like(vectors[0])] * (-len(vectors) % 8)
     lane = lax.broadcasted_iota(jnp.int32, vectors[0].shape, 1)
     columns = [[] for _ in range(4)]
     for start in range(0, len(vectors), 8):
@@ -366,12 +374,17 @@
     matrix = jnp.concatenate([jnp.concatenate(c, axis=1) for c in columns], axis=0)
     high, low = split(matrix)
     count = high.shape[0] // 2
-    ordered = lax.dot_general(
+    lanes = matrix.shape[1]
+    return lax.dot_general(
         jnp.concatenate([high[:count], low[:count], high[count:], low[count:]], axis=0),
-        select_ref[...],
+        select_ref[half * lanes : (half + 1) * lanes],
         NN,
         preferred_element_type=jnp.float32,
     )
+
+
+def level_rows(ordered, table_ref):
+    count = ordered.shape[0] // 4
     half = ordered.shape[1]
     real = ordered[: 2 * count]
     imag = pltpu.roll(ordered[2 * count :], half // 2, 1)
@@ -459,18 +472,25 @@
     return (1.0 - g) * lower + g * higher
 
 
+def early_kernel(lat_dev, *refs):
+    *piece_refs, select_ref, out_ref = refs
+    for level in range(out_ref.shape[0]):
+        out_ref[level] = ordered_part(level, lat_dev, piece_refs, 0, select_ref)
+
+
 def first_kernel(lat_dev, piece_count, *refs):
-    piece_refs, plan_refs = refs[:piece_count], refs[piece_count + 2 : -3]
-    select_ref, table_ref = refs[piece_count : piece_count + 2]
+    piece_refs, plan_refs = refs[:piece_count], refs[piece_count + 3 : -3]
+    early_ref, select_ref, table_ref = refs[piece_count : piece_count + 3]
     field_ref, horizontal_ref, near_ref = refs[-3:]
-    rows = level_rows(0, lat_dev, piece_refs, select_ref, table_ref)
+    ordered = early_ref[0] + ordered_part(0, lat_dev, piece_refs, 1, select_ref)
+    rows = level_rows(ordered, table_ref)
     store_rows(rows, field_ref, 0, lat_dev, near_ref)
     horizontal_ref[...] = interpolate(lat_dev, *[ref[...] for ref in plan_refs], near_ref)
 
 
 def later_kernel(lat_dev, piece_count, *refs):
-    piece_refs, plan_refs = refs[:piece_count], refs[piece_count + 2 : -9]
-    select_ref, table_ref = refs[piece_count : piece_count + 2]
+    piece_refs, plan_refs = refs[:piece_count], refs[piece_count + 3 : -9]
+    early_ref, select_ref, table_ref = refs[piece_count : piece_count + 3]
     vertical_ref, below_ref, first_ref = refs[-9:-6]
     field_hbm, departed_ref, horizontal_ref, field_ref, near_ref, sems = refs[-6:]
     copies = [pltpu.make_async_copy(first_ref, field_hbm.at[pl.ds(0, 1)], sems.at[0])]
@@ -479,7 +499,8 @@
     below = below_ref[...]
     plans = [ref[...] for ref in plan_refs]
     for level in range(1, departed_ref.shape[0] + 1):
-        rows = level_rows(level, lat_dev, piece_refs, select_ref, table_ref)
+        ordered = early_ref[level] + ordered_part(level, lat_dev, piece_refs, 1, select_ref)
+        rows = level_rows(ordered, table_ref)
         store_rows(rows, field_ref, level - 1, lat_dev, near_ref)
         copy = pltpu.make_async_copy(
             field_ref.at[pl.ds(level - 1, 1)], field_hbm.at[pl.ds(level, 1)], sems.at[level]
@@ -501,7 +522,7 @@
     vertical = vertical_ref[...]
     below = below_ref[...]
     above = below
-    for color, above_ref in enumerate(above_refs[::-1]):
+    for color, above_ref in enumerate(above_refs):
         above = jnp.where(lev % COLORS == color, above_ref[...], above)
     above = jnp.where(is_last, below, above)
     out_ref[...] = (1.0 - vertical) * below + vertical * above
@@ -533,20 +554,33 @@
         tilt_steps,
         pair_local,
         lat_dev,
-        wave_size * slots,
+        2 * GROUP * half_vectors(wave_size // 2, slots // GROUP),
         wavenumber_count,
     )
     received[-1], select = lax.optimization_barrier((received[-1], select))
     blocks = lon_count // LANES
     points = 2 * lat_dev * blocks
     ext_pad = pl.cdiv(lat_dev + 2 * HALO, 8) * 8
-    pieces = []
-    for step in chip_order(len(received)):
-        pieces += [received[step], swap(received[step], 1)]
+    received = [received[step] for step in chip_order(len(received))]
+    pieces = [swap(piece, 1) for piece in received]
     vmem = pl.BlockSpec(memory_space=pltpu.VMEM)
     params = pltpu.CompilerParams(vmem_limit_bytes=24 * MIB)
+    early = pl.pallas_call(
+        functools.partial(early_kernel, lat_dev),
+        in_specs=[vmem] * (len(received) + 1),
+        out_specs=vmem,
+        out_shape=jax.ShapeDtypeStruct(
+            (level_count, 8 * ext_pad, wavenumber_count), jnp.float32
+        ),
+        compiler_params=params,
+        cost_estimate=pl.CostEstimate(
+            flops=10**8, bytes_accessed=2 * 10**6, transcendentals=0
+        ),
+        name="early",
+    )(*received, select)
     operands = (
         *pieces,
+        early,
         select,
         tables,
         *plans,
@@ -594,7 +628,7 @@
         out_shape=flat,
         compiler_params=params,
         name="top_level",
-    )(top, *above[::-1], vertical)
+    )(top, *above, vertical)
     departed = jnp.concatenate([departed, final[None]], axis=0)
     return grid_field, departed.reshape(level_count, 2 * lat_dev, lon_count)
 

time: 18.8 us -> 18.5 us (0.984)
  waiting for transfers between devices: 3.57 us -> 3.05 us
  Pallas kernels: 6.43 us -> 6.72 us
    ppermute x7, waiting for transfers between devices: 3.55 us -> 2.91 us  [swap(): return lax.ppermute(value, 'wave', [(i, i ^ by) for i in range(wave_size)])]
    pallas_call x0 -> x1, Pallas kernels: none -> 0.54 us  [per_device(): pl.pallas_call(functools.partial(early_kernel, lat_dev), in_specs=[vmem]...]
  transfers between devices with their start and end apart: 10 -> 10, of which waited for: 6 -> 6; matrix products, arithmetic and copies ran while one was open for 0% -> 0% of each run, Pallas kernels for 15% -> 17%
where the time goes in v6:
time: 18.5 us; the launch traced here: 18.3 us
  starting transfers between devices  7.18 us (39%)
  Pallas kernels  6.72 us (36%)
  waiting for transfers between devices  3.05 us (16%)
  between operations  0.71 us (4%)
  other arithmetic  0.63 us (3%)
    ppermute x7, starting transfers between devices, swap(): return lax.ppermute(value, 'wave', [(i, i ^ by) for i in range(wave_size)])  5.03 us
    ppermute x7, waiting for transfers between devices, swap(): return lax.ppermute(value, 'wave', [(i, i ^ by) for i in range(wave_size)])  2.91 us
    pallas_call x1, Pallas kernels, legendre_sums(): pl.pallas_call(functools.partial(legendre_kernel, pair_local, lat_dev), i...  2.47 us
    ppermute x3, starting transfers between devices, trade(): return lax.ppermute(value, ('lev', 'wave'), pairs)  2.15 us
    pallas_call x1, Pallas kernels, per_device(): pl.pallas_call(functools.partial(later_kernel, lat_dev, len(pieces)), in_...  1.54 us
    pallas_call x1, Pallas kernels, per_device(): pl.pallas_call(functools.partial(first_kernel, lat_dev, len(pieces)), in_...  1.08 us
    pallas_call x1, Pallas kernels, plan(): pl.pallas_call(functools.partial(plan_kernel, pair_local, lat_dev), in_sp...  1.07 us
    concatenate x1, other arithmetic, per_device(): departed = jnp.concatenate([departed, final[None]], axis=0)  0.63 us
  transfers between devices with their start and end apart: 10, of which 6 were waited for; matrix products, arithmetic and copies ran while one was open for 0% of the time, Pallas kernels for 17%

profile of v6, /device:TPU:0, one launch (start us, length us, event | category | flops | bytes accessed | tf_op | source)
XLA Modules:
  0.0 18.3 jit_solution(15307919782882139107)
XLA Ops:
  0.6 2.5 %legendre.1 = (f32[2,32,128]{2,1,0:T(8,128)S(1)}, f32[2,32,128]{2,1,0:T(8,128)S(1)}, f32[2,32,128]{2,1,0:T(8,128)S(1)}, f32[2,32,128]{2,1,0:T(8,128)S(1)}, bf16[2,640,640]{2,1,0:T(8,128)(2,1)S(1)}) custom-call(s32[320]{0:T(512)} %refs_0_.3, f32[40,2,2,641]{3,2,1,0:T(2,128)} %refs_1_.2, f32[40,16,641]{2,1,0:T(8,128)} %refs_2_.2, ...), custom_call_target="tpu_custom_call" | custom-call | tf_op jit(solution)/shard_map/legendre/pallas_call | solution.py:178
  3.1 4.0 %collective-permute-start.1 = (f32[2,32,128]{2,1,0:T(8,128)S(1)}, f32[2,32,128]{2,1,0:T(8,128)S(1)}, u32[]{:S(2)}, u32[]{:S(2)}) collective-permute-start(f32[2,32,128]{2,1,0:T(8,128)S(1)} %get-tuple-element.21), channel_id=1, source_target_pairs={{0,6},{1,7},{2,4},{3,5},{4,2},{5,3},{6,0},{7,1},{8,14},{9,15},{10,... | collective-permute-start | bytes 98312 | tf_op jit(solution)/shard_map/ppermute | solution.py:204
  7.1 0.5 %collective-permute-start.3 = (f32[2,32,128]{2,1,0:T(8,128)S(1)}, f32[2,32,128]{2,1,0:T(8,128)S(1)}, u32[]{:S(2)}, u32[]{:S(2)}) collective-permute-start(f32[2,32,128]{2,1,0:T(8,128)S(1)} %get-tuple-element.24), channel_id=1, source_target_pairs={{0,4},{1,5},{2,6},{3,7},{4,0},{5,1},{6,2},{7,3},{8,12},{9,13},{10,... | collective-permute-start | bytes 98312 | tf_op jit(solution)/shard_map/ppermute | solution.py:204
  7.6 0.1 collective-permute-start.5
  7.7 0.0 collective-permute-start
  7.7 1.1 %plan.1 = (bf16[768,640]{1,0:T(8,128)(2,1)S(1)}, s32[40,128]{1,0:T(8,128)S(1)}, s32[40,128]{1,0:T(8,128)S(1)}, f32[40,128]{1,0:T(8,128)S(1)}, f32[40,128]{1,0:T(8,128)S(1)}, /*index=5*/f32[40,128]{1,0:T(8,128)S(1)}) custom-call(f32[2,32,128]{2,1,0:T(8,128)S(1)} %get-tuple-element.20.after_ref.refs_0_, s32[320]{0:T(512)} %refs_0_.3, s32[40]{0:T(128)} %refs_1_.3, ...), custom_call_target="tpu_custom_call" | custom-call | flops 10000000 | bytes 4000000 | tf_op jit(solution)/shard_map/plan/pallas_call | solution.py:264
  8.8 0.2 collective-permute-done.1.refs_1_
  9.0 0.4 %collective-permute-start.2 = (f32[2,32,128]{2,1,0:T(8,128)S(1)}, f32[2,32,128]{2,1,0:T(8,128)S(1)}, u32[]{:S(2)}, u32[]{:S(2)}) collective-permute-start(f32[2,32,128]{2,1,0:T(8,128)S(1)} %collective-permute-done.1.refs_1_), channel_id=1, source_target_pairs={{0,1},{1,0},{2,3},{3,2},{4,5},{5,4},{6,7},{7,6},{8,9},{9,8},{10,11... | collective-permute-start | bytes 98312 | tf_op jit(solution)/shard_map/ppermute | solution.py:204
  9.4 1.6 %collective-permute-done.3.refs_2_ = f32[2,32,128]{2,1,0:T(8,128)S(1)} collective-permute-done((f32[2,32,128]{2,1,0:T(8,128)S(1)}, f32[2,32,128]{2,1,0:T(8,128)S(1)}, u32[]{:S(2)}, u32[]{:S(2)}) %collective-permute-start.3) | collective-permute-done | bytes 32800 | tf_op jit(solution)/shard_map/ppermute | solution.py:204
  11.0 0.0 collective-permute-start.4
  11.0 0.5 %collective-permute-done.5.refs_3_ = f32[2,32,128]{2,1,0:T(8,128)S(1)} collective-permute-done((f32[2,32,128]{2,1,0:T(8,128)S(1)}, f32[2,32,128]{2,1,0:T(8,128)S(1)}, u32[]{:S(2)}, u32[]{:S(2)}) %collective-permute-start.5) | collective-permute-done | bytes 32800 | tf_op jit(solution)/shard_map/ppermute | solution.py:204
  11.5 0.0 collective-permute-start.6
  11.5 0.5 %early.1.refs_4_ = f32[2,64,640]{2,1,0:T(8,128)S(1)} custom-call(f32[2,32,128]{2,1,0:T(8,128)S(1)} %get-tuple-element.20.after_ref.refs_0_, f32[2,32,128]{2,1,0:T(8,128)S(1)} %collective-permute-done.1.refs_1_, f32[2,32,128]{2,1,0:T(8,128)S(1)} %collective-permute-done.3.refs_2_, f32[2,32,128]{2,1,0:T(8,128)S(1)} %collective-permute-done.5.refs_3_, ...), custom_call_target="tpu_custom_call" | custom-call | flops 100000000 | bytes 2000000 | tf_op jit(solution)/shard_map/early/pallas_call | solution.py:568
  12.0 0.0 collective-permute-done.refs_0_
  12.1 0.0 collective-permute-done.2.refs_1_
  12.1 0.1 collective-permute-done.4.refs_2_
  12.2 0.5 %collective-permute-done.6.refs_3_ = f32[2,32,128]{2,1,0:T(8,128)S(1)} collective-permute-done((f32[2,32,128]{2,1,0:T(8,128)S(1)}, f32[2,32,128]{2,1,0:T(8,128)S(1)}, u32[]{:S(2)}, u32[]{:S(2)}) %collective-permute-start.6) | collective-permute-done | bytes 32800 | tf_op jit(solution)/shard_map/ppermute | solution.py:204
  12.7 1.1 %first_level.1 = (f32[1,4,1280]{2,1,0:T(4,128)S(1)}, f32[40,128]{1,0:T(8,128)S(1)}) custom-call(f32[2,32,128]{2,1,0:T(8,128)S(1)} %collective-permute-done.refs_0_, f32[2,32,128]{2,1,0:T(8,128)S(1)} %collective-permute-done.2.refs_1_, f32[2,32,128]{2,1,0:T(8,128)S(1)} %collective-permute-done.4.refs_2_, f32[2,32,128]{2,1,0:T(8,128)S(1)} %collective-permute-done.6.refs_3_, ...), custom_call_target="tpu_custom_call" | custom-call | flops 100000000 | bytes 4000000 | tf_op jit(solution)/shard_map/first_level/pallas_call | solution.py:590
  13.8 1.6 %collective-permute-start.7 = (f32[40,128]{1,0:T(8,128)S(1)}, f32[40,128]{1,0:T(8,128)S(1)}, u32[]{:S(2)}, u32[]{:S(2)}) collective-permute-start(f32[40,128]{1,0:T(8,128)S(1)} %get-tuple-element.33.refs_12_), channel_id=1, source_target_pairs={{0,8},{1,9},{2,10},{3,11},{4,12},{5,13},{6,14},{7,15},{8,0},{9,1},... | collective-permute-start | bytes 61448 | tf_op jit(solution)/shard_map/ppermute | solution.py:219
  15.4 0.0 collective-permute-start.8
  15.4 0.5 %collective-permute-start.9 = (f32[40,128]{1,0:T(8,128)S(1)}, f32[40,128]{1,0:T(8,128)S(1)}, u32[]{:S(2)}, u32[]{:S(2)}) collective-permute-start(f32[40,128]{1,0:T(8,128)S(1)} %get-tuple-element.33.refs_12_), channel_id=1, source_target_pairs={{0,1},{1,0},{2,3},{3,2},{4,5},{5,4},{6,7},{7,6},{8,9},{9,8},{10,11... | collective-permute-start | bytes 61448 | tf_op jit(solution)/shard_map/ppermute | solution.py:219
  15.9 1.5 %later_levels.1 = (f32[2,4,1280]{2,1,0:T(4,128)}, f32[1,40,128]{2,1,0:T(8,128)S(1)}, f32[40,128]{1,0:T(8,128)S(1)}) custom-call(f32[2,32,128]{2,1,0:T(8,128)S(1)} %collective-permute-done.refs_0_, f32[2,32,128]{2,1,0:T(8,128)S(1)} %collective-permute-done.2.refs_1_, f32[2,32,128]{2,1,0:T(8,128)S(1)} %collective-permute-done.4.refs_2_, ...), custom_call_target="tpu_custom_call" | custom-call | flops 100000000 | bytes 4000000 | tf_op jit(solution)/shard_map/later_levels/pallas_call | solution.py:604
  17.5 0.1 collective-permute-done.7.refs_0_
  17.6 0.0 collective-permute-done.8.refs_1_
  17.6 0.0 collective-permute-done.9.refs_2_
  17.7 0.6 %pad_maximum_fusion = f32[2,4,1280]{2,1,0:T(4,128)} fusion(f32[1,4,1280]{2,1,0:T(4,128)S(1)} %concatenate.9, f32[1,4,1280]{2,1,0:T(4,128)S(1)} %concatenate.8), kind=kLoop, calls=%fused_computation | loop fusion | flops 10240 | bytes 81920 | tf_op jit(solution)/shard_map/concatenate | solution.py:632
  (3 shorter events, 0.1 us)
Async XLA Ops:
  3.1 5.9 %collective-permute-start.1 = (f32[2,32,128]{2,1,0:T(8,128)S(1)}, f32[2,32,128]{2,1,0:T(8,128)S(1)}, u32[]{:S(2)}, u32[]{:S(2)}) collective-permute-start(f32[2,32,128]{2,1,0:T(8,128)S(1)} %get-tuple-element.21), channel_id=1, source_target_pairs={{0,6},{1,7},{2,4},{3,5},{4,2},{5,3},{6,0},{7,1},{8,14},{9,15},{10,... | collective-permute-start | bytes 98312 | tf_op jit(solution)/shard_map/ppermute | solution.py:204
  7.1 3.9 %collective-permute-start.3 = (f32[2,32,128]{2,1,0:T(8,128)S(1)}, f32[2,32,128]{2,1,0:T(8,128)S(1)}, u32[]{:S(2)}, u32[]{:S(2)}) collective-permute-start(f32[2,32,128]{2,1,0:T(8,128)S(1)} %get-tuple-element.24), channel_id=1, source_target_pairs={{0,4},{1,5},{2,6},{3,7},{4,0},{5,1},{6,2},{7,3},{8,12},{9,13},{10,... | collective-permute-start | bytes 98312 | tf_op jit(solution)/shard_map/ppermute | solution.py:204
  7.6 3.9 %collective-permute-start.5 = (f32[2,32,128]{2,1,0:T(8,128)S(1)}, f32[2,32,128]{2,1,0:T(8,128)S(1)}, u32[]{:S(2)}, u32[]{:S(2)}) collective-permute-start(f32[2,32,128]{2,1,0:T(8,128)S(1)} %get-tuple-element.25), channel_id=1, source_target_pairs={{0,2},{1,3},{2,0},{3,1},{4,6},{5,7},{6,4},{7,5},{8,10},{9,11},{10,... | collective-permute-start | bytes 98312 | tf_op jit(solution)/shard_map/ppermute | solution.py:204
  7.7 4.3 %collective-permute-start = (f32[2,32,128]{2,1,0:T(8,128)S(1)}, f32[2,32,128]{2,1,0:T(8,128)S(1)}, u32[]{:S(2)}, u32[]{:S(2)}) collective-permute-start(f32[2,32,128]{2,1,0:T(8,128)S(1)} %get-tuple-element.20.after_ref.refs_0_), channel_id=1, source_target_pairs={{0,1},{1,0},{2,3},{3,2},{4,5},{5,4},{6,7},{7,6},{8,9},{9,8},{10,11... | collective-permute-start | bytes 98312 | tf_op jit(solution)/shard_map/ppermute | solution.py:204
  9.0 3.1 %collective-permute-start.2 = (f32[2,32,128]{2,1,0:T(8,128)S(1)}, f32[2,32,128]{2,1,0:T(8,128)S(1)}, u32[]{:S(2)}, u32[]{:S(2)}) collective-permute-start(f32[2,32,128]{2,1,0:T(8,128)S(1)} %collective-permute-done.1.refs_1_), channel_id=1, source_target_pairs={{0,1},{1,0},{2,3},{3,2},{4,5},{5,4},{6,7},{7,6},{8,9},{9,8},{10,11... | collective-permute-start | bytes 98312 | tf_op jit(solution)/shard_map/ppermute | solution.py:204
  11.0 1.2 %collective-permute-start.4 = (f32[2,32,128]{2,1,0:T(8,128)S(1)}, f32[2,32,128]{2,1,0:T(8,128)S(1)}, u32[]{:S(2)}, u32[]{:S(2)}) collective-permute-start(f32[2,32,128]{2,1,0:T(8,128)S(1)} %collective-permute-done.3.refs_2_), channel_id=1, source_target_pairs={{0,1},{1,0},{2,3},{3,2},{4,5},{5,4},{6,7},{7,6},{8,9},{9,8},{10,11... | collective-permute-start | bytes 98312 | tf_op jit(solution)/shard_map/ppermute | solution.py:204
  11.5 1.2 %collective-permute-start.6 = (f32[2,32,128]{2,1,0:T(8,128)S(1)}, f32[2,32,128]{2,1,0:T(8,128)S(1)}, u32[]{:S(2)}, u32[]{:S(2)}) collective-permute-start(f32[2,32,128]{2,1,0:T(8,128)S(1)} %collective-permute-done.5.refs_3_), channel_id=1, source_target_pairs={{0,1},{1,0},{2,3},{3,2},{4,5},{5,4},{6,7},{7,6},{8,9},{9,8},{10,11... | collective-permute-start | bytes 98312 | tf_op jit(solution)/shard_map/ppermute | solution.py:204
  13.8 3.8 %collective-permute-start.7 = (f32[40,128]{1,0:T(8,128)S(1)}, f32[40,128]{1,0:T(8,128)S(1)}, u32[]{:S(2)}, u32[]{:S(2)}) collective-permute-start(f32[40,128]{1,0:T(8,128)S(1)} %get-tuple-element.33.refs_12_), channel_id=1, source_target_pairs={{0,8},{1,9},{2,10},{3,11},{4,12},{5,13},{6,14},{7,15},{8,0},{9,1},... | collective-permute-start | bytes 61448 | tf_op jit(solution)/shard_map/ppermute | solution.py:219
  15.4 2.2 %collective-permute-start.8 = (f32[40,128]{1,0:T(8,128)S(1)}, f32[40,128]{1,0:T(8,128)S(1)}, u32[]{:S(2)}, u32[]{:S(2)}) collective-permute-start(f32[40,128]{1,0:T(8,128)S(1)} %get-tuple-element.33.refs_12_), channel_id=1, source_target_pairs={{0,1},{1,0},{2,3},{3,2},{4,5},{5,4},{6,7},{7,6},{8,16},{9,17},{10,... | collective-permute-start | bytes 61448 | tf_op jit(solution)/shard_map/ppermute | solution.py:219
  15.4 2.2 %collective-permute-start.9 = (f32[40,128]{1,0:T(8,128)S(1)}, f32[40,128]{1,0:T(8,128)S(1)}, u32[]{:S(2)}, u32[]{:S(2)}) collective-permute-start(f32[40,128]{1,0:T(8,128)S(1)} %get-tuple-element.33.refs_12_), channel_id=1, source_target_pairs={{0,1},{1,0},{2,3},{3,2},{4,5},{5,4},{6,7},{7,6},{8,9},{9,8},{10,11... | collective-permute-start | bytes 61448 | tf_op jit(solution)/shard_map/ppermute | solution.py:219

commit v7 on v6

--- a/solution.py
+++ b/solution.py
@@ -219,9 +219,9 @@
     return lax.ppermute(value, ("lev", "wave"), pairs)
 
 
-def plan_kernel(pair_local, lat_dev, after_ref, *refs):
+def plan_kernel(pair_local, lat_dev, table_ref, *refs):
     sources = refs[:5]
-    select_ref, *plan_refs = refs[5:-7]
+    select_ref, turned_ref, turn_ref, *plan_refs = refs[5:-7]
     low_ref, lat_ref, col_ref, lon_ref, tilt_ref, waves_ref, sems = refs[-7:]
     copies = [
         pltpu.make_async_copy(there, here, sems.at[i])
@@ -247,14 +247,32 @@
         waves = jnp.concatenate([waves] * (half // LANES), axis=1)
         match = jnp.where(waves == order, 1.0, 0.0).astype(jnp.bfloat16)
         select_ref[2 * start : 2 * (start + GROUP)] = match
-
-
-def plan(after, pair_low, dep_lat, dep_col, lon_steps, tilt_steps, pair_local, lat_dev, slots, half):
+    row = lax.broadcasted_iota(jnp.int32, (2 * GROUP, half), 0)
+    sign = jnp.where((kind == 0) | (kind == 2), 1.0, -1.0)
+    turns = jnp.where((row == 0) == (kind < 2), sign, 0.0)
+    turns = jnp.where(row < 2, turns, 0.0).astype(jnp.bfloat16)
+    lanes = select_ref.shape[0] // 2
+    late = select_ref[lanes:]
+    turn_ref[...] = lax.dot_general(turns, late, NT, preferred_element_type=jnp.float32)
+    even, odd = table_ref[0], table_ref[1]
+    both = (
+        jnp.concatenate([even[: half // 2], odd[half // 2 :]], axis=0),
+        jnp.concatenate([even[half // 2 :], odd[: half // 2]], axis=0),
+    )
+    for part, table in enumerate(both):
+        turned_ref[part * lanes : (part + 1) * lanes] = lax.dot_general(
+            late, table, NN, preferred_element_type=jnp.float32
+        ).astype(jnp.bfloat16)
+
+
+def plan(tables, pair_low, dep_lat, dep_col, lon_steps, tilt_steps, pair_local, lat_dev, slots, half):
     operands = (pair_low, dep_lat, dep_col, lon_steps, tilt_steps)
     integer = jax.ShapeDtypeStruct(lon_steps.shape, jnp.int32)
     fraction = jax.ShapeDtypeStruct(lon_steps.shape, jnp.float32)
     outs = [
         jax.ShapeDtypeStruct((2 * slots, half), jnp.bfloat16),
+        jax.ShapeDtypeStruct((2 * slots, tables.shape[2]), jnp.bfloat16),
+        jax.ShapeDtypeStruct((2 * GROUP, slots), jnp.float32),
         integer,
         integer,
         fraction,
@@ -263,7 +281,7 @@
     ]
     return pl.pallas_call(
         functools.partial(plan_kernel, pair_local, lat_dev),
-        in_specs=[pl.BlockSpec(memory_space=pl.ANY)]
+        in_specs=[pl.BlockSpec(memory_space=pltpu.VMEM)]
         + [pl.BlockSpec(memory_space=pltpu.HBM)] * len(operands),
         out_specs=[pl.BlockSpec(memory_space=pltpu.VMEM)] * len(outs),
         out_shape=outs,
@@ -281,7 +299,7 @@
             flops=10**7, bytes_accessed=4 * 10**6, transcendentals=0
         ),
         name="plan",
-    )(after, *[pltpu.with_memory_space_constraint(x, pltpu.HBM) for x in operands])
+    )(tables, *[pltpu.with_memory_space_constraint(x, pltpu.HBM) for x in operands])
 
 
 def fourier_tables(wavenumber_count):
@@ -353,7 +371,7 @@
     return pieces
 
 
-def ordered_part(level, lat_dev, piece_refs, half, select_ref):
+def slot_matrix(level, lat_dev, piece_refs):
     ext = lat_dev + 2 * HALO
     ext_pad = pl.cdiv(ext, 8) * 8
     core = lax.axis_index("wave") % 2
@@ -372,6 +390,11 @@
         for kind, piece in enumerate(regroup(vectors[start : start + 8], level, lane)):
             columns[kind].append(piece)
     matrix = jnp.concatenate([jnp.concatenate(c, axis=1) for c in columns], axis=0)
+    return matrix
+
+
+def ordered_part(level, lat_dev, piece_refs, half, select_ref):
+    matrix = slot_matrix(level, lat_dev, piece_refs)
     high, low = split(matrix)
     count = high.shape[0] // 2
     lanes = matrix.shape[1]
@@ -383,7 +406,7 @@
     )
 
 
-def level_rows(ordered, table_ref):
+def level_quarters(ordered, table_ref):
     count = ordered.shape[0] // 4
     half = ordered.shape[1]
     real = ordered[: 2 * count]
@@ -408,13 +431,41 @@
     near, far = [
         [add_halves(product, start, count) for product in products] for start in (0, 2 * count)
     ]
-    first = join(
-        [a + b for a, b in zip(*near, strict=True)], [a + b for a, b in zip(*far, strict=True)]
+    return [
+        [a + b for a, b in zip(*near, strict=True)],
+        [a + b for a, b in zip(*far, strict=True)],
+        [a - b for a, b in zip(*near, strict=True)],
+        [a - b for a, b in zip(*far, strict=True)],
+    ]
+
+
+def level_rows(quarters):
+    return join(quarters[0], quarters[1]) + join(quarters[2], quarters[3])
+
+
+def late_quarters(matrix, turned_ref, turn_ref):
+    count = matrix.shape[0] // 2
+    cosine = jnp.broadcast_to(turn_ref[0:1], (count, matrix.shape[1]))
+    sine = jnp.broadcast_to(turn_ref[1:2], (count, matrix.shape[1]))
+    square = cosine * cosine - sine * sine
+    parts = [
+        (part[:count].astype(jnp.float32), part[count:].astype(jnp.float32))
+        for part in split(matrix)
+    ]
+    rows = []
+    rows += [(re, im) for re, im in parts]
+    rows += [(cosine * re - sine * im, cosine * im + sine * re) for re, im in parts]
+    rows += [(square * re, square * im) for re, im in parts]
+    rows += [(cosine * re + sine * im, cosine * im - sine * re) for re, im in parts]
+    product = lax.dot_general(
+        jnp.concatenate([jnp.concatenate(row, axis=1) for row in rows], axis=0).astype(
+            jnp.bfloat16
+        ),
+        turned_ref[...],
+        NN,
+        preferred_element_type=jnp.float32,
     )
-    later = join(
-        [a - b for a, b in zip(*near, strict=True)], [a - b for a, b in zip(*far, strict=True)]
-    )
-    return first + later
+    return [add_halves(product, 2 * count * quarter, count) for quarter in range(4)]
 
 
 def store_rows(rows, field_ref, level, lat_dev, near_ref):
@@ -472,19 +523,29 @@
     return (1.0 - g) * lower + g * higher
 
 
-def early_kernel(lat_dev, *refs):
-    *piece_refs, select_ref, out_ref = refs
-    for level in range(out_ref.shape[0]):
-        out_ref[level] = ordered_part(level, lat_dev, piece_refs, 0, select_ref)
+def early_kernel(lat_dev, piece_count, *refs):
+    piece_refs = refs[:piece_count]
+    select_ref, table_ref, quarters_ref, later_ref = refs[piece_count:]
+    ordered = ordered_part(0, lat_dev, piece_refs, 0, select_ref)
+    pieces = sum(level_quarters(ordered, table_ref), [])
+    for index, piece in enumerate(pieces):
+        quarters_ref[index] = piece
+    for level in range(later_ref.shape[0]):
+        later_ref[level] = ordered_part(level + 1, lat_dev, piece_refs, 0, select_ref)
 
 
 def first_kernel(lat_dev, piece_count, *refs):
     piece_refs, plan_refs = refs[:piece_count], refs[piece_count + 3 : -3]
-    early_ref, select_ref, table_ref = refs[piece_count : piece_count + 3]
+    quarters_ref, turned_ref, turn_ref = refs[piece_count : piece_count + 3]
     field_ref, horizontal_ref, near_ref = refs[-3:]
-    ordered = early_ref[0] + ordered_part(0, lat_dev, piece_refs, 1, select_ref)
-    rows = level_rows(ordered, table_ref)
-    store_rows(rows, field_ref, 0, lat_dev, near_ref)
+    matrix = slot_matrix(0, lat_dev, piece_refs)
+    quarters = late_quarters(matrix, turned_ref, turn_ref)
+    size = len(quarters[0])
+    quarters = [
+        [piece + quarters_ref[size * i + j] for j, piece in enumerate(quarter)]
+        for i, quarter in enumerate(quarters)
+    ]
+    store_rows(level_rows(quarters), field_ref, 0, lat_dev, near_ref)
     horizontal_ref[...] = interpolate(lat_dev, *[ref[...] for ref in plan_refs], near_ref)
 
 
@@ -499,8 +560,9 @@
     below = below_ref[...]
     plans = [ref[...] for ref in plan_refs]
     for level in range(1, departed_ref.shape[0] + 1):
-        ordered = early_ref[level] + ordered_part(level, lat_dev, piece_refs, 1, select_ref)
-        rows = level_rows(ordered, table_ref)
+        ordered = early_ref[level - 1]
+        ordered = ordered + ordered_part(level, lat_dev, piece_refs, 1, select_ref)
+        rows = level_rows(level_quarters(ordered, table_ref))
         store_rows(rows, field_ref, level - 1, lat_dev, near_ref)
         copy = pltpu.make_async_copy(
             field_ref.at[pl.ds(level - 1, 1)], field_hbm.at[pl.ds(level, 1)], sems.at[level]
@@ -545,8 +607,8 @@
         (pair_low, spectral, legendre, tables), pair_local, wave_size
     )
     received = [swap(part, 2 * step) if step else part for step, part in enumerate(parts)]
-    select, *plans, vertical = plan(
-        parts[0],
+    select, turned, turn, *plans, vertical = plan(
+        tables,
         pair_low,
         dep_lat,
         dep_col,
@@ -565,31 +627,30 @@
     pieces = [swap(piece, 1) for piece in received]
     vmem = pl.BlockSpec(memory_space=pltpu.VMEM)
     params = pltpu.CompilerParams(vmem_limit_bytes=24 * MIB)
-    early = pl.pallas_call(
-        functools.partial(early_kernel, lat_dev),
-        in_specs=[vmem] * (len(received) + 1),
-        out_specs=vmem,
-        out_shape=jax.ShapeDtypeStruct(
-            (level_count, 8 * ext_pad, wavenumber_count), jnp.float32
-        ),
+    quarter_pieces = 4 * pl.cdiv(lon_count // 4, LANES)
+    quarters, early = pl.pallas_call(
+        functools.partial(early_kernel, lat_dev, len(received)),
+        in_specs=[vmem] * (len(received) + 2),
+        out_specs=[vmem] * 2,
+        out_shape=[
+            jax.ShapeDtypeStruct((quarter_pieces, 2 * ext_pad, LANES), jnp.float32),
+            jax.ShapeDtypeStruct(
+                (level_count - 1, 8 * ext_pad, wavenumber_count), jnp.float32
+            ),
+        ],
         compiler_params=params,
         cost_estimate=pl.CostEstimate(
             flops=10**8, bytes_accessed=2 * 10**6, transcendentals=0
         ),
         name="early",
-    )(*received, select)
-    operands = (
-        *pieces,
-        early,
-        select,
-        tables,
-        *plans,
-    )
+    )(*received, select, tables)
+    first_operands = (*pieces, quarters, turned, turn, *plans)
+    operands = (*pieces, early, select, tables, *plans)
     near = pltpu.VMEM((3, 2 * ext_pad * blocks, LANES), jnp.float32)
     flat = jax.ShapeDtypeStruct((points, LANES), jnp.float32)
     field_first, horizontal = pl.pallas_call(
         functools.partial(first_kernel, lat_dev, len(pieces)),
-        in_specs=[vmem] * len(operands),
+        in_specs=[vmem] * len(first_operands),
         out_specs=[vmem] * 2,
         out_shape=[jax.ShapeDtypeStruct((1, 2 * lat_dev, lon_count), jnp.float32), flat],
         scratch_shapes=[near],
@@ -598,7 +659,7 @@
             flops=10**8, bytes_accessed=4 * 10**6, transcendentals=0
         ),
         name="first_level",
-    )(*operands)
+    )(*first_operands)
     above = [trade(horizontal, color) for color in range(COLORS)]
     levels = jax.ShapeDtypeStruct((level_count, 2 * lat_dev, lon_count), jnp.float32)
     grid_field, departed, top = pl.pallas_call(

time: 18.5 us -> 18.3 us (0.989)
  waiting for transfers between devices: 3.05 us -> 1.34 us
  Pallas kernels: 6.72 us -> 7.99 us
    ppermute x7, waiting for transfers between devices: 2.91 us -> 1.21 us  [swap(): return lax.ppermute(value, 'wave', [(i, i ^ by) for i in range(wave_size)])]
    pallas_call x1, Pallas kernels: 1.07 us -> 2.25 us  [plan(): pl.pallas_call(functools.partial(plan_kernel, pair_local, lat_dev), in_sp...]
    pallas_call x1, Pallas kernels: 0.54 us -> 0.89 us  [per_device(): pl.pallas_call(functools.partial(early_kernel, lat_dev, len(received)), i...]
    pallas_call x1, Pallas kernels: 1.08 us -> 0.82 us  [per_device(): pl.pallas_call(functools.partial(first_kernel, lat_dev, len(pieces)), in_...]
  transfers between devices with their start and end apart: 10 -> 10, of which waited for: 6 -> 4; matrix products, arithmetic and copies ran while one was open for 0% -> 0% of each run, Pallas kernels for 17% -> 26%
where the time goes in v7:
time: 18.3 us; the launch traced here: 18.1 us
  Pallas kernels  7.99 us (44%)
  starting transfers between devices  7.34 us (40%)
  waiting for transfers between devices  1.34 us (7%)
  between operations  0.72 us (4%)
  other arithmetic  0.63 us (3%)
    ppermute x7, starting transfers between devices, swap(): return lax.ppermute(value, 'wave', [(i, i ^ by) for i in range(wave_size)])  5.19 us
    pallas_call x1, Pallas kernels, legendre_sums(): pl.pallas_call(functools.partial(legendre_kernel, pair_local, lat_dev), i...  2.47 us
    pallas_call x1, Pallas kernels, plan(): pl.pallas_call(functools.partial(plan_kernel, pair_local, lat_dev), in_sp...  2.25 us
    ppermute x3, starting transfers between devices, trade(): return lax.ppermute(value, ('lev', 'wave'), pairs)  2.15 us
    pallas_call x1, Pallas kernels, per_device(): pl.pallas_call(functools.partial(later_kernel, lat_dev, len(pieces)), in_...  1.54 us
    ppermute x7, waiting for transfers between devices, swap(): return lax.ppermute(value, 'wave', [(i, i ^ by) for i in range(wave_size)])  1.21 us
    pallas_call x1, Pallas kernels, per_device(): pl.pallas_call(functools.partial(early_kernel, lat_dev, len(received)), i...  0.89 us
    pallas_call x1, Pallas kernels, per_device(): pl.pallas_call(functools.partial(first_kernel, lat_dev, len(pieces)), in_...  0.82 us
  transfers between devices with their start and end apart: 10, of which 4 were waited for; matrix products, arithmetic and copies ran while one was open for 0% of the time, Pallas kernels for 26%

profile of v7, /device:TPU:0, one launch (start us, length us, event | category | flops | bytes accessed | tf_op | source)
XLA Modules:
  0.0 18.1 jit_solution(12648702765411655330)
XLA Ops:
  0.6 2.5 %legendre.1 = (f32[2,32,128]{2,1,0:T(8,128)S(1)}, f32[2,32,128]{2,1,0:T(8,128)S(1)}, f32[2,32,128]{2,1,0:T(8,128)S(1)}, f32[2,32,128]{2,1,0:T(8,128)S(1)}, bf16[2,640,640]{2,1,0:T(8,128)(2,1)S(1)}) custom-call(s32[320]{0:T(512)} %refs_0_.3, f32[40,2,2,641]{3,2,1,0:T(2,128)} %refs_1_.2, f32[40,16,641]{2,1,0:T(8,128)} %refs_2_.2, ...), custom_call_target="tpu_custom_call" | custom-call | tf_op jit(solution)/shard_map/legendre/pallas_call | solution.py:178
  3.1 4.0 %collective-permute-start.1 = (f32[2,32,128]{2,1,0:T(8,128)S(1)}, f32[2,32,128]{2,1,0:T(8,128)S(1)}, u32[]{:S(2)}, u32[]{:S(2)}) collective-permute-start(f32[2,32,128]{2,1,0:T(8,128)S(1)} %get-tuple-element.25), channel_id=1, source_target_pairs={{0,6},{1,7},{2,4},{3,5},{4,2},{5,3},{6,0},{7,1},{8,14},{9,15},{10,... | collective-permute-start | bytes 98312 | tf_op jit(solution)/shard_map/ppermute | solution.py:204
  7.1 0.5 %collective-permute-start.3 = (f32[2,32,128]{2,1,0:T(8,128)S(1)}, f32[2,32,128]{2,1,0:T(8,128)S(1)}, u32[]{:S(2)}, u32[]{:S(2)}) collective-permute-start(f32[2,32,128]{2,1,0:T(8,128)S(1)} %get-tuple-element.29), channel_id=1, source_target_pairs={{0,4},{1,5},{2,6},{3,7},{4,0},{5,1},{6,2},{7,3},{8,12},{9,13},{10,... | collective-permute-start | bytes 98312 | tf_op jit(solution)/shard_map/ppermute | solution.py:204
  7.6 0.1 collective-permute-start.5
  7.7 0.0 collective-permute-start
  7.7 2.3 %plan.1 = (bf16[768,640]{1,0:T(8,128)(2,1)S(1)}, bf16[768,640]{1,0:T(8,128)(2,1)S(1)}, f32[16,384]{1,0:T(8,128)S(1)}, s32[40,128]{1,0:T(8,128)S(1)}, s32[40,128]...) custom-call(bf16[2,640,640]{2,1,0:T(8,128)(2,1)S(1)} %get-tuple-element.26.table_ref.refs_5_., ...), custom_call_target="tpu_custom_call" | custom-call | flops 10000000 | bytes 4000000 | tf_op jit(solution)/shard_map/plan/pallas_call | solution.py:282
  10.0 0.0 collective-permute-done.1.refs_1_
  10.0 0.6 %collective-permute-start.2 = (f32[2,32,128]{2,1,0:T(8,128)S(1)}, f32[2,32,128]{2,1,0:T(8,128)S(1)}, u32[]{:S(2)}, u32[]{:S(2)}) collective-permute-start(f32[2,32,128]{2,1,0:T(8,128)S(1)} %collective-permute-done.1.refs_1_), channel_id=1, source_target_pairs={{0,1},{1,0},{2,3},{3,2},{4,5},{5,4},{6,7},{7,6},{8,9},{9,8},{10,11... | collective-permute-start | bytes 98312 | tf_op jit(solution)/shard_map/ppermute | solution.py:204
  10.6 0.4 %collective-permute-done.3.refs_2_ = f32[2,32,128]{2,1,0:T(8,128)S(1)} collective-permute-done((f32[2,32,128]{2,1,0:T(8,128)S(1)}, f32[2,32,128]{2,1,0:T(8,128)S(1)}, u32[]{:S(2)}, u32[]{:S(2)}) %collective-permute-start.3) | collective-permute-done | bytes 32800 | tf_op jit(solution)/shard_map/ppermute | solution.py:204
  11.0 0.0 collective-permute-start.4
  11.0 0.5 %collective-permute-done.5.refs_3_ = f32[2,32,128]{2,1,0:T(8,128)S(1)} collective-permute-done((f32[2,32,128]{2,1,0:T(8,128)S(1)}, f32[2,32,128]{2,1,0:T(8,128)S(1)}, u32[]{:S(2)}, u32[]{:S(2)}) %collective-permute-start.5) | collective-permute-done | bytes 32800 | tf_op jit(solution)/shard_map/ppermute | solution.py:204
  11.5 0.0 collective-permute-start.6
  11.5 0.9 %early.1 = (f32[12,16,128]{2,1,0:T(8,128)S(1)}, f32[1,64,640]{2,1,0:T(8,128)S(1)}) custom-call(f32[2,32,128]{2,1,0:T(8,128)S(1)} %get-tuple-element.24.refs_0_, f32[2,32,128]{2,1,0:T(8,128)S(1)} %collective-permute-done.1.refs_1_, f32[2,32,128]{2,1,0:T(8,128)S(1)} %collective-permute-done.3.refs_2_, f32[2,32,128]{2,1,0:T(8,128)S(1)} %collective-permute-done.5.refs_3_, ...), custom_call_target="tpu_custom_call" | custom-call | flops 100000000 | bytes 2000000 | tf_op jit(solution)/shard_map/early/pallas_call | solution.py:631
  12.4 0.0 collective-permute-done.refs_0_
  12.4 0.0 collective-permute-done.2.refs_1_
  12.4 0.0 collective-permute-done.4.refs_2_
  12.4 0.3 %collective-permute-done.6.refs_3_ = f32[2,32,128]{2,1,0:T(8,128)S(1)} collective-permute-done((f32[2,32,128]{2,1,0:T(8,128)S(1)}, f32[2,32,128]{2,1,0:T(8,128)S(1)}, u32[]{:S(2)}, u32[]{:S(2)}) %collective-permute-start.6) | collective-permute-done | bytes 32800 | tf_op jit(solution)/shard_map/ppermute | solution.py:204
  12.7 0.8 %first_level.1 = (f32[1,4,1280]{2,1,0:T(4,128)S(1)}, f32[40,128]{1,0:T(8,128)S(1)}) custom-call(f32[2,32,128]{2,1,0:T(8,128)S(1)} %collective-permute-done.refs_0_, f32[2,32,128]{2,1,0:T(8,128)S(1)} %collective-permute-done.2.refs_1_, f32[2,32,128]{2,1,0:T(8,128)S(1)} %collective-permute-done.4.refs_2_, f32[2,32,128]{2,1,0:T(8,128)S(1)} %collective-permute-done.6.refs_3_, ...), custom_call_target="tpu_custom_call" | custom-call | flops 100000000 | bytes 4000000 | tf_op jit(solution)/shard_map/first_level/pallas_call | solution.py:651
  13.5 1.6 %collective-permute-start.7 = (f32[40,128]{1,0:T(8,128)S(1)}, f32[40,128]{1,0:T(8,128)S(1)}, u32[]{:S(2)}, u32[]{:S(2)}) collective-permute-start(f32[40,128]{1,0:T(8,128)S(1)} %get-tuple-element.41.refs_12_), channel_id=1, source_target_pairs={{0,8},{1,9},{2,10},{3,11},{4,12},{5,13},{6,14},{7,15},{8,0},{9,1},... | collective-permute-start | bytes 61448 | tf_op jit(solution)/shard_map/ppermute | solution.py:219
  15.2 0.0 collective-permute-start.8
  15.2 0.5 %collective-permute-start.9 = (f32[40,128]{1,0:T(8,128)S(1)}, f32[40,128]{1,0:T(8,128)S(1)}, u32[]{:S(2)}, u32[]{:S(2)}) collective-permute-start(f32[40,128]{1,0:T(8,128)S(1)} %get-tuple-element.41.refs_12_), channel_id=1, source_target_pairs={{0,1},{1,0},{2,3},{3,2},{4,5},{5,4},{6,7},{7,6},{8,9},{9,8},{10,11... | collective-permute-start | bytes 61448 | tf_op jit(solution)/shard_map/ppermute | solution.py:219
  15.7 1.5 %later_levels.1 = (f32[2,4,1280]{2,1,0:T(4,128)}, f32[1,40,128]{2,1,0:T(8,128)S(1)}, f32[40,128]{1,0:T(8,128)S(1)}) custom-call(f32[2,32,128]{2,1,0:T(8,128)S(1)} %collective-permute-done.refs_0_, f32[2,32,128]{2,1,0:T(8,128)S(1)} %collective-permute-done.2.refs_1_, f32[2,32,128]{2,1,0:T(8,128)S(1)} %collective-permute-done.4.refs_2_, ...), custom_call_target="tpu_custom_call" | custom-call | flops 100000000 | bytes 4000000 | tf_op jit(solution)/shard_map/later_levels/pallas_call | solution.py:665
  17.2 0.1 collective-permute-done.7.refs_0_
  17.4 0.0 collective-permute-done.8.refs_1_
  17.4 0.0 collective-permute-done.9.refs_2_
  17.4 0.6 %pad_maximum_fusion = f32[2,4,1280]{2,1,0:T(4,128)} fusion(f32[1,4,1280]{2,1,0:T(4,128)S(1)} %concatenate.9, f32[1,4,1280]{2,1,0:T(4,128)S(1)} %concatenate.8), kind=kLoop, calls=%fused_computation | loop fusion | flops 10240 | bytes 81920 | tf_op jit(solution)/shard_map/concatenate | solution.py:693
  (3 shorter events, 0.1 us)
Async XLA Ops:
  3.1 6.9 %collective-permute-start.1 = (f32[2,32,128]{2,1,0:T(8,128)S(1)}, f32[2,32,128]{2,1,0:T(8,128)S(1)}, u32[]{:S(2)}, u32[]{:S(2)}) collective-permute-start(f32[2,32,128]{2,1,0:T(8,128)S(1)} %get-tuple-element.25), channel_id=1, source_target_pairs={{0,6},{1,7},{2,4},{3,5},{4,2},{5,3},{6,0},{7,1},{8,14},{9,15},{10,... | collective-permute-start | bytes 98312 | tf_op jit(solution)/shard_map/ppermute | solution.py:204
  7.1 3.9 %collective-permute-start.3 = (f32[2,32,128]{2,1,0:T(8,128)S(1)}, f32[2,32,128]{2,1,0:T(8,128)S(1)}, u32[]{:S(2)}, u32[]{:S(2)}) collective-permute-start(f32[2,32,128]{2,1,0:T(8,128)S(1)} %get-tuple-element.29), channel_id=1, source_target_pairs={{0,4},{1,5},{2,6},{3,7},{4,0},{5,1},{6,2},{7,3},{8,12},{9,13},{10,... | collective-permute-start | bytes 98312 | tf_op jit(solution)/shard_map/ppermute | solution.py:204
  7.6 3.9 %collective-permute-start.5 = (f32[2,32,128]{2,1,0:T(8,128)S(1)}, f32[2,32,128]{2,1,0:T(8,128)S(1)}, u32[]{:S(2)}, u32[]{:S(2)}) collective-permute-start(f32[2,32,128]{2,1,0:T(8,128)S(1)} %get-tuple-element.30), channel_id=1, source_target_pairs={{0,2},{1,3},{2,0},{3,1},{4,6},{5,7},{6,4},{7,5},{8,10},{9,11},{10,... | collective-permute-start | bytes 98312 | tf_op jit(solution)/shard_map/ppermute | solution.py:204
  7.7 4.7 %collective-permute-start = (f32[2,32,128]{2,1,0:T(8,128)S(1)}, f32[2,32,128]{2,1,0:T(8,128)S(1)}, u32[]{:S(2)}, u32[]{:S(2)}) collective-permute-start(f32[2,32,128]{2,1,0:T(8,128)S(1)} %get-tuple-element.24.refs_0_), channel_id=1, source_target_pairs={{0,1},{1,0},{2,3},{3,2},{4,5},{5,4},{6,7},{7,6},{8,9},{9,8},{10,11... | collective-permute-start | bytes 98312 | tf_op jit(solution)/shard_map/ppermute | solution.py:204
  10.0 2.4 %collective-permute-start.2 = (f32[2,32,128]{2,1,0:T(8,128)S(1)}, f32[2,32,128]{2,1,0:T(8,128)S(1)}, u32[]{:S(2)}, u32[]{:S(2)}) collective-permute-start(f32[2,32,128]{2,1,0:T(8,128)S(1)} %collective-permute-done.1.refs_1_), channel_id=1, source_target_pairs={{0,1},{1,0},{2,3},{3,2},{4,5},{5,4},{6,7},{7,6},{8,9},{9,8},{10,11... | collective-permute-start | bytes 98312 | tf_op jit(solution)/shard_map/ppermute | solution.py:204
  11.0 1.4 %collective-permute-start.4 = (f32[2,32,128]{2,1,0:T(8,128)S(1)}, f32[2,32,128]{2,1,0:T(8,128)S(1)}, u32[]{:S(2)}, u32[]{:S(2)}) collective-permute-start(f32[2,32,128]{2,1,0:T(8,128)S(1)} %collective-permute-done.3.refs_2_), channel_id=1, source_target_pairs={{0,1},{1,0},{2,3},{3,2},{4,5},{5,4},{6,7},{7,6},{8,9},{9,8},{10,11... | collective-permute-start | bytes 98312 | tf_op jit(solution)/shard_map/ppermute | solution.py:204
  11.5 1.2 %collective-permute-start.6 = (f32[2,32,128]{2,1,0:T(8,128)S(1)}, f32[2,32,128]{2,1,0:T(8,128)S(1)}, u32[]{:S(2)}, u32[]{:S(2)}) collective-permute-start(f32[2,32,128]{2,1,0:T(8,128)S(1)} %collective-permute-done.5.refs_3_), channel_id=1, source_target_pairs={{0,1},{1,0},{2,3},{3,2},{4,5},{5,4},{6,7},{7,6},{8,9},{9,8},{10,11... | collective-permute-start | bytes 98312 | tf_op jit(solution)/shard_map/ppermute | solution.py:204
  13.5 3.8 %collective-permute-start.7 = (f32[40,128]{1,0:T(8,128)S(1)}, f32[40,128]{1,0:T(8,128)S(1)}, u32[]{:S(2)}, u32[]{:S(2)}) collective-permute-start(f32[40,128]{1,0:T(8,128)S(1)} %get-tuple-element.41.refs_12_), channel_id=1, source_target_pairs={{0,8},{1,9},{2,10},{3,11},{4,12},{5,13},{6,14},{7,15},{8,0},{9,1},... | collective-permute-start | bytes 61448 | tf_op jit(solution)/shard_map/ppermute | solution.py:219
  15.2 2.2 %collective-permute-start.8 = (f32[40,128]{1,0:T(8,128)S(1)}, f32[40,128]{1,0:T(8,128)S(1)}, u32[]{:S(2)}, u32[]{:S(2)}) collective-permute-start(f32[40,128]{1,0:T(8,128)S(1)} %get-tuple-element.41.refs_12_), channel_id=1, source_target_pairs={{0,1},{1,0},{2,3},{3,2},{4,5},{5,4},{6,7},{7,6},{8,16},{9,17},{10,... | collective-permute-start | bytes 61448 | tf_op jit(solution)/shard_map/ppermute | solution.py:219
  15.2 2.2 %collective-permute-start.9 = (f32[40,128]{1,0:T(8,128)S(1)}, f32[40,128]{1,0:T(8,128)S(1)}, u32[]{:S(2)}, u32[]{:S(2)}) collective-permute-start(f32[40,128]{1,0:T(8,128)S(1)} %get-tuple-element.41.refs_12_), channel_id=1, source_target_pairs={{0,1},{1,0},{2,3},{3,2},{4,5},{5,4},{6,7},{7,6},{8,9},{9,8},{10,11... | collective-permute-start | bytes 61448 | tf_op jit(solution)/shard_map/ppermute | solution.py:219

commit v8 on v7

--- a/solution.py
+++ b/solution.py
@@ -252,6 +252,8 @@
     turns = jnp.where((row == 0) == (kind < 2), sign, 0.0)
     turns = jnp.where(row < 2, turns, 0.0).astype(jnp.bfloat16)
     lanes = select_ref.shape[0] // 2
+    groups = pl.cdiv(pair_local, GROUP)
+    used = low_ref.shape[0] // pair_local // 2 * groups * 2 * GROUP
     late = select_ref[lanes:]
     turn_ref[...] = lax.dot_general(turns, late, NT, preferred_element_type=jnp.float32)
     even, odd = table_ref[0], table_ref[1]
@@ -260,9 +262,13 @@
         jnp.concatenate([even[half // 2 :], odd[: half // 2]], axis=0),
     )
     for part, table in enumerate(both):
-        turned_ref[part * lanes : (part + 1) * lanes] = lax.dot_general(
-            late, table, NN, preferred_element_type=jnp.float32
+        turned_ref[part * lanes : part * lanes + used] = lax.dot_general(
+            late[:used], table, NN, preferred_element_type=jnp.float32
         ).astype(jnp.bfloat16)
+        if used < lanes:
+            turned_ref[part * lanes + used : (part + 1) * lanes] = jnp.zeros(
+                (lanes - used, table.shape[1]), jnp.bfloat16
+            )
 
 
 def plan(tables, pair_low, dep_lat, dep_col, lon_steps, tilt_steps, pair_local, lat_dev, slots, half):

time: 18.3 us -> 18.3 us (level)
  transfers between devices with their start and end apart: 10 -> 10, of which waited for: 4 -> 4; matrix products, arithmetic and copies ran while one was open for 0% -> 0% of each run, Pallas kernels for 26% -> 25%
where the time goes in v8:
time: 18.3 us; the launch traced here: 18.1 us
  Pallas kernels  7.84 us (43%)
  starting transfers between devices  7.34 us (40%)
  waiting for transfers between devices  1.49 us (8%)
  between operations  0.72 us (4%)
  other arithmetic  0.63 us (3%)
    ppermute x7, starting transfers between devices, swap(): return lax.ppermute(value, 'wave', [(i, i ^ by) for i in range(wave_size)])  5.19 us
    pallas_call x1, Pallas kernels, legendre_sums(): pl.pallas_call(functools.partial(legendre_kernel, pair_local, lat_dev), i...  2.47 us
    ppermute x3, starting transfers between devices, trade(): return lax.ppermute(value, ('lev', 'wave'), pairs)  2.15 us
    pallas_call x1, Pallas kernels, plan(): pl.pallas_call(functools.partial(plan_kernel, pair_local, lat_dev), in_sp...  2.1 us
    pallas_call x1, Pallas kernels, per_device(): pl.pallas_call(functools.partial(later_kernel, lat_dev, len(pieces)), in_...  1.54 us
    ppermute x7, waiting for transfers between devices, swap(): return lax.ppermute(value, 'wave', [(i, i ^ by) for i in range(wave_size)])  1.36 us
    pallas_call x1, Pallas kernels, per_device(): pl.pallas_call(functools.partial(early_kernel, lat_dev, len(received)), i...  0.89 us
    pallas_call x1, Pallas kernels, per_device(): pl.pallas_call(functools.partial(first_kernel, lat_dev, len(pieces)), in_...  0.82 us
  transfers between devices with their start and end apart: 10, of which 4 were waited for; matrix products, arithmetic and copies ran while one was open for 0% of the time, Pallas kernels for 25%

profile of v8, /device:TPU:0, one launch (start us, length us, event | category | flops | bytes accessed | tf_op | source)
XLA Modules:
  0.0 18.1 jit_solution(12635191593328180128)
XLA Ops:
  0.6 2.5 %legendre.1 = (f32[2,32,128]{2,1,0:T(8,128)S(1)}, f32[2,32,128]{2,1,0:T(8,128)S(1)}, f32[2,32,128]{2,1,0:T(8,128)S(1)}, f32[2,32,128]{2,1,0:T(8,128)S(1)}, bf16[2,640,640]{2,1,0:T(8,128)(2,1)S(1)}) custom-call(s32[320]{0:T(512)} %refs_0_.3, f32[40,2,2,641]{3,2,1,0:T(2,128)} %refs_1_.2, f32[40,16,641]{2,1,0:T(8,128)} %refs_2_.2, ...), custom_call_target="tpu_custom_call" | custom-call | tf_op jit(solution)/shard_map/legendre/pallas_call | solution.py:178
  3.1 4.0 %collective-permute-start.1 = (f32[2,32,128]{2,1,0:T(8,128)S(1)}, f32[2,32,128]{2,1,0:T(8,128)S(1)}, u32[]{:S(2)}, u32[]{:S(2)}) collective-permute-start(f32[2,32,128]{2,1,0:T(8,128)S(1)} %get-tuple-element.25), channel_id=1, source_target_pairs={{0,6},{1,7},{2,4},{3,5},{4,2},{5,3},{6,0},{7,1},{8,14},{9,15},{10,... | collective-permute-start | bytes 98312 | tf_op jit(solution)/shard_map/ppermute | solution.py:204
  7.1 0.5 %collective-permute-start.3 = (f32[2,32,128]{2,1,0:T(8,128)S(1)}, f32[2,32,128]{2,1,0:T(8,128)S(1)}, u32[]{:S(2)}, u32[]{:S(2)}) collective-permute-start(f32[2,32,128]{2,1,0:T(8,128)S(1)} %get-tuple-element.29), channel_id=1, source_target_pairs={{0,4},{1,5},{2,6},{3,7},{4,0},{5,1},{6,2},{7,3},{8,12},{9,13},{10,... | collective-permute-start | bytes 98312 | tf_op jit(solution)/shard_map/ppermute | solution.py:204
  7.6 0.1 collective-permute-start.5
  7.7 0.0 collective-permute-start
  7.7 2.1 %plan.1 = (bf16[768,640]{1,0:T(8,128)(2,1)S(1)}, bf16[768,640]{1,0:T(8,128)(2,1)S(1)}, f32[16,384]{1,0:T(8,128)S(1)}, s32[40,128]{1,0:T(8,128)S(1)}, s32[40,128]...) custom-call(bf16[2,640,640]{2,1,0:T(8,128)(2,1)S(1)} %get-tuple-element.26.table_ref.refs_5_., ...), custom_call_target="tpu_custom_call" | custom-call | flops 10000000 | bytes 4000000 | tf_op jit(solution)/shard_map/plan/pallas_call | solution.py:288
  9.8 0.0 collective-permute-done.1.refs_1_
  9.8 0.6 %collective-permute-start.2 = (f32[2,32,128]{2,1,0:T(8,128)S(1)}, f32[2,32,128]{2,1,0:T(8,128)S(1)}, u32[]{:S(2)}, u32[]{:S(2)}) collective-permute-start(f32[2,32,128]{2,1,0:T(8,128)S(1)} %collective-permute-done.1.refs_1_), channel_id=1, source_target_pairs={{0,1},{1,0},{2,3},{3,2},{4,5},{5,4},{6,7},{7,6},{8,9},{9,8},{10,11... | collective-permute-start | bytes 98312 | tf_op jit(solution)/shard_map/ppermute | solution.py:204
  10.4 0.6 %collective-permute-done.3.refs_2_ = f32[2,32,128]{2,1,0:T(8,128)S(1)} collective-permute-done((f32[2,32,128]{2,1,0:T(8,128)S(1)}, f32[2,32,128]{2,1,0:T(8,128)S(1)}, u32[]{:S(2)}, u32[]{:S(2)}) %collective-permute-start.3) | collective-permute-done | bytes 32800 | tf_op jit(solution)/shard_map/ppermute | solution.py:204
  11.0 0.0 collective-permute-start.4
  11.0 0.5 %collective-permute-done.5.refs_3_ = f32[2,32,128]{2,1,0:T(8,128)S(1)} collective-permute-done((f32[2,32,128]{2,1,0:T(8,128)S(1)}, f32[2,32,128]{2,1,0:T(8,128)S(1)}, u32[]{:S(2)}, u32[]{:S(2)}) %collective-permute-start.5) | collective-permute-done | bytes 32800 | tf_op jit(solution)/shard_map/ppermute | solution.py:204
  11.5 0.0 collective-permute-start.6
  11.5 0.9 %early.1 = (f32[12,16,128]{2,1,0:T(8,128)S(1)}, f32[1,64,640]{2,1,0:T(8,128)S(1)}) custom-call(f32[2,32,128]{2,1,0:T(8,128)S(1)} %get-tuple-element.24.refs_0_, f32[2,32,128]{2,1,0:T(8,128)S(1)} %collective-permute-done.1.refs_1_, f32[2,32,128]{2,1,0:T(8,128)S(1)} %collective-permute-done.3.refs_2_, f32[2,32,128]{2,1,0:T(8,128)S(1)} %collective-permute-done.5.refs_3_, ...), custom_call_target="tpu_custom_call" | custom-call | flops 100000000 | bytes 2000000 | tf_op jit(solution)/shard_map/early/pallas_call | solution.py:637
  12.4 0.0 collective-permute-done.refs_0_
  12.4 0.0 collective-permute-done.2.refs_1_
  12.4 0.0 collective-permute-done.4.refs_2_
  12.4 0.3 %collective-permute-done.6.refs_3_ = f32[2,32,128]{2,1,0:T(8,128)S(1)} collective-permute-done((f32[2,32,128]{2,1,0:T(8,128)S(1)}, f32[2,32,128]{2,1,0:T(8,128)S(1)}, u32[]{:S(2)}, u32[]{:S(2)}) %collective-permute-start.6) | collective-permute-done | bytes 32800 | tf_op jit(solution)/shard_map/ppermute | solution.py:204
  12.7 0.8 %first_level.1 = (f32[1,4,1280]{2,1,0:T(4,128)S(1)}, f32[40,128]{1,0:T(8,128)S(1)}) custom-call(f32[2,32,128]{2,1,0:T(8,128)S(1)} %collective-permute-done.refs_0_, f32[2,32,128]{2,1,0:T(8,128)S(1)} %collective-permute-done.2.refs_1_, f32[2,32,128]{2,1,0:T(8,128)S(1)} %collective-permute-done.4.refs_2_, f32[2,32,128]{2,1,0:T(8,128)S(1)} %collective-permute-done.6.refs_3_, ...), custom_call_target="tpu_custom_call" | custom-call | flops 100000000 | bytes 4000000 | tf_op jit(solution)/shard_map/first_level/pallas_call | solution.py:657
  13.5 1.6 %collective-permute-start.7 = (f32[40,128]{1,0:T(8,128)S(1)}, f32[40,128]{1,0:T(8,128)S(1)}, u32[]{:S(2)}, u32[]{:S(2)}) collective-permute-start(f32[40,128]{1,0:T(8,128)S(1)} %get-tuple-element.41.refs_12_), channel_id=1, source_target_pairs={{0,8},{1,9},{2,10},{3,11},{4,12},{5,13},{6,14},{7,15},{8,0},{9,1},... | collective-permute-start | bytes 61448 | tf_op jit(solution)/shard_map/ppermute | solution.py:219
  15.2 0.0 collective-permute-start.8
  15.2 0.5 %collective-permute-start.9 = (f32[40,128]{1,0:T(8,128)S(1)}, f32[40,128]{1,0:T(8,128)S(1)}, u32[]{:S(2)}, u32[]{:S(2)}) collective-permute-start(f32[40,128]{1,0:T(8,128)S(1)} %get-tuple-element.41.refs_12_), channel_id=1, source_target_pairs={{0,1},{1,0},{2,3},{3,2},{4,5},{5,4},{6,7},{7,6},{8,9},{9,8},{10,11... | collective-permute-start | bytes 61448 | tf_op jit(solution)/shard_map/ppermute | solution.py:219
  15.7 1.5 %later_levels.1 = (f32[2,4,1280]{2,1,0:T(4,128)}, f32[1,40,128]{2,1,0:T(8,128)S(1)}, f32[40,128]{1,0:T(8,128)S(1)}) custom-call(f32[2,32,128]{2,1,0:T(8,128)S(1)} %collective-permute-done.refs_0_, f32[2,32,128]{2,1,0:T(8,128)S(1)} %collective-permute-done.2.refs_1_, f32[2,32,128]{2,1,0:T(8,128)S(1)} %collective-permute-done.4.refs_2_, ...), custom_call_target="tpu_custom_call" | custom-call | flops 100000000 | bytes 4000000 | tf_op jit(solution)/shard_map/later_levels/pallas_call | solution.py:671
  17.2 0.1 collective-permute-done.7.refs_0_
  17.4 0.0 collective-permute-done.8.refs_1_
  17.4 0.0 collective-permute-done.9.refs_2_
  17.4 0.6 %pad_maximum_fusion = f32[2,4,1280]{2,1,0:T(4,128)} fusion(f32[1,4,1280]{2,1,0:T(4,128)S(1)} %concatenate.9, f32[1,4,1280]{2,1,0:T(4,128)S(1)} %concatenate.8), kind=kLoop, calls=%fused_computation | loop fusion | flops 10240 | bytes 81920 | tf_op jit(solution)/shard_map/concatenate | solution.py:699
  (3 shorter events, 0.1 us)
Async XLA Ops:
  3.1 6.7 %collective-permute-start.1 = (f32[2,32,128]{2,1,0:T(8,128)S(1)}, f32[2,32,128]{2,1,0:T(8,128)S(1)}, u32[]{:S(2)}, u32[]{:S(2)}) collective-permute-start(f32[2,32,128]{2,1,0:T(8,128)S(1)} %get-tuple-element.25), channel_id=1, source_target_pairs={{0,6},{1,7},{2,4},{3,5},{4,2},{5,3},{6,0},{7,1},{8,14},{9,15},{10,... | collective-permute-start | bytes 98312 | tf_op jit(solution)/shard_map/ppermute | solution.py:204
  7.1 3.9 %collective-permute-start.3 = (f32[2,32,128]{2,1,0:T(8,128)S(1)}, f32[2,32,128]{2,1,0:T(8,128)S(1)}, u32[]{:S(2)}, u32[]{:S(2)}) collective-permute-start(f32[2,32,128]{2,1,0:T(8,128)S(1)} %get-tuple-element.29), channel_id=1, source_target_pairs={{0,4},{1,5},{2,6},{3,7},{4,0},{5,1},{6,2},{7,3},{8,12},{9,13},{10,... | collective-permute-start | bytes 98312 | tf_op jit(solution)/shard_map/ppermute | solution.py:204
  7.6 3.9 %collective-permute-start.5 = (f32[2,32,128]{2,1,0:T(8,128)S(1)}, f32[2,32,128]{2,1,0:T(8,128)S(1)}, u32[]{:S(2)}, u32[]{:S(2)}) collective-permute-start(f32[2,32,128]{2,1,0:T(8,128)S(1)} %get-tuple-element.30), channel_id=1, source_target_pairs={{0,2},{1,3},{2,0},{3,1},{4,6},{5,7},{6,4},{7,5},{8,10},{9,11},{10,... | collective-permute-start | bytes 98312 | tf_op jit(solution)/shard_map/ppermute | solution.py:204
  7.7 4.7 %collective-permute-start = (f32[2,32,128]{2,1,0:T(8,128)S(1)}, f32[2,32,128]{2,1,0:T(8,128)S(1)}, u32[]{:S(2)}, u32[]{:S(2)}) collective-permute-start(f32[2,32,128]{2,1,0:T(8,128)S(1)} %get-tuple-element.24.refs_0_), channel_id=1, source_target_pairs={{0,1},{1,0},{2,3},{3,2},{4,5},{5,4},{6,7},{7,6},{8,9},{9,8},{10,11... | collective-permute-start | bytes 98312 | tf_op jit(solution)/shard_map/ppermute | solution.py:204
  9.8 2.6 %collective-permute-start.2 = (f32[2,32,128]{2,1,0:T(8,128)S(1)}, f32[2,32,128]{2,1,0:T(8,128)S(1)}, u32[]{:S(2)}, u32[]{:S(2)}) collective-permute-start(f32[2,32,128]{2,1,0:T(8,128)S(1)} %collective-permute-done.1.refs_1_), channel_id=1, source_target_pairs={{0,1},{1,0},{2,3},{3,2},{4,5},{5,4},{6,7},{7,6},{8,9},{9,8},{10,11... | collective-permute-start | bytes 98312 | tf_op jit(solution)/shard_map/ppermute | solution.py:204
  11.0 1.4 %collective-permute-start.4 = (f32[2,32,128]{2,1,0:T(8,128)S(1)}, f32[2,32,128]{2,1,0:T(8,128)S(1)}, u32[]{:S(2)}, u32[]{:S(2)}) collective-permute-start(f32[2,32,128]{2,1,0:T(8,128)S(1)} %collective-permute-done.3.refs_2_), channel_id=1, source_target_pairs={{0,1},{1,0},{2,3},{3,2},{4,5},{5,4},{6,7},{7,6},{8,9},{9,8},{10,11... | collective-permute-start | bytes 98312 | tf_op jit(solution)/shard_map/ppermute | solution.py:204
  11.5 1.2 %collective-permute-start.6 = (f32[2,32,128]{2,1,0:T(8,128)S(1)}, f32[2,32,128]{2,1,0:T(8,128)S(1)}, u32[]{:S(2)}, u32[]{:S(2)}) collective-permute-start(f32[2,32,128]{2,1,0:T(8,128)S(1)} %collective-permute-done.5.refs_3_), channel_id=1, source_target_pairs={{0,1},{1,0},{2,3},{3,2},{4,5},{5,4},{6,7},{7,6},{8,9},{9,8},{10,11... | collective-permute-start | bytes 98312 | tf_op jit(solution)/shard_map/ppermute | solution.py:204
  13.5 3.8 %collective-permute-start.7 = (f32[40,128]{1,0:T(8,128)S(1)}, f32[40,128]{1,0:T(8,128)S(1)}, u32[]{:S(2)}, u32[]{:S(2)}) collective-permute-start(f32[40,128]{1,0:T(8,128)S(1)} %get-tuple-element.41.refs_12_), channel_id=1, source_target_pairs={{0,8},{1,9},{2,10},{3,11},{4,12},{5,13},{6,14},{7,15},{8,0},{9,1},... | collective-permute-start | bytes 61448 | tf_op jit(solution)/shard_map/ppermute | solution.py:219
  15.2 2.2 %collective-permute-start.8 = (f32[40,128]{1,0:T(8,128)S(1)}, f32[40,128]{1,0:T(8,128)S(1)}, u32[]{:S(2)}, u32[]{:S(2)}) collective-permute-start(f32[40,128]{1,0:T(8,128)S(1)} %get-tuple-element.41.refs_12_), channel_id=1, source_target_pairs={{0,1},{1,0},{2,3},{3,2},{4,5},{5,4},{6,7},{7,6},{8,16},{9,17},{10,... | collective-permute-start | bytes 61448 | tf_op jit(solution)/shard_map/ppermute | solution.py:219
  15.2 2.2 %collective-permute-start.9 = (f32[40,128]{1,0:T(8,128)S(1)}, f32[40,128]{1,0:T(8,128)S(1)}, u32[]{:S(2)}, u32[]{:S(2)}) collective-permute-start(f32[40,128]{1,0:T(8,128)S(1)} %get-tuple-element.41.refs_12_), channel_id=1, source_target_pairs={{0,1},{1,0},{2,3},{3,2},{4,5},{5,4},{6,7},{7,6},{8,9},{9,8},{10,11... | collective-permute-start | bytes 61448 | tf_op jit(solution)/shard_map/ppermute | solution.py:219

commit v9 on v8

--- a/solution.py
+++ b/solution.py
@@ -99,8 +99,8 @@
     for index, (start, stop) in enumerate(zip(bounds[:-1], bounds[1:], strict=True)):
         part = pl.ds(start * GROUP, (stop - start) * GROUP)
         pair = (
+            pltpu.make_async_copy(leg_hbm.at[part], leg_ref.at[part], leg_sem.at[index]),
             pltpu.make_async_copy(spec_hbm.at[part], spec_ref.at[part], spec_sem.at[index]),
-            pltpu.make_async_copy(leg_hbm.at[part], leg_ref.at[part], leg_sem.at[index]),
         )
         for copy in pair:
             copy.start()

time: 18.3 us -> 18.2 us (level)
  no operation moved by 1% of the time
where the time goes in v9:
time: 18.2 us; the launch traced here: 18 us
  Pallas kernels  7.76 us (43%)
  starting transfers between devices  7.34 us (40%)
  waiting for transfers between devices  1.49 us (8%)
  between operations  0.72 us (4%)
  other arithmetic  0.63 us (3%)
    ppermute x7, starting transfers between devices, swap(): return lax.ppermute(value, 'wave', [(i, i ^ by) for i in range(wave_size)])  5.19 us
    pallas_call x1, Pallas kernels, legendre_sums(): pl.pallas_call(functools.partial(legendre_kernel, pair_local, lat_dev), i...  2.38 us
    ppermute x3, starting transfers between devices, trade(): return lax.ppermute(value, ('lev', 'wave'), pairs)  2.15 us
    pallas_call x1, Pallas kernels, plan(): pl.pallas_call(functools.partial(plan_kernel, pair_local, lat_dev), in_sp...  2.1 us
    pallas_call x1, Pallas kernels, per_device(): pl.pallas_call(functools.partial(later_kernel, lat_dev, len(pieces)), in_...  1.54 us
    ppermute x7, waiting for transfers between devices, swap(): return lax.ppermute(value, 'wave', [(i, i ^ by) for i in range(wave_size)])  1.35 us
    pallas_call x1, Pallas kernels, per_device(): pl.pallas_call(functools.partial(early_kernel, lat_dev, len(received)), i...  0.89 us
    pallas_call x1, Pallas kernels, per_device(): pl.pallas_call(functools.partial(first_kernel, lat_dev, len(pieces)), in_...  0.82 us
  transfers between devices with their start and end apart: 10, of which 4 were waited for; matrix products, arithmetic and copies ran while one was open for 0% of the time, Pallas kernels for 25%

profile of v9, /device:TPU:0, one launch (start us, length us, event | category | flops | bytes accessed | tf_op | source)
XLA Modules:
  0.0 18.0 jit_solution(6415233834457036901)
XLA Ops:
  0.6 2.4 %legendre.1 = (f32[2,32,128]{2,1,0:T(8,128)S(1)}, f32[2,32,128]{2,1,0:T(8,128)S(1)}, f32[2,32,128]{2,1,0:T(8,128)S(1)}, f32[2,32,128]{2,1,0:T(8,128)S(1)}, bf16[2,640,640]{2,1,0:T(8,128)(2,1)S(1)}) custom-call(s32[320]{0:T(512)} %refs_0_.3, f32[40,2,2,641]{3,2,1,0:T(2,128)} %refs_1_.2, f32[40,16,641]{2,1,0:T(8,128)} %refs_2_.2, ...), custom_call_target="tpu_custom_call" | custom-call | tf_op jit(solution)/shard_map/legendre/pallas_call | solution.py:178
  3.0 4.0 %collective-permute-start.1 = (f32[2,32,128]{2,1,0:T(8,128)S(1)}, f32[2,32,128]{2,1,0:T(8,128)S(1)}, u32[]{:S(2)}, u32[]{:S(2)}) collective-permute-start(f32[2,32,128]{2,1,0:T(8,128)S(1)} %get-tuple-element.25), channel_id=1, source_target_pairs={{0,6},{1,7},{2,4},{3,5},{4,2},{5,3},{6,0},{7,1},{8,14},{9,15},{10,... | collective-permute-start | bytes 98312 | tf_op jit(solution)/shard_map/ppermute | solution.py:204
  7.0 0.5 %collective-permute-start.3 = (f32[2,32,128]{2,1,0:T(8,128)S(1)}, f32[2,32,128]{2,1,0:T(8,128)S(1)}, u32[]{:S(2)}, u32[]{:S(2)}) collective-permute-start(f32[2,32,128]{2,1,0:T(8,128)S(1)} %get-tuple-element.29), channel_id=1, source_target_pairs={{0,4},{1,5},{2,6},{3,7},{4,0},{5,1},{6,2},{7,3},{8,12},{9,13},{10,... | collective-permute-start | bytes 98312 | tf_op jit(solution)/shard_map/ppermute | solution.py:204
  7.5 0.1 collective-permute-start.5
  7.6 0.0 collective-permute-start
  7.6 2.1 %plan.1 = (bf16[768,640]{1,0:T(8,128)(2,1)S(1)}, bf16[768,640]{1,0:T(8,128)(2,1)S(1)}, f32[16,384]{1,0:T(8,128)S(1)}, s32[40,128]{1,0:T(8,128)S(1)}, s32[40,128]...) custom-call(bf16[2,640,640]{2,1,0:T(8,128)(2,1)S(1)} %get-tuple-element.26.table_ref.refs_5_., ...), custom_call_target="tpu_custom_call" | custom-call | flops 10000000 | bytes 4000000 | tf_op jit(solution)/shard_map/plan/pallas_call | solution.py:288
  9.7 0.0 collective-permute-done.1.refs_1_
  9.8 0.6 %collective-permute-start.2 = (f32[2,32,128]{2,1,0:T(8,128)S(1)}, f32[2,32,128]{2,1,0:T(8,128)S(1)}, u32[]{:S(2)}, u32[]{:S(2)}) collective-permute-start(f32[2,32,128]{2,1,0:T(8,128)S(1)} %collective-permute-done.1.refs_1_), channel_id=1, source_target_pairs={{0,1},{1,0},{2,3},{3,2},{4,5},{5,4},{6,7},{7,6},{8,9},{9,8},{10,11... | collective-permute-start | bytes 98312 | tf_op jit(solution)/shard_map/ppermute | solution.py:204
  10.3 0.6 %collective-permute-done.3.refs_2_ = f32[2,32,128]{2,1,0:T(8,128)S(1)} collective-permute-done((f32[2,32,128]{2,1,0:T(8,128)S(1)}, f32[2,32,128]{2,1,0:T(8,128)S(1)}, u32[]{:S(2)}, u32[]{:S(2)}) %collective-permute-start.3) | collective-permute-done | bytes 32800 | tf_op jit(solution)/shard_map/ppermute | solution.py:204
  10.9 0.0 collective-permute-start.4
  10.9 0.5 %collective-permute-done.5.refs_3_ = f32[2,32,128]{2,1,0:T(8,128)S(1)} collective-permute-done((f32[2,32,128]{2,1,0:T(8,128)S(1)}, f32[2,32,128]{2,1,0:T(8,128)S(1)}, u32[]{:S(2)}, u32[]{:S(2)}) %collective-permute-start.5) | collective-permute-done | bytes 32800 | tf_op jit(solution)/shard_map/ppermute | solution.py:204
  11.4 0.0 collective-permute-start.6
  11.4 0.9 %early.1 = (f32[12,16,128]{2,1,0:T(8,128)S(1)}, f32[1,64,640]{2,1,0:T(8,128)S(1)}) custom-call(f32[2,32,128]{2,1,0:T(8,128)S(1)} %get-tuple-element.24.refs_0_, f32[2,32,128]{2,1,0:T(8,128)S(1)} %collective-permute-done.1.refs_1_, f32[2,32,128]{2,1,0:T(8,128)S(1)} %collective-permute-done.3.refs_2_, f32[2,32,128]{2,1,0:T(8,128)S(1)} %collective-permute-done.5.refs_3_, ...), custom_call_target="tpu_custom_call" | custom-call | flops 100000000 | bytes 2000000 | tf_op jit(solution)/shard_map/early/pallas_call | solution.py:637
  12.3 0.0 collective-permute-done.refs_0_
  12.3 0.0 collective-permute-done.2.refs_1_
  12.3 0.0 collective-permute-done.4.refs_2_
  12.3 0.3 %collective-permute-done.6.refs_3_ = f32[2,32,128]{2,1,0:T(8,128)S(1)} collective-permute-done((f32[2,32,128]{2,1,0:T(8,128)S(1)}, f32[2,32,128]{2,1,0:T(8,128)S(1)}, u32[]{:S(2)}, u32[]{:S(2)}) %collective-permute-start.6) | collective-permute-done | bytes 32800 | tf_op jit(solution)/shard_map/ppermute | solution.py:204
  12.6 0.8 %first_level.1 = (f32[1,4,1280]{2,1,0:T(4,128)S(1)}, f32[40,128]{1,0:T(8,128)S(1)}) custom-call(f32[2,32,128]{2,1,0:T(8,128)S(1)} %collective-permute-done.refs_0_, f32[2,32,128]{2,1,0:T(8,128)S(1)} %collective-permute-done.2.refs_1_, f32[2,32,128]{2,1,0:T(8,128)S(1)} %collective-permute-done.4.refs_2_, f32[2,32,128]{2,1,0:T(8,128)S(1)} %collective-permute-done.6.refs_3_, ...), custom_call_target="tpu_custom_call" | custom-call | flops 100000000 | bytes 4000000 | tf_op jit(solution)/shard_map/first_level/pallas_call | solution.py:657
  13.4 1.6 %collective-permute-start.7 = (f32[40,128]{1,0:T(8,128)S(1)}, f32[40,128]{1,0:T(8,128)S(1)}, u32[]{:S(2)}, u32[]{:S(2)}) collective-permute-start(f32[40,128]{1,0:T(8,128)S(1)} %get-tuple-element.41.refs_12_), channel_id=1, source_target_pairs={{0,8},{1,9},{2,10},{3,11},{4,12},{5,13},{6,14},{7,15},{8,0},{9,1},... | collective-permute-start | bytes 61448 | tf_op jit(solution)/shard_map/ppermute | solution.py:219
  15.1 0.0 collective-permute-start.8
  15.1 0.5 %collective-permute-start.9 = (f32[40,128]{1,0:T(8,128)S(1)}, f32[40,128]{1,0:T(8,128)S(1)}, u32[]{:S(2)}, u32[]{:S(2)}) collective-permute-start(f32[40,128]{1,0:T(8,128)S(1)} %get-tuple-element.41.refs_12_), channel_id=1, source_target_pairs={{0,1},{1,0},{2,3},{3,2},{4,5},{5,4},{6,7},{7,6},{8,9},{9,8},{10,11... | collective-permute-start | bytes 61448 | tf_op jit(solution)/shard_map/ppermute | solution.py:219
  15.6 1.5 %later_levels.1 = (f32[2,4,1280]{2,1,0:T(4,128)}, f32[1,40,128]{2,1,0:T(8,128)S(1)}, f32[40,128]{1,0:T(8,128)S(1)}) custom-call(f32[2,32,128]{2,1,0:T(8,128)S(1)} %collective-permute-done.refs_0_, f32[2,32,128]{2,1,0:T(8,128)S(1)} %collective-permute-done.2.refs_1_, f32[2,32,128]{2,1,0:T(8,128)S(1)} %collective-permute-done.4.refs_2_, ...), custom_call_target="tpu_custom_call" | custom-call | flops 100000000 | bytes 4000000 | tf_op jit(solution)/shard_map/later_levels/pallas_call | solution.py:671
  17.2 0.1 collective-permute-done.7.refs_0_
  17.3 0.0 collective-permute-done.8.refs_1_
  17.3 0.0 collective-permute-done.9.refs_2_
  17.3 0.6 %pad_maximum_fusion = f32[2,4,1280]{2,1,0:T(4,128)} fusion(f32[1,4,1280]{2,1,0:T(4,128)S(1)} %concatenate.9, f32[1,4,1280]{2,1,0:T(4,128)S(1)} %concatenate.8), kind=kLoop, calls=%fused_computation | loop fusion | flops 10240 | bytes 81920 | tf_op jit(solution)/shard_map/concatenate | solution.py:699
  (3 shorter events, 0.1 us)
Async XLA Ops:
  3.0 6.7 %collective-permute-start.1 = (f32[2,32,128]{2,1,0:T(8,128)S(1)}, f32[2,32,128]{2,1,0:T(8,128)S(1)}, u32[]{:S(2)}, u32[]{:S(2)}) collective-permute-start(f32[2,32,128]{2,1,0:T(8,128)S(1)} %get-tuple-element.25), channel_id=1, source_target_pairs={{0,6},{1,7},{2,4},{3,5},{4,2},{5,3},{6,0},{7,1},{8,14},{9,15},{10,... | collective-permute-start | bytes 98312 | tf_op jit(solution)/shard_map/ppermute | solution.py:204
  7.0 3.9 %collective-permute-start.3 = (f32[2,32,128]{2,1,0:T(8,128)S(1)}, f32[2,32,128]{2,1,0:T(8,128)S(1)}, u32[]{:S(2)}, u32[]{:S(2)}) collective-permute-start(f32[2,32,128]{2,1,0:T(8,128)S(1)} %get-tuple-element.29), channel_id=1, source_target_pairs={{0,4},{1,5},{2,6},{3,7},{4,0},{5,1},{6,2},{7,3},{8,12},{9,13},{10,... | collective-permute-start | bytes 98312 | tf_op jit(solution)/shard_map/ppermute | solution.py:204
  7.5 3.9 %collective-permute-start.5 = (f32[2,32,128]{2,1,0:T(8,128)S(1)}, f32[2,32,128]{2,1,0:T(8,128)S(1)}, u32[]{:S(2)}, u32[]{:S(2)}) collective-permute-start(f32[2,32,128]{2,1,0:T(8,128)S(1)} %get-tuple-element.30), channel_id=1, source_target_pairs={{0,2},{1,3},{2,0},{3,1},{4,6},{5,7},{6,4},{7,5},{8,10},{9,11},{10,... | collective-permute-start | bytes 98312 | tf_op jit(solution)/shard_map/ppermute | solution.py:204
  7.6 4.7 %collective-permute-start = (f32[2,32,128]{2,1,0:T(8,128)S(1)}, f32[2,32,128]{2,1,0:T(8,128)S(1)}, u32[]{:S(2)}, u32[]{:S(2)}) collective-permute-start(f32[2,32,128]{2,1,0:T(8,128)S(1)} %get-tuple-element.24.refs_0_), channel_id=1, source_target_pairs={{0,1},{1,0},{2,3},{3,2},{4,5},{5,4},{6,7},{7,6},{8,9},{9,8},{10,11... | collective-permute-start | bytes 98312 | tf_op jit(solution)/shard_map/ppermute | solution.py:204
  9.8 2.6 %collective-permute-start.2 = (f32[2,32,128]{2,1,0:T(8,128)S(1)}, f32[2,32,128]{2,1,0:T(8,128)S(1)}, u32[]{:S(2)}, u32[]{:S(2)}) collective-permute-start(f32[2,32,128]{2,1,0:T(8,128)S(1)} %collective-permute-done.1.refs_1_), channel_id=1, source_target_pairs={{0,1},{1,0},{2,3},{3,2},{4,5},{5,4},{6,7},{7,6},{8,9},{9,8},{10,11... | collective-permute-start | bytes 98312 | tf_op jit(solution)/shard_map/ppermute | solution.py:204
  10.9 1.4 %collective-permute-start.4 = (f32[2,32,128]{2,1,0:T(8,128)S(1)}, f32[2,32,128]{2,1,0:T(8,128)S(1)}, u32[]{:S(2)}, u32[]{:S(2)}) collective-permute-start(f32[2,32,128]{2,1,0:T(8,128)S(1)} %collective-permute-done.3.refs_2_), channel_id=1, source_target_pairs={{0,1},{1,0},{2,3},{3,2},{4,5},{5,4},{6,7},{7,6},{8,9},{9,8},{10,11... | collective-permute-start | bytes 98312 | tf_op jit(solution)/shard_map/ppermute | solution.py:204
  11.4 1.2 %collective-permute-start.6 = (f32[2,32,128]{2,1,0:T(8,128)S(1)}, f32[2,32,128]{2,1,0:T(8,128)S(1)}, u32[]{:S(2)}, u32[]{:S(2)}) collective-permute-start(f32[2,32,128]{2,1,0:T(8,128)S(1)} %collective-permute-done.5.refs_3_), channel_id=1, source_target_pairs={{0,1},{1,0},{2,3},{3,2},{4,5},{5,4},{6,7},{7,6},{8,9},{9,8},{10,11... | collective-permute-start | bytes 98312 | tf_op jit(solution)/shard_map/ppermute | solution.py:204
  13.4 3.8 %collective-permute-start.7 = (f32[40,128]{1,0:T(8,128)S(1)}, f32[40,128]{1,0:T(8,128)S(1)}, u32[]{:S(2)}, u32[]{:S(2)}) collective-permute-start(f32[40,128]{1,0:T(8,128)S(1)} %get-tuple-element.41.refs_12_), channel_id=1, source_target_pairs={{0,8},{1,9},{2,10},{3,11},{4,12},{5,13},{6,14},{7,15},{8,0},{9,1},... | collective-permute-start | bytes 61448 | tf_op jit(solution)/shard_map/ppermute | solution.py:219
  15.1 2.2 %collective-permute-start.8 = (f32[40,128]{1,0:T(8,128)S(1)}, f32[40,128]{1,0:T(8,128)S(1)}, u32[]{:S(2)}, u32[]{:S(2)}) collective-permute-start(f32[40,128]{1,0:T(8,128)S(1)} %get-tuple-element.41.refs_12_), channel_id=1, source_target_pairs={{0,1},{1,0},{2,3},{3,2},{4,5},{5,4},{6,7},{7,6},{8,16},{9,17},{10,... | collective-permute-start | bytes 61448 | tf_op jit(solution)/shard_map/ppermute | solution.py:219
  15.1 2.2 %collective-permute-start.9 = (f32[40,128]{1,0:T(8,128)S(1)}, f32[40,128]{1,0:T(8,128)S(1)}, u32[]{:S(2)}, u32[]{:S(2)}) collective-permute-start(f32[40,128]{1,0:T(8,128)S(1)} %get-tuple-element.41.refs_12_), channel_id=1, source_target_pairs={{0,1},{1,0},{2,3},{3,2},{4,5},{5,4},{6,7},{7,6},{8,9},{9,8},{10,11... | collective-permute-start | bytes 61448 | tf_op jit(solution)/shard_map/ppermute | solution.py:219
